TPU v7x, 32 devices: a whole 2x2x4 slice. The times are simulated.
32 devices in a mesh: groups: 2 (over y), dp: 4 (over z), tp: 4 (over x, core).
Axes of the slice: x: 2, y: 2, z: 4, core: 2. Of those that a mesh axis runs over, the one named last changes fastest.
Arguments:
- hidden: bfloat16 [4096, 3584], P(('groups', 'dp')), parts along dimension 0, may hold values from -24 to 24
- lengths: int32 [8, 32], P(('groups', 'dp')), parts along dimension 0, may hold values from 1 to 128, 512 in all within a row
- list_ids: int32 [8, 32], P(('groups', 'dp')), parts along dimension 0, may hold values from 0 to 31, as said below
- list_slot: int32 [64], P('groups'), parts along dimension 0, may hold values from 0 to 31, as said below
- gain: float32 [3584], replicated, may hold values from 0.1 to 1.9
- w_query: bfloat16 [3584, 2048], P('dp', 'tp'), may hold values from -0.09375 to 0.09375
- b_query: bfloat16 [2048], P('tp'), may hold values from -100 to 100
- w_keyval: bfloat16 [3584, 1024], P('dp', 'tp'), may hold values from -0.09375 to 0.09375
- b_keyval: bfloat16 [1024], replicated, may hold values from -6 to 6
- w_out: bfloat16 [2048, 3584], P('tp', 'dp'), may hold values from -0.125 to 0.125
- w_pool: bfloat16 [3584, 1024], P('tp'), may hold values from -0.09375 to 0.09375
- centroids: float32 [32, 1024], P('dp', 'tp'), may hold values from -5 to 5
Outputs:
- layer_out: bfloat16 [4096, 3584], P(('groups', 'dp'), 'tp'), parts along dimension 0
- residual_sums: float32 [64, 1024], P(('groups', 'dp'), 'tp'), parts along dimension 0
- list_counts: int32 [64], P(('groups', 'dp')), parts along dimension 0
There are 2 independent parts, one for each index of `groups`. A program takes and returns all parts, laid end to end along the dimension named above; an argument that names none is the same for every part. Nothing has to cross between parts.
Inputs may be any that keep to these rules, and one draw needn't show every extreme that they name: List l is owned by index list_slot[l] // 8 of dp; list_slot is a permutation. `list_ids`: the captions of one index of dp go to at most 16 captions for any one owner; in every draw some owner gets exactly 16 from every index of dp.
All inputs are finite; a program needn't handle non-finite values.
Results may differ from a plain program's by a relative error of at most 0.009.
Values may be sent and summed in bfloat16 or wider, within the bound.
No kernel may reach another device: no remote copies, remote signals or barrier semaphores. Data moves between devices by JAX's collectives and lax.ppermute only.
A program may use at most 128 MiB of HBM per device.

v0:
```python
import jax
import jax.numpy as jnp
from jax import lax
from jax.sharding import PartitionSpec as P

KV_HEADS = 4
HD = 128
Q_HEADS = 16


rope_base = 1000000.0


def rotate(values, places):
    half = HD // 2
    freq = rope_base ** (-(2.0 / HD) * jnp.arange(half, dtype=jnp.float32))
    angle = places.astype(jnp.float32)[:, None] * freq[None, :]
    cosine = jnp.cos(angle)[:, None, :]
    sine = jnp.sin(angle)[:, None, :]
    shaped = values.reshape(values.shape[0], -1, HD)
    first = shaped[..., :half]
    second = shaped[..., half:]
    turned = jnp.concatenate(
        [first * cosine - second * sine, second * cosine + first * sine], axis=-1
    )
    return turned.reshape(values.shape)


def positions_of(lengths_row, token_count, caption_count):
    ends = jnp.cumsum(lengths_row, dtype=jnp.int32)
    index = jnp.arange(token_count, dtype=jnp.int32)
    segment = jnp.sum((index[:, None] >= ends[None, :]).astype(jnp.int32), axis=1, dtype=jnp.int32)
    member = segment[None, :] == jnp.arange(caption_count, dtype=jnp.int32)[:, None]
    starts = ends - lengths_row
    place = index - jnp.sum(jnp.where(member, starts[:, None], 0), axis=0, dtype=jnp.int32)
    return (segment, member, place)


def shards(
    hidden,
    lengths,
    list_ids,
    list_slot,
    gain,
    w_query,
    b_query,
    w_keyval,
    b_keyval,
    w_out,
    w_pool,
    centroids,
):
    token_count = hidden.shape[0]
    caption_count = lengths.shape[1]
    dp_count = lax.axis_size("dp")
    tp_index = lax.axis_index("tp")
    wide = hidden.astype(jnp.float32)
    normed = (wide * lax.rsqrt(jnp.mean(wide * wide, axis=1, keepdims=True) + 1e-06) * gain).astype(
        jnp.bfloat16
    )
    segment, member, place = positions_of(lengths[0], token_count, caption_count)
    query_cols = w_query.shape[1]
    kv_width = b_keyval.shape[0] // 2
    head_group = tp_index * (query_cols // HD) // (Q_HEADS // KV_HEADS)
    full_cols = lax.all_gather(w_keyval, "tp", axis=1, tiled=True)
    query_sum = jnp.dot(
        normed,
        lax.all_gather(w_query, "dp", axis=0, tiled=True),
        preferred_element_type=jnp.float32,
    )
    keyval_sum = jnp.dot(
        normed,
        lax.all_gather(full_cols, "dp", axis=0, tiled=True),
        preferred_element_type=jnp.float32,
    )
    keyval_sum = keyval_sum + b_keyval.astype(jnp.float32)
    keys_all = rotate(keyval_sum[:, :kv_width], place).astype(jnp.bfloat16)
    values_all = keyval_sum[:, kv_width:].astype(jnp.bfloat16)
    keys = lax.dynamic_slice_in_dim(keys_all, head_group * HD, HD, 1)
    values = lax.dynamic_slice_in_dim(values_all, head_group * HD, HD, 1)
    query = rotate(query_sum + b_query.astype(jnp.float32), place).astype(jnp.bfloat16)
    grouped = query.reshape(token_count, query_cols // HD, HD)
    scores = jnp.einsum("sgd,td->gst", grouped, keys, preferred_element_type=jnp.float32) * HD ** (
        -0.5
    )
    allowed = segment[:, None] == segment[None, :]
    scores = jnp.where(allowed[None], scores, -1e30)
    probs = jax.nn.softmax(scores, axis=-1).astype(jnp.bfloat16)
    attn = jnp.einsum("gst,td->sgd", probs, values, preferred_element_type=jnp.float32)
    attn = attn.astype(jnp.bfloat16).reshape(token_count, query_cols)
    partial_out = jnp.dot(
        attn, lax.all_gather(w_out, "dp", axis=1, tiled=True), preferred_element_type=jnp.float32
    )
    summed = lax.psum_scatter(
        partial_out.astype(jnp.bfloat16), "tp", scatter_dimension=1, tiled=True
    ).astype(jnp.float32)
    feature_share = summed.shape[1]
    own_input = lax.dynamic_slice_in_dim(wide, tp_index * feature_share, feature_share, 1)
    layer_out = (own_input + summed).astype(jnp.bfloat16)
    pooled = jnp.dot(member.astype(jnp.bfloat16), layer_out, preferred_element_type=jnp.float32)
    pooled = (pooled / lengths[0].astype(jnp.float32)[:, None]).astype(jnp.bfloat16)
    pooled_part = jnp.dot(pooled, w_pool, preferred_element_type=jnp.float32)
    vec = lax.psum_scatter(pooled_part.astype(jnp.bfloat16), "tp", scatter_dimension=1, tiled=True)
    lists_total = list_slot.shape[0]
    caption_lists = list_ids.reshape(-1)
    slot = jnp.sum(
        jnp.where(
            caption_lists[:, None] == jnp.arange(lists_total, dtype=jnp.int32)[None, :],
            list_slot[None, :],
            0,
        ),
        axis=1,
        dtype=jnp.int32,
    )
    lists_own = centroids.shape[0]
    send_cap = max(2, 2 * caption_count // dp_count)
    owner = slot // lists_own
    local = slot % lists_own
    order = jnp.arange(caption_count, dtype=jnp.int32)
    earlier = (owner[None, :] == owner[:, None]) & (order[None, :] < order[:, None])
    rank = jnp.sum(earlier.astype(jnp.int32), axis=1, dtype=jnp.int32)
    target = owner * send_cap + rank
    placed = jnp.arange(dp_count * send_cap, dtype=jnp.int32)[:, None] == target[None, :]
    send_values = jnp.dot(
        placed.astype(jnp.bfloat16), vec, preferred_element_type=jnp.float32
    ).astype(jnp.bfloat16)
    send_values = send_values.reshape(dp_count, send_cap, vec.shape[1])
    send_rows = jnp.sum(jnp.where(placed, local[None, :] + 1, 0), axis=1, dtype=jnp.int32).reshape(
        dp_count, send_cap
    )
    got_values, got_rows = (
        lax.all_to_all(send_values, "dp", split_axis=0, concat_axis=0, tiled=True),
        lax.all_to_all(send_rows, "dp", split_axis=0, concat_axis=0, tiled=True),
    )
    got_values = got_values.reshape(dp_count * send_cap, vec.shape[1])
    got_rows = got_rows.reshape(dp_count * send_cap)
    hits = got_rows[None, :] - 1 == jnp.arange(lists_own, dtype=jnp.int32)[:, None]
    totals = jnp.dot(hits.astype(jnp.bfloat16), got_values, preferred_element_type=jnp.float32)
    list_counts = jnp.sum(hits.astype(jnp.int32), axis=1, dtype=jnp.int32)
    residual_sums = totals - list_counts.astype(jnp.float32)[:, None] * centroids
    return (layer_out, residual_sums, list_counts)


def solution(mesh):
    return jax.shard_map(
        shards,
        mesh=mesh,
        in_specs=(
            P(("groups", "dp"), None),
            P(("groups", "dp"), None),
            P(("groups", "dp"), None),
            P("groups"),
            P(),
            P("dp", "tp"),
            P("tp"),
            P("dp", "tp"),
            P(),
            P("tp", "dp"),
            P("tp", None),
            P("dp", "tp"),
        ),
        out_specs=(P(("groups", "dp"), "tp"), P(("groups", "dp"), "tp"), P(("groups", "dp"))),
        check_vma=False,
    )
```

profile of v0, /device:TPU:0, one launch (start us, length us, event | category | flops | bytes accessed | tf_op | source)
XLA Modules:
  0.0 409.4 jit_solution(9973302083545957893)
XLA Ops:
  7.3 0.7 all-gather.5.cloned.1.call-update
  8.0 0.7 all-gather.9.cloned.1.call-update
  8.8 24.9 %all-gather.5.cloned.1.call-done = bf16[896,1024]{1,0:T(8,128)(2,1)} async-done(((bf16[896,256]{1,0:T(8,128)(2,1)}), bf16[896,1024]{1,0:T(8,128)(2,1)}) %all-gather.5.cloned.1.call-update) | async-done | bytes 1835024 | tf_op jit(solution)/shard_map/all_gather | solution.py:65
  33.7 0.5 all-gather.11.cloned.1.call-update
  34.3 0.7 copy.41
  35.1 0.1 reduce
  35.2 0.1 convert_reduce_fusion
  35.4 0.1 select_reduce_fusion
  35.5 2.8 multiply_reduce_fusion
  38.4 0.9 broadcast_compare_fusion
  39.3 1.8 multiply_cosine_fusion
  41.1 66.3 %all-gather.9.cloned.1.call-done = bf16[3584,512]{1,0:T(8,128)(2,1)} async-done(((bf16[896,512]{1,0:T(8,128)(2,1)}), bf16[3584,512]{1,0:T(8,128)(2,1)}) %all-gather.9.cloned.1.call-update) | async-done | bytes 3670032 | tf_op jit(solution)/shard_map/all_gather | solution.py:68
  107.4 5.4 %convolution_add_fusion.1 = f32[512,512]{0,1:T(8,128)S(1)} fusion(bf16[3584,512]{1,0:T(8,128)(2,1)} %all-gather.9.cloned.1.call-done, f32[3584]{0:T(1024)S(1)} %copy-done.7, f32[512]{0:T(512)S(1)} %add_rsqrt_fusion, bf16[512,3584]{1,0:T(8,128)(2,1)} %param.12, f32[512]{0:T(512)S(1)} %convert_element_type.86), kind=kOutput, calls=%fused_computation.14 | convolution fusion | flops 1886650368 | bytes 8407040 | tf_op jit(solution)/shard_map/dot_general | solution.py:66
  112.8 1.3 copy.59
  114.2 1.3 copy.60
  115.5 124.6 %all-gather.7.cloned.1.call-done = bf16[3584,1024]{1,0:T(8,128)(2,1)} async-done(((bf16[896,1024]{1,0:T(8,128)(2,1)}), bf16[3584,1024]{1,0:T(8,128)(2,1)}) %all-gather.7.cloned.1.call-update) | async-done | bytes 7340048 | tf_op jit(solution)/shard_map/all_gather | solution.py:73
  240.1 7.4 %convolution_add_fusion = f32[512,1024]{1,0:T(8,128)S(1)} fusion(bf16[3584,1024]{1,0:T(8,128)(2,1)} %all-gather.7.cloned.1.call-done, f32[3584]{0:T(1024)S(1)} %copy-done.7, f32[512]{0:T(512)S(1)} %add_rsqrt_fusion, bf16[512,3584]{1,0:T(8,128)(2,1)} %param.12, f32[1024]{0:T(1024)S(1)} %convert_element_type.82), kind=kOutput, calls=%fused_computation.13 | convolution fusion | flops 3765960704 | bytes 13127680 | tf_op jit(solution)/shard_map/dot_general | solution.py:71
  247.5 1.1 slice.26
  248.6 0.9 slice.25
  249.5 1.6 reshape.233
  251.1 0.6 fusion.28
  251.7 0.6 copy-done.1
  252.3 0.3 copy-done.2
  252.6 1.6 subtract_convert_fusion.1
  254.3 0.3 pad_maximum_fusion
  254.6 1.0 copy.44
  255.6 1.7 fusion.8
  257.3 2.1 fusion.30
  259.5 1.4 fusion.6
  260.8 51.1 %all-gather.11.cloned.1.call-done = bf16[512,3584]{1,0:T(8,128)(2,1)} async-done(((bf16[512,896]{1,0:T(8,128)(2,1)}), bf16[512,3584]{1,0:T(8,128)(2,1)}) %all-gather.11.cloned.1.call-update) | async-done | bytes 3670032 | tf_op jit(solution)/shard_map/all_gather | solution.py:92
  311.9 5.9 %convolution_convert_fusion = bf16[512,3584]{1,0:T(8,128)(2,1)} fusion(bf16[512,512]{0,1:T(8,128)(2,1)S(1)} %bitcast.45, bf16[512,3584]{1,0:T(8,128)(2,1)} %all-gather.11.cloned.1.call-done), kind=kOutput, calls=%fused_computation.3 | convolution fusion | flops 1880883200 | bytes 7864320 | tf_op jit(solution)/shard_map/dot_general | solution.py:91
  317.9 6.0 %copy.54 = bf16[512,3584]{0,1:T(8,128)(2,1)} copy(bf16[512,3584]{1,0:T(8,128)(2,1)} %convolution_convert_fusion) | data formatting | bytes 7340032
  323.9 6.5 %convert_element_type.80 = f32[512,3584]{1,0:T(8,128)} convert(bf16[512,3584]{1,0:T(8,128)(2,1)} %param.12) | non-fusion elementwise | flops 1835008 | bytes 11010048 | tf_op jit(solution)/shard_map/convert_element_type | solution.py:57
  330.5 0.2 select_reduce_fusion.2
  330.7 0.2 convert_reduce_fusion.1
  330.9 33.0 %reduce-scatter.7.cloned.1.call-done = bf16[896,512]{1,0:T(8,128)(2,1)} async-done(((bf16[3584,512]{1,0:T(8,128)(2,1)}), bf16[896,512]{1,0:T(8,128)(2,1)}) %reduce-scatter.7.cloned.1.call-update) | async-done | bytes 917520
  363.9 1.5 copy.55
  365.4 2.6 add_convert_fusion
  368.0 2.4 convolution_convert_fusion.1
  370.4 0.1 select_reduce_fusion.1
  370.6 9.9 %all_to_all.14 = s32[4,1,16]{2,1,0:T(1,128)S(1)} all-to-all(s32[4,1,16]{2,1,0:T(1,128)S(1)} %bitcast.47), channel_id=1, replica_groups=mesh['groups'=2,'dp'=4,'tp'=4] {'dp'}, dimensions={0} | all-to-all | bytes 512 | tf_op jit(solution)/shard_map/all_to_all | solution.py:133
  380.6 0.1 sub.56
  380.6 9.4 %reduce-scatter.5.cloned.1.call-done = bf16[32,256]{1,0:T(8,128)(2,1)} async-done(((bf16[32,1024]{1,0:T(8,128)(2,1)}), bf16[32,256]{1,0:T(8,128)(2,1)}) %reduce-scatter.5.cloned.1.call-update) | async-done | bytes 16400 | tf_op jit(solution)/shard_map/reduce_scatter | solution.py:103
  390.0 1.6 convolution_convert_fusion.2
  391.6 4.6 %all-to-all-start.1 = ((bf16[4,16,256]{2,1,0:T(8,128)(2,1)}), bf16[4,16,256]{2,1,0:T(8,128)(2,1)S(1)}, u32[]{:S(2)}, u32[]{:S(2)}) async-start(bf16[4,16,256]{2,1,0:T(8,128)(2,1)} %bitcast.11), calls=%async_computation.2 | async-start | bytes 65536 | tf_op jit(solution)/shard_map/all_to_all | solution.py:132
  396.2 0.1 convert_reduce_fusion.2
  396.3 5.5 %all-to-all-done.1 = bf16[4,16,256]{2,1,0:T(8,128)(2,1)S(1)} async-done(((bf16[4,16,256]{2,1,0:T(8,128)(2,1)}), bf16[4,16,256]{2,1,0:T(8,128)(2,1)S(1)}, u32[]{:S(2)}, u32[]{:S(2)}) %all-to-all-start.1) | async-done | bytes 32800 | tf_op jit(solution)/shard_map/all_to_all | solution.py:132
  401.9 0.7 convolution_subtract_fusion
  (45 shorter events, 0.6 us)
Async XLA Ops:
  7.2 360.8 %copy-start = (bf16[896,1024]{1,0:T(8,128)(2,1)S(1)}, bf16[896,1024]{1,0:T(8,128)(2,1)}, u32[]{:S(2)}) copy-start(bf16[896,1024]{1,0:T(8,128)(2,1)} %param.22) | copy-start | bytes 5505028
  7.2 28.1 %copy-start.6 = (s32[1,32]{1,0:T(1,128)S(1)}, s32[1,32]{1,0:T(1,128)}, u32[]{:S(2)}) copy-start(s32[1,32]{1,0:T(1,128)} %param.13) | copy-start | bytes 388
  7.2 28.2 %copy-start.4 = (bf16[1024]{0:T(1024)(128)(2,1)S(1)}, bf16[1024]{0:T(1024)(128)(2,1)}, u32[]{:S(2)}) copy-start(bf16[1024]{0:T(1024)(128)(2,1)} %param.20) | copy-start | bytes 6148
  7.2 28.2 %copy-start.5 = (bf16[512]{0:T(512)(128)(2,1)S(1)}, bf16[512]{0:T(512)(128)(2,1)}, u32[]{:S(2)}) copy-start(bf16[512]{0:T(512)(128)(2,1)} %param.18) | copy-start | bytes 3076
  7.2 26.5 %all-gather.5.cloned.1.call-start = ((), (), s32[]{:S(2)}) async-start(), calls=%async_computation.4 | async-start | bytes 2293760 | tf_op jit(solution)/shard_map/all_gather | solution.py:65
  7.9 99.4 %copy-start.7 = (f32[3584]{0:T(1024)S(1)}, f32[3584]{0:T(1024)}, u32[]{:S(2)}) copy-start(f32[3584]{0:T(1024)} %param.16) | copy-start | bytes 43012
  8.0 99.4 %all-gather.9.cloned.1.call-start = ((), (), s32[]{:S(2)}) async-start(), calls=%async_computation.6 | async-start | bytes 4587520 | tf_op jit(solution)/shard_map/all_gather | solution.py:68
  8.7 231.4 %all-gather.7.cloned.1.call-start = ((), (), s32[]{:S(2)}) async-start(), calls=%async_computation.5 | async-start | bytes 9175040 | tf_op jit(solution)/shard_map/all_gather | solution.py:73
  33.7 278.2 %all-gather.11.cloned.1.call-start = ((), (), s32[]{:S(2)}) async-start(), calls=%async_computation.7 | async-start | bytes 4587520 | tf_op jit(solution)/shard_map/all_gather | solution.py:92
  34.3 329.6 %reduce-scatter.7.cloned.1.call-start = ((), (), s32[]{:S(2)}) async-start(), calls=%async_computation.9 | async-start | bytes 4587520
  251.1 1.2 copy-start.1
  251.1 1.5 copy-start.2
  255.6 1.7 copy-start.3
  323.8 6.6 %copy-start.9 = (s32[32]{0:T(128)S(1)}, s32[32]{0:T(128)}, u32[]{:S(2)}) copy-start(s32[32]{0:T(128)} %param.15) | copy-start | bytes 388
  323.8 6.6 %copy-start.10 = (s32[1,32]{1,0:T(1,128)S(1)}, s32[1,32]{1,0:T(1,128)}, u32[]{:S(2)}) copy-start(s32[1,32]{1,0:T(1,128)} %param.14) | copy-start | bytes 388
  323.9 66.1 %reduce-scatter.5.cloned.1.call-start = ((), (), s32[]{:S(2)}) async-start(), calls=%async_computation.8 | async-start | bytes 81920 | tf_op jit(solution)/shard_map/reduce_scatter | solution.py:103
  363.9 38.0 %copy-start.8 = (f32[8,256]{1,0:T(8,128)S(1)}, f32[8,256]{1,0:T(8,128)}, u32[]{:S(2)}) copy-start(f32[8,256]{1,0:T(8,128)} %param.23) | copy-start | bytes 24580
  391.6 10.3 %all-to-all-start.1 = ((bf16[4,16,256]{2,1,0:T(8,128)(2,1)}), bf16[4,16,256]{2,1,0:T(8,128)(2,1)S(1)}, u32[]{:S(2)}, u32[]{:S(2)}) async-start(bf16[4,16,256]{2,1,0:T(8,128)(2,1)} %bitcast.11), calls=%async_computation.2 | async-start | bytes 65536 | tf_op jit(solution)/shard_map/all_to_all | solution.py:132
  396.3 6.3 %copy-start.11 = (s32[8]{0:T(128)}, s32[8]{0:T(128)S(1)}, u32[]{:S(2)}) copy-start(s32[8]{0:T(128)S(1)} %convert_reduce_fusion.2) | copy-start | bytes 100
Sparse Core Ops, SparseCore 0:
  9.6 24.0 all-gather.4
  35.2 72.1 all-gather.8
  109.0 131.0 all-gather.6
  241.6 70.3 all-gather.10
  324.0 39.8 reduce-scatter.6
  370.5 19.4 reduce-scatter.4
where the time goes:
time: 410 us; the launch traced here: 409 us
  waiting for transfers between devices  317 us (77%)
  matrix products  26.5 us (6%)
  other arithmetic  19.7 us (5%)
  local copies, waits for them, and re-layouts  17.3 us (4%)
  between operations  14.4 us (4%)
  blocking collectives  9.94 us (2%)
  starting transfers between devices  4.84 us (1%)
    all_gather x1, waiting for transfers between devices, shards(): lax.all_gather(full_cols, 'dp', axis=0, tiled=True)  125 us
    all_gather x1, waiting for transfers between devices, shards(): lax.all_gather(w_query, 'dp', axis=0, tiled=True)  66.3 us
    all_gather x1, waiting for transfers between devices, shards(): lax.all_gather(w_out, 'dp', axis=1, tiled=True)  51.1 us
    unnamed x7, waiting for transfers between devices  35 us
    all_gather x1, waiting for transfers between devices, shards(): full_cols = lax.all_gather(w_keyval, 'tp', axis=1, tiled=True)  24.9 us
    unnamed x28, local copies, waits for them, and re-layouts  11.1 us
    all_to_all x1, blocking collectives, shards(): lax.all_to_all(send_rows, 'dp', split_axis=0, concat_axis=0, tiled=True)  9.94 us
    reduce_scatter x1, waiting for transfers between devices, shards(): lax.psum_scatter(pooled_part.astype(jnp.bfloat16), 'tp', scatter_dimensio...  9.36 us
  transfers between devices with their start and end apart: 7, of which 7 were waited for; matrix products, arithmetic and copies ran while one was open for 10% of the time, Pallas kernels for 0%

commit v1 on v0

--- a/solution.py
+++ b/solution.py
@@ -1,6 +1,8 @@
 import jax
 import jax.numpy as jnp
 from jax import lax
+from jax.experimental import pallas as pl
+from jax.experimental.pallas import tpu as pltpu
 from jax.sharding import PartitionSpec as P
 
 KV_HEADS = 4
@@ -9,6 +11,8 @@
 
 
 rope_base = 1000000.0
+bf16 = jnp.bfloat16
+f32 = jnp.float32
 
 
 def rotate(values, places):
@@ -36,7 +40,7 @@
     return (segment, member, place)
 
 
-def shards(
+def wide_slice_shards(
     hidden,
     lengths,
     list_ids,
@@ -68,16 +72,22 @@
         lax.all_gather(w_query, "dp", axis=0, tiled=True),
         preferred_element_type=jnp.float32,
     )
+    own_cols = jnp.concatenate(
+        [
+            lax.dynamic_slice_in_dim(full_cols, head_group * HD, HD, 1),
+            lax.dynamic_slice_in_dim(full_cols, kv_width + head_group * HD, HD, 1),
+        ],
+        axis=1,
+    )
     keyval_sum = jnp.dot(
         normed,
-        lax.all_gather(full_cols, "dp", axis=0, tiled=True),
+        lax.all_gather(own_cols, "dp", axis=0, tiled=True),
         preferred_element_type=jnp.float32,
     )
-    keyval_sum = keyval_sum + b_keyval.astype(jnp.float32)
-    keys_all = rotate(keyval_sum[:, :kv_width], place).astype(jnp.bfloat16)
-    values_all = keyval_sum[:, kv_width:].astype(jnp.bfloat16)
-    keys = lax.dynamic_slice_in_dim(keys_all, head_group * HD, HD, 1)
-    values = lax.dynamic_slice_in_dim(values_all, head_group * HD, HD, 1)
+    key_bias = lax.dynamic_slice_in_dim(b_keyval, head_group * HD, HD, 0)
+    value_bias = lax.dynamic_slice_in_dim(b_keyval, kv_width + head_group * HD, HD, 0)
+    keys = rotate(keyval_sum[:, :HD] + key_bias.astype(jnp.float32), place).astype(jnp.bfloat16)
+    values = (keyval_sum[:, HD:] + value_bias.astype(jnp.float32)).astype(jnp.bfloat16)
     query = rotate(query_sum + b_query.astype(jnp.float32), place).astype(jnp.bfloat16)
     grouped = query.reshape(token_count, query_cols // HD, HD)
     scores = jnp.einsum("sgd,td->gst", grouped, keys, preferred_element_type=jnp.float32) * HD ** (
@@ -141,9 +151,282 @@
     return (layer_out, residual_sums, list_counts)
 
 
+def attention_kernel(q_own, q_oth, key_ref, value_ref, cos_ref, sin_ref, seg_col, seg_row, out_ref):
+    def turn(x, cosine, sine):
+        return (x * cosine + pltpu.roll(x, HD // 2, 1) * sine).astype(bf16)
+
+    keys = turn(key_ref[...], cos_ref[...], sin_ref[...])
+    values = value_ref[...].astype(bf16)
+    rows = 128
+    tokens = key_ref.shape[0]
+    for i in range(tokens // rows):
+        at = pl.ds(i * rows, rows)
+        cosine, sine = cos_ref[at, :], sin_ref[at, :]
+        allowed = seg_col[at, :] == seg_row[...]
+        for part, ref in enumerate((q_own, q_oth)):
+            heads = ref.shape[1] // HD
+            for h in range(heads):
+                query = turn(ref[at, h * HD : (h + 1) * HD], cosine, sine)
+                scores = lax.dot_general(
+                    query, keys, (((1,), (1,)), ((), ())), preferred_element_type=f32
+                ) * HD ** (-0.5)
+                scores = jnp.where(allowed, scores, -1e30)
+                top = jnp.max(scores, axis=1, keepdims=True)
+                weights = jnp.exp(scores - top)
+                probs = (weights / jnp.sum(weights, axis=1, keepdims=True)).astype(bf16)
+                mixed = jnp.dot(probs, values, preferred_element_type=f32)
+                lo = (part * heads + h) * HD
+                out_ref[at, lo : lo + HD] = mixed.astype(bf16)
+
+
+def attend(q_own, q_oth, keys, values, cosine, sine, segment):
+    tokens = q_own.shape[0]
+    return pl.pallas_call(
+        attention_kernel,
+        out_shape=jax.ShapeDtypeStruct((tokens, q_own.shape[1] * 2), bf16),
+        compiler_params=pltpu.CompilerParams(vmem_limit_bytes=32 * 1024 * 1024),
+        cost_estimate=pl.CostEstimate(
+            flops=4 * tokens * tokens * q_own.shape[1] * 2,
+            bytes_accessed=8 * 1024 * 1024,
+            transcendentals=tokens * tokens * 4,
+        ),
+    )(q_own, q_oth, keys, values, cosine, sine, segment[:, None], segment[None, :])
+
+
+def folded_ring(n):
+    return list(range(0, 1)) + list(range(1, n, 2)) + list(range(2 * ((n - 1) // 2), 0, -2))
+
+
+def shards(
+    hidden,
+    lengths,
+    list_ids,
+    list_slot,
+    gain,
+    w_query,
+    b_query,
+    w_keyval,
+    b_keyval,
+    w_out,
+    w_pool,
+    centroids,
+):
+    tokens, width = hidden.shape
+    captions = lengths.shape[1]
+    n_dp, n_tp = lax.axis_size("dp"), lax.axis_size("tp")
+    g, z, t = lax.axis_index("groups"), lax.axis_index("dp"), lax.axis_index("tp")
+    ring = folded_ring(n_dp)
+    place_in = {v: i for i, v in enumerate(ring)}
+    ring_pairs = [(ring[i], ring[(i + 1) % n_dp]) for i in range(n_dp)]
+    source_of = [[ring[(place_in[d] - m) % n_dp] for m in range(n_dp)] for d in range(n_dp)]
+    blocks_at = jnp.array(source_of, jnp.int32)[z]
+    blk = [blocks_at[m] for m in range(n_dp)]
+    swap = [(0, 1), (1, 0)]
+    core = [(i, i ^ 1) for i in range(n_tp)]
+    share = width // n_dp
+
+    q_half = w_query.shape[1] // 2
+    o_half = w_out.shape[0] // 2
+
+    def half(w, i, size, axis):
+        return lax.dynamic_slice_in_dim(w, i * size, size, axis)
+
+    q0 = (half(w_query, g, q_half, 1), half(w_query, 1 - g, q_half, 1))
+    per_dev = w_keyval.shape[1] // HD
+    rounds = [[] for _ in range(per_dev)]
+    for gg in range(2):
+        for tt in range(n_tp):
+            head = tt * (w_query.shape[1] // HD) // (Q_HEADS // KV_HEADS)
+            col = gg * KV_HEADS + head
+            rounds[col % per_dev].append((gg * n_tp + col // per_dev, gg * n_tp + tt))
+    came = [
+        lax.ppermute(w_keyval[:, r * HD : (r + 1) * HD], ("groups", "tp"), rounds[r])
+        for r in range(per_dev)
+    ]
+    head = t * (w_query.shape[1] // HD) // (Q_HEADS // KV_HEADS)
+    kv_own = came[0]
+    for r in range(1, per_dev):
+        kv_own = jnp.where(head % per_dev == r, came[r], kv_own)
+    cut = 512
+    oa0 = half(w_out[:, :cut], g, o_half, 0)
+    ob0 = half(w_out[:, cut:], g, o_half, 0)
+
+    order = []
+    for m in range(1, n_dp):
+        order += [("q", m), ("k", m)]
+    for m in range(1, n_dp):
+        order += [("a", m), ("b", m)]
+    zres = {("q", 0): q0[0], ("k", 0): kv_own, ("a", 0): oa0, ("b", 0): ob0}
+    yres = {("q", 0): q0[1]}
+    for i, key in enumerate(order):
+        operand = zres[(key[0], key[1] - 1)]
+        ties = []
+        if i >= 2:
+            ties.append((zres, order[i - 2]))
+        if i >= 4:
+            ties.append((yres, order[i - 4]))
+        if ties:
+            got = lax.optimization_barrier((operand, *[d[k] for d, k in ties]))
+            operand = got[0]
+            for (d, k), v in zip(ties, got[1:]):
+                d[k] = v
+        zres[key] = lax.ppermute(operand, "dp", ring_pairs)
+        yres[key] = lax.ppermute(zres[key], "groups", swap)
+        if i == 1:
+            yres[("k", 0)] = lax.ppermute(kv_own, "groups", swap)
+
+    wide = hidden.astype(f32)
+    normed = (wide * lax.rsqrt(jnp.mean(wide * wide, axis=1, keepdims=True) + 1e-06) * gain).astype(
+        bf16
+    )
+    segment, member, place = positions_of(lengths[0], tokens, captions)
+    freq = rope_base ** (-(2.0 / HD) * jnp.arange(HD // 2, dtype=f32))
+    angle = place.astype(f32)[:, None] * freq[None, :]
+    cosine, sine = jnp.cos(angle), jnp.sin(angle)
+    cosine = jnp.concatenate([cosine, cosine], axis=1)
+    sine = jnp.concatenate([-sine, sine], axis=1)
+
+    sums = {}
+    for m in range(n_dp):
+        rows = lax.dynamic_slice_in_dim(normed, blk[m] * share, share, 1)
+        for name, res in (("q", zres), ("k", zres), ("Q", yres), ("K", yres)):
+            part = jnp.dot(rows, res[(name.lower(), m)], preferred_element_type=f32)
+            sums[name] = sums[name] + part if name in sums else part
+    bq = b_query.astype(f32)
+    q_own = sums["q"] + half(bq, g, q_half, 0)
+    q_oth = sums["Q"] + half(bq, 1 - g, q_half, 0)
+    kv_width = b_keyval.shape[0] // 2
+    bkv = b_keyval.astype(f32)
+    keys = jnp.where(g == 0, sums["k"], sums["K"]) + half(bkv, head, HD, 0)
+    values = jnp.where(g == 0, sums["K"], sums["k"]) + lax.dynamic_slice_in_dim(
+        bkv, kv_width + head * HD, HD, 0
+    )
+    attn = attend(q_own, q_oth, keys, values, cosine, sine, segment)
+
+    inverse = 1.0 / lengths[0].astype(f32)[:, None]
+    member16 = member.astype(bf16)
+    pooled_hidden = jnp.dot(member16, hidden, preferred_element_type=f32) * inverse
+    lists_total = list_slot.shape[0]
+    slot = jnp.sum(
+        jnp.where(
+            list_ids.reshape(-1)[:, None] == jnp.arange(lists_total, dtype=jnp.int32)[None, :],
+            list_slot[None, :],
+            0,
+        ),
+        axis=1,
+        dtype=jnp.int32,
+    )
+    early = jnp.concatenate(
+        [
+            pooled_hidden.astype(bf16).reshape(captions, n_dp, share).transpose(1, 0, 2),
+            jnp.broadcast_to(slot.astype(bf16)[None, :, None], (n_dp, captions, HD)),
+        ],
+        axis=2,
+    )
+    early = lax.all_to_all(early, "dp", split_axis=0, concat_axis=0, tiled=True)
+    slots = early[:, :, share].astype(jnp.int32)
+    hits = slots[:, None, :] == jnp.arange(lists_total, dtype=jnp.int32)[None, :, None]
+    hits16 = hits.astype(bf16)
+    counts = jnp.sum(hits.astype(jnp.int32), axis=(0, 2), dtype=jnp.int32)
+    lists_own = centroids.shape[0]
+    list_counts = lax.dynamic_slice_in_dim(counts, z * lists_own, lists_own, 0)
+    hidden_lists = jnp.einsum(
+        "dlc,dcf->lf", hits16, early[:, :, :share], preferred_element_type=f32
+    )
+    pooled_attn = (jnp.dot(member16, attn, preferred_element_type=f32) * inverse).astype(bf16)
+    attn_lists = jnp.zeros((lists_total, attn.shape[1]), f32)
+    for m in range(n_dp):
+        pairs = [(source_of[d][m], d) for d in range(n_dp)]
+        came_pool = lax.ppermute(pooled_attn, "dp", pairs) if m else pooled_attn
+        hit = lax.dynamic_index_in_dim(hits16, blk[m], 0, keepdims=False)
+        attn_lists = attn_lists + jnp.dot(hit, came_pool, preferred_element_type=f32)
+    attn_lists = attn_lists.astype(bf16)
+    own_rows, oth_rows = half(w_out, g, o_half, 0), half(w_out, 1 - g, o_half, 0)
+    pooled_lists = (
+        jnp.dot(attn_lists[:, :o_half], own_rows, preferred_element_type=f32)
+        + jnp.dot(attn_lists[:, o_half:], oth_rows, preferred_element_type=f32)
+        + hidden_lists * (1.0 / n_tp)
+    ).astype(bf16)
+    across = lax.ppermute(
+        w_pool, ("dp", "tp"), [(d * n_tp + d, d * n_tp + (d ^ 2)) for d in range(n_dp)]
+    )
+    have = jnp.where(t == z, w_pool, across)
+    beside = lax.ppermute(
+        have,
+        ("dp", "tp"),
+        [(d * n_tp + (d ^ k), d * n_tp + (d ^ k ^ 1)) for d in range(n_dp) for k in (0, 2)],
+    )
+    holds = (t == z) | (t == (z ^ 2))
+    vec_lists = jnp.dot(
+        jnp.where(holds, pooled_lists, 0), have, preferred_element_type=f32
+    ) + jnp.dot(pooled_lists, beside, preferred_element_type=f32)
+    cols = centroids.shape[1]
+    late = vec_lists.astype(bf16).reshape(n_dp, lists_own, n_tp, cols).transpose(0, 2, 1, 3)
+    late = late.reshape(n_dp * n_tp, lists_own, cols)
+    late = lax.all_to_all(late, ("dp", "tp"), split_axis=0, concat_axis=0, tiled=True)
+    totals = jnp.sum(late.astype(f32), axis=0)
+    residual_sums = totals - list_counts.astype(f32)[:, None] * centroids
+
+    c = t % 2
+    rows_half = tokens // 2
+    own_cols = slice(0, o_half)
+    oth_cols = slice(o_half, 2 * o_half)
+
+    def project(own, oth):
+        out = jnp.dot(attn[:, own_cols], own, preferred_element_type=f32)
+        out = out + jnp.dot(attn[:, oth_cols], oth, preferred_element_type=f32)
+        return out.astype(bf16)
+
+    def reduce_block(part, m):
+        keep = half(part, c, rows_half, 0)
+        sent = lax.ppermute(half(part, 1 - c, rows_half, 0), "tp", core)
+        pair = (keep.astype(f32) + sent.astype(f32)).astype(bf16)
+        pairs = []
+        for d in range(n_dp):
+            j = source_of[d][m]
+            for k in (2, 3):
+                pairs.append((d * n_tp + (j ^ k), d * n_tp + (j ^ k ^ 2)))
+        came = lax.ppermute(pair, ("dp", "tp"), pairs)
+        return pair.astype(f32) + came.astype(f32)
+
+    sums_a, sums_b = [], []
+    for m in range(n_dp):
+        if m == 0:
+            pa = project(oa0, half(w_out[:, :cut], 1 - g, o_half, 0))
+            pb = project(ob0, half(w_out[:, cut:], 1 - g, o_half, 0))
+        else:
+            pa = project(zres[("a", m)], yres[("a", m)])
+            pb = project(zres[("b", m)], yres[("b", m)])
+        if m < n_dp - 1:
+            whole = reduce_block(jnp.concatenate([pa, pb], axis=1), m)
+            sums_a.append(whole[:, :cut])
+            sums_b.append(whole[:, cut:])
+        else:
+            sums_a.append(reduce_block(pa, m))
+            sums_b.append(reduce_block(pb, m))
+
+    def chosen(index):
+        a, b = sums_a[0], sums_b[0]
+        for m in range(1, n_dp):
+            a = jnp.where(blk[m] == index, sums_a[m], a)
+            b = jnp.where(blk[m] == index, sums_b[m], b)
+        return jnp.concatenate([a, b], axis=1)
+
+    mine = chosen(t)
+    other = lax.ppermute(chosen(t ^ 1).astype(bf16), "tp", core).astype(f32)
+    first = jnp.where(c == 0, mine, other)
+    second = jnp.where(c == 0, other, mine)
+    summed = jnp.concatenate([first, second], axis=0)
+    own_input = lax.dynamic_slice_in_dim(hidden, t * share, share, 1).astype(f32)
+    layer_out = (own_input + summed).astype(bf16)
+    return (layer_out, residual_sums, list_counts)
+
+
 def solution(mesh):
+    sizes = mesh.shape
+    square = sizes["groups"] == 2 and sizes["dp"] == 4 and sizes["tp"] == 4
     return jax.shard_map(
-        shards,
+        shards if square else wide_slice_shards,
         mesh=mesh,
         in_specs=(
             P(("groups", "dp"), None),

time: 410 us -> 230 us (0.56)
  waiting for transfers between devices: 317 us -> 73.6 us
  starting transfers between devices: 4.84 us -> 72.1 us
  blocking collectives: 9.94 us -> 0 us
  Pallas kernels: 0 us -> 6.12 us
  local copies, waits for them, and re-layouts: 17.3 us -> 12.4 us
    all_gather x4 -> x0, waiting for transfers between devices: 267 us -> none  [the longest x1 125 us: shards(): lax.all_gather(full_cols, 'dp', axis=0, tiled=True)]
    ppermute x0 -> x43, waiting for transfers between devices: none -> 69.5 us  [the longest x12 30.7 us: shards(): yres[key] = lax.ppermute(zres[key], 'groups', swap)]
    ppermute x0 -> x43, starting transfers between devices: none -> 61.6 us  [the longest x12 22.9 us: shards(): zres[key] = lax.ppermute(operand, 'dp', ring_pairs)]
    unnamed x7 -> x0, waiting for transfers between devices: 35 us -> none
    all_to_all x1 -> x0, blocking collectives: 9.94 us -> none  [shards(): lax.all_to_all(send_rows, 'dp', split_axis=0, concat_axis=0, tiled=True)]
    reduce_scatter x1 -> x0, waiting for transfers between devices: 9.36 us -> none  [shards(): lax.psum_scatter(pooled_part.astype(jnp.bfloat16), 'tp', scatter_dimensio...]
    unnamed x28 -> x48, local copies, waits for them, and re-layouts: 11.1 us -> 2.85 us
    pallas_call x0 -> x1, Pallas kernels: none -> 6.12 us  [attend(): pl.pallas_call(attention_kernel, out_shape=jax.ShapeDtypeStruct((tokens,...]
  transfers between devices with their start and end apart: 7 -> 45, of which waited for: 7 -> 18; matrix products, arithmetic and copies ran while one was open for 10% -> 26% of each run, Pallas kernels for 0% -> 3%
where the time goes in v1:
time: 230 us; the launch traced here: 229 us
  waiting for transfers between devices  73.6 us (32%)
  starting transfers between devices  72.1 us (31%)
  matrix products  27.3 us (12%)
  other arithmetic  22 us (10%)
  between operations  15.5 us (7%)
  local copies, waits for them, and re-layouts  12.4 us (5%)
  Pallas kernels  6.12 us (3%)
    ppermute x12, waiting for transfers between devices, shards(): yres[key] = lax.ppermute(zres[key], 'groups', swap)  30.7 us
    ppermute x12, waiting for transfers between devices, shards(): zres[key] = lax.ppermute(operand, 'dp', ring_pairs)  23.4 us
    ppermute x12, starting transfers between devices, shards(): zres[key] = lax.ppermute(operand, 'dp', ring_pairs)  22.9 us
    dot_general x16, matrix products, shards(): part = jnp.dot(rows, res[name.lower(), m], preferred_element_type=f32)  15.5 us
    ppermute x5, waiting for transfers between devices, reduce_block(): came = lax.ppermute(pair, ('dp', 'tp'), pairs)  15 us
    ppermute x12, starting transfers between devices, shards(): yres[key] = lax.ppermute(zres[key], 'groups', swap)  14.2 us
    ppermute x5, starting transfers between devices, reduce_block(): came = lax.ppermute(pair, ('dp', 'tp'), pairs)  9.32 us
    ppermute x2, starting transfers between devices, shards(): lax.ppermute(w_keyval[:, r * HD:(r + 1) * HD], ('groups', 'tp'), rounds[r])  6.53 us
  transfers between devices with their start and end apart: 45, of which 18 were waited for; matrix products, arithmetic and copies ran while one was open for 26% of the time, Pallas kernels for 3%

profile of v1, /device:TPU:0, one launch (start us, length us, event | category | flops | bytes accessed | tf_op | source)
XLA Modules:
  0.0 229.2 jit_solution(11081336566163400618)
XLA Ops:
  0.7 1.9 fusion.133
  2.6 3.0 %collective-permute-start.7 = (bf16[896,128]{1,0:T(8,128)(2,1)}, bf16[896,128]{1,0:T(8,128)(2,1)}, u32[]{:S(2)}, u32[]{:S(2)}) collective-permute-start(bf16[896,128]{1,0:T(8,128)(2,1)} %get-tuple-element.75), channel_id=1, source_target_pairs={{0,1},{1,3},{18,17},{19,19},{4,5},{5,7},{22,21},{23,23},{8,9},{9,1... | collective-permute-start | bytes 688136 | tf_op jit(solution)/shard_map/ppermute | solution.py:243
  5.6 3.5 %collective-permute-start.8 = (bf16[896,128]{1,0:T(8,128)(2,1)}, bf16[896,128]{1,0:T(8,128)(2,1)}, u32[]{:S(2)}, u32[]{:S(2)}) collective-permute-start(bf16[896,128]{1,0:T(8,128)(2,1)} %get-tuple-element.74), channel_id=1, source_target_pairs={{0,0},{1,2},{18,16},{19,18},{4,4},{5,6},{22,20},{23,22},{8,8},{9,1... | collective-permute-start | bytes 688136 | tf_op jit(solution)/shard_map/ppermute | solution.py:243
  10.0 2.4 %collective-permute-start = (bf16[896,256]{1,0:T(8,128)(2,1)}, bf16[896,256]{1,0:T(8,128)(2,1)}, u32[]{:S(2)}, u32[]{:S(2)}) collective-permute-start(bf16[896,256]{1,0:T(8,128)(2,1)} %constant_dynamic-slice_fusion.4), channel_id=1, source_target_pairs={{0,4},{4,12},{12,8},{8,0},{1,5},{5,13},{13,9},{9,1},{2,6},{6,14},{... | collective-permute-start | bytes 1376264 | tf_op jit(solution)/shard_map/ppermute | solution.py:273
  14.1 2.8 %fusion.3 = bf16[32,3584]{1,0:T(8,128)(2,1)S(1)} fusion(bf16[512,3584]{1,0:T(8,128)(2,1)} %param.13, f32[32]{0:T(128)S(1)} %fusion.130, s32[512]{0:T(512)S(1)} %convert_reduce_fusion.3), kind=kOutput, calls=%fused_computation.6 | convolution fusion | flops 117686272 | bytes 3901568 | tf_op jit(solution)/shard_map/dot_general | solution.py:308
  18.0 4.0 %all-to-all-start = ((bf16[4,32,1024]{2,1,0:T(8,128)(2,1)}), bf16[4,32,1024]{2,1,0:T(8,128)(2,1)}, u32[]{:S(2)}, u32[]{:S(2)}) async-start(bf16[4,32,1024]{2,1,0:T(8,128)(2,1)} %pad_maximum_fusion.4), calls=%async_computation | async-start | bytes 524288 | tf_op jit(solution)/shard_map/all_to_all | solution.py:326
  22.0 2.5 %collective-permute-start.41 = (bf16[896,1024]{1,0:T(8,128)(2,1)}, bf16[896,1024]{1,0:T(8,128)(2,1)}, u32[]{:S(2)}, u32[]{:S(2)}) collective-permute-start(bf16[896,1024]{1,0:T(8,128)(2,1)} %param.23), channel_id=1, source_target_pairs={{0,2},{5,7},{10,8},{15,13},{16,18},{21,23},{26,24},{31,29}} | collective-permute-start | bytes 5505032 | tf_op jit(solution)/shard_map/ppermute | solution.py:350
  24.6 2.8 %fusion = f32[512]{0:T(512)S(1)} fusion(bf16[512,3584]{1,0:T(8,128)(2,1)} %param.13), kind=kLoop, calls=%fused_computation.2 | loop fusion | flops 5504512 | bytes 3672064 | tf_op jit(solution)/shard_map/reduce_sum | solution.py:279
  30.2 5.1 %fusion.2 = bf16[512,3584]{1,0:T(8,128)(2,1)} fusion(bf16[512,3584]{1,0:T(8,128)(2,1)} %param.13, f32[3584]{0:T(1024)S(1)} %copy-done.12, f32[512]{0:T(512)S(1)} %add_rsqrt_fusion), kind=kLoop, calls=%fused_computation.4 | loop fusion | flops 7340032 | bytes 7356416 | tf_op jit(solution)/shard_map/convert_element_type | solution.py:279
  35.3 2.5 %fusion.48 = f32[512,256]{1,0:T(8,128)} fusion(bf16[896,256]{1,0:T(8,128)(2,1)} %constant_dynamic-slice_fusion.4, bf16[512,3584]{1,0:T(8,128)(2,1)} %fusion.2, s32[]{:T(128)S(6)} %select_n.220), kind=kOutput, calls=%fused_computation.96 | convolution fusion | flops 234881024 | bytes 1900548 | tf_op jit(solution)/shard_map/dot_general | solution.py:293
  37.8 2.4 %fusion.46 = f32[512,256]{1,0:T(8,128)} fusion(bf16[512,3584]{1,0:T(8,128)(2,1)} %fusion.2, s32[]{:T(128)S(6)} %select_n.220, bf16[896,512]{1,0:T(8,128)(2,1)S(1)} %copy-done, s32[]{:T(128)S(6)} %select_n.225), kind=kOutput, calls=%fused_computation.94 | convolution fusion | flops 234881024 | bytes 1900552 | tf_op jit(solution)/shard_map/dot_general | solution.py:293
  41.2 2.2 constant_dynamic-slice_fusion.6
  43.3 1.9 fusion.63
  62.3 1.7 broadcast_select_fusion.1
  64.0 2.0 collective-permute-start.9
  68.0 3.4 %collective-permute-done.9 = bf16[896,128]{1,0:T(8,128)(2,1)} collective-permute-done((bf16[896,128]{1,0:T(8,128)(2,1)}, bf16[896,128]{1,0:T(8,128)(2,1)}, u32[]{:S(2)}, u32[]{:S(2)}) %collective-permute-start.9) | collective-permute-done | bytes 229408 | tf_op jit(solution)/shard_map/ppermute | solution.py:273
  71.4 2.3 %collective-permute-start.10 = (bf16[896,128]{1,0:T(8,128)(2,1)}, bf16[896,128]{1,0:T(8,128)(2,1)S(1)}, u32[]{:S(2)}, u32[]{:S(2)}) collective-permute-start(bf16[896,128]{1,0:T(8,128)(2,1)} %collective-permute-done.9), channel_id=1, source_target_pairs={{0,4},{4,12},{12,8},{8,0},{1,5},{5,13},{13,9},{9,1},{2,6},{6,14},{... | collective-permute-start | bytes 688136 | tf_op jit(solution)/shard_map/ppermute | solution.py:273
  74.9 1.6 fusion.39
  76.5 1.9 convolution_add_fusion.11
  80.0 2.0 collective-permute-start.2
  83.4 3.5 %collective-permute-done.11 = bf16[896,128]{1,0:T(8,128)(2,1)S(1)} collective-permute-done((bf16[896,128]{1,0:T(8,128)(2,1)}, bf16[896,128]{1,0:T(8,128)(2,1)S(1)}, u32[]{:S(2)}, u32[]{:S(2)}) %collective-permute-start.11) | collective-permute-done | bytes 229408 | tf_op jit(solution)/shard_map/ppermute | solution.py:274
  87.8 6.2 %collective-permute-done.12 = bf16[896,128]{1,0:T(8,128)(2,1)S(1)} collective-permute-done((bf16[896,128]{1,0:T(8,128)(2,1)S(1)}, bf16[896,128]{1,0:T(8,128)(2,1)S(1)}, u32[]{:S(2)}, u32[]{:S(2)}) %collective-permute-start.12) | collective-permute-done | bytes 229408 | tf_op jit(solution)/shard_map/ppermute | solution.py:273
  94.0 5.5 %collective-permute-done.13 = bf16[896,128]{1,0:T(8,128)(2,1)S(1)} collective-permute-done((bf16[896,128]{1,0:T(8,128)(2,1)S(1)}, bf16[896,128]{1,0:T(8,128)(2,1)S(1)}, u32[]{:S(2)}, u32[]{:S(2)}) %collective-permute-start.13) | collective-permute-done | bytes 229408 | tf_op jit(solution)/shard_map/ppermute | solution.py:274
  102.3 1.8 collective-permute-start.16
  104.8 3.5 %collective-permute-done.15 = bf16[256,384]{1,0:T(8,128)(2,1)S(1)} collective-permute-done((bf16[256,384]{1,0:T(8,128)(2,1)S(1)}, bf16[256,384]{1,0:T(8,128)(2,1)S(1)}, u32[]{:S(2)}, u32[]{:S(2)}) %collective-permute-start.15) | collective-permute-done | bytes 196640 | tf_op jit(solution)/shard_map/ppermute | solution.py:273
  108.3 1.7 collective-permute-start.25
  110.9 2.5 %collective-permute-start.24 = (bf16[256,384]{1,0:T(8,128)(2,1)S(1)}, bf16[256,384]{1,0:T(8,128)(2,1)S(1)}, u32[]{:S(2)}, u32[]{:S(2)}) collective-permute-start(bf16[256,384]{1,0:T(8,128)(2,1)S(1)} %collective-permute-done.15), channel_id=1, source_target_pairs={{0,4},{4,12},{12,8},{8,0},{1,5},{5,13},{13,9},{9,1},{2,6},{6,14},{... | collective-permute-start | bytes 589832 | tf_op jit(solution)/shard_map/ppermute | solution.py:273
  114.2 7.5 %collective-permute-done.25 = bf16[256,384]{1,0:T(8,128)(2,1)S(1)} collective-permute-done((bf16[256,384]{1,0:T(8,128)(2,1)S(1)}, bf16[256,384]{1,0:T(8,128)(2,1)S(1)}, u32[]{:S(2)}, u32[]{:S(2)}) %collective-permute-start.25) | collective-permute-done | bytes 196640 | tf_op jit(solution)/shard_map/ppermute | solution.py:274
  121.7 4.0 %collective-permute-start.33 = (bf16[256,384]{1,0:T(8,128)(2,1)S(1)}, bf16[256,384]{1,0:T(8,128)(2,1)S(1)}, u32[]{:S(2)}, u32[]{:S(2)}) collective-permute-start(bf16[256,384]{1,0:T(8,128)(2,1)S(1)} %collective-permute-done.24), channel_id=1, source_target_pairs={{0,4},{4,12},{12,8},{8,0},{1,5},{5,13},{13,9},{9,1},{2,6},{6,14},{... | collective-permute-start | bytes 589832 | tf_op jit(solution)/shard_map/ppermute | solution.py:273
  125.8 1.7 collective-permute-start.26
  129.3 1.8 collective-permute-done.33
  131.1 1.7 collective-permute-start.34
  132.8 2.2 collective-permute-done.5
  135.9 7.5 %collective-permute-done.6 = bf16[896,256]{1,0:T(8,128)(2,1)S(1)} collective-permute-done((bf16[896,256]{1,0:T(8,128)(2,1)S(1)}, bf16[896,256]{1,0:T(8,128)(2,1)S(1)}, u32[]{:S(2)}, u32[]{:S(2)}) %collective-permute-start.6) | collective-permute-done | bytes 458784 | tf_op jit(solution)/shard_map/ppermute | solution.py:274
  144.3 6.1 %shard_map.148 = bf16[512,512]{1,0:T(8,128)(2,1)S(1)} custom-call(f32[512,256]{1,0:T(8,128)S(1)} %fusion.16.q_own, f32[512,256]{1,0:T(8,128)S(1)} %fusion.15.q_oth, f32[512,128]{1,0:T(8,128)S(1)} %get-tuple-element.73.key_ref, f32[512,128]{1,0:T(8,128)S(1)} %get-tuple-element.72.value_ref, f32[512,128]{1,0:T(8,128)S(1)} %get-tuple-element.87.cos_ref, ...), custom_call_target="tpu_custom_call" | custom-call | flops 536870912 | bytes 8388608 | tf_op jit(solution)/shard_map/pallas_call | solution.py:184
  153.1 2.6 %collective-permute-start.40 = (bf16[32,512]{1,0:T(8,128)(2,1)S(1)}, bf16[32,512]{1,0:T(8,128)(2,1)S(1)}, u32[]{:S(2)}, u32[]{:S(2)}) collective-permute-start(bf16[32,512]{1,0:T(8,128)(2,1)S(1)} %fusion.25), channel_id=1, source_target_pairs={{4,0},{12,4},{0,8},{8,12},{5,1},{13,5},{1,9},{9,13},{6,2},{14,6},{... | collective-permute-start | bytes 98312 | tf_op jit(solution)/shard_map/ppermute | solution.py:340
  159.0 2.0 collective-permute-start.17
  165.6 1.8 collective-permute-done.17
  167.3 3.8 %collective-permute-start.19 = (bf16[256,512]{1,0:T(8,128)(2,1)S(1)}, bf16[256,512]{1,0:T(8,128)(2,1)S(1)}, u32[]{:S(2)}, u32[]{:S(2)}) collective-permute-start(bf16[256,512]{1,0:T(8,128)(2,1)S(1)} %collective-permute-done.17), channel_id=1, source_target_pairs={{0,4},{4,12},{12,8},{8,0},{1,5},{5,13},{13,9},{9,1},{2,6},{6,14},{... | collective-permute-start | bytes 786440 | tf_op jit(solution)/shard_map/ppermute | solution.py:273
  172.1 1.7 collective-permute-start.23
  173.9 4.5 %collective-permute-done.19 = bf16[256,512]{1,0:T(8,128)(2,1)S(1)} collective-permute-done((bf16[256,512]{1,0:T(8,128)(2,1)S(1)}, bf16[256,512]{1,0:T(8,128)(2,1)S(1)}, u32[]{:S(2)}, u32[]{:S(2)}) %collective-permute-start.19) | collective-permute-done | bytes 262176 | tf_op jit(solution)/shard_map/ppermute | solution.py:273
  180.7 1.7 collective-permute-start.20
  183.4 5.1 %collective-permute-done.20 = bf16[256,512]{1,0:T(8,128)(2,1)S(1)} collective-permute-done((bf16[256,512]{1,0:T(8,128)(2,1)S(1)}, bf16[256,512]{1,0:T(8,128)(2,1)S(1)}, u32[]{:S(2)}, u32[]{:S(2)}) %collective-permute-start.20) | collective-permute-done | bytes 262176 | tf_op jit(solution)/shard_map/ppermute | solution.py:274
  188.6 4.1 %collective-permute-start.30 = (bf16[256,896]{0,1:T(8,128)(2,1)S(1)}, bf16[256,896]{0,1:T(8,128)(2,1)S(1)}, u32[]{:S(2)}, u32[]{:S(2)}) collective-permute-start(bf16[256,896]{0,1:T(8,128)(2,1)S(1)} %add_convert_fusion.1), channel_id=1, source_target_pairs={{0,2},{1,3},{6,4},{7,5},{9,11},{8,10},{15,13},{14,12},{16,18},{17,... | collective-permute-start | bytes 1376264 | tf_op jit(solution)/shard_map/ppermute | solution.py:389
  196.2 7.5 %collective-permute-done.30 = bf16[256,896]{0,1:T(8,128)(2,1)S(1)} collective-permute-done((bf16[256,896]{0,1:T(8,128)(2,1)S(1)}, bf16[256,896]{0,1:T(8,128)(2,1)S(1)}, u32[]{:S(2)}, u32[]{:S(2)}) %collective-permute-start.30) | collective-permute-done | bytes 458784 | tf_op jit(solution)/shard_map/ppermute | solution.py:389
  203.8 7.5 %collective-permute-done.28 = bf16[256,896]{0,1:T(8,128)(2,1)S(1)} collective-permute-done((bf16[256,896]{0,1:T(8,128)(2,1)S(1)}, bf16[256,896]{0,1:T(8,128)(2,1)S(1)}, u32[]{:S(2)}, u32[]{:S(2)}) %collective-permute-start.28) | collective-permute-done | bytes 458784 | tf_op jit(solution)/shard_map/ppermute | solution.py:389
  215.1 6.4 %all-to-all-start.1 = ((bf16[16,8,256]{2,1,0:T(8,128)(2,1)}), bf16[16,8,256]{2,1,0:T(8,128)(2,1)S(1)}, u32[]{:S(2)}, u32[]{:S(2)}) async-start(bf16[16,8,256]{2,1,0:T(8,128)(2,1)} %bitcast.17), calls=%async_computation.1 | async-start | bytes 131072 | tf_op jit(solution)/shard_map/all_to_all | solution.py:366
  224.3 4.2 %all-to-all-done.1 = bf16[16,8,256]{2,1,0:T(8,128)(2,1)S(1)} async-done(((bf16[16,8,256]{2,1,0:T(8,128)(2,1)}), bf16[16,8,256]{2,1,0:T(8,128)(2,1)S(1)}, u32[]{:S(2)}, u32[]{:S(2)}) %all-to-all-start.1) | async-done | bytes 65568 | tf_op jit(solution)/shard_map/all_to_all | solution.py:366
  (193 shorter events, 51.1 us)
Async XLA Ops:
  2.6 59.7 %collective-permute-start.7 = (bf16[896,128]{1,0:T(8,128)(2,1)}, bf16[896,128]{1,0:T(8,128)(2,1)}, u32[]{:S(2)}, u32[]{:S(2)}) collective-permute-start(bf16[896,128]{1,0:T(8,128)(2,1)} %get-tuple-element.75), channel_id=1, source_target_pairs={{0,1},{1,3},{18,17},{19,19},{4,5},{5,7},{22,21},{23,23},{8,9},{9,1... | collective-permute-start | bytes 688136 | tf_op jit(solution)/shard_map/ppermute | solution.py:243
  5.6 56.6 %collective-permute-start.8 = (bf16[896,128]{1,0:T(8,128)(2,1)}, bf16[896,128]{1,0:T(8,128)(2,1)}, u32[]{:S(2)}, u32[]{:S(2)}) collective-permute-start(bf16[896,128]{1,0:T(8,128)(2,1)} %get-tuple-element.74), channel_id=1, source_target_pairs={{0,0},{1,2},{18,16},{19,18},{4,4},{5,6},{22,20},{23,22},{8,8},{9,1... | collective-permute-start | bytes 688136 | tf_op jit(solution)/shard_map/ppermute | solution.py:243
  10.0 63.7 %collective-permute-start = (bf16[896,256]{1,0:T(8,128)(2,1)}, bf16[896,256]{1,0:T(8,128)(2,1)}, u32[]{:S(2)}, u32[]{:S(2)}) collective-permute-start(bf16[896,256]{1,0:T(8,128)(2,1)} %constant_dynamic-slice_fusion.4), channel_id=1, source_target_pairs={{0,4},{4,12},{12,8},{8,0},{1,5},{5,13},{13,9},{9,1},{2,6},{6,14},{... | collective-permute-start | bytes 1376264 | tf_op jit(solution)/shard_map/ppermute | solution.py:273
  18.0 48.2 %all-to-all-start = ((bf16[4,32,1024]{2,1,0:T(8,128)(2,1)}), bf16[4,32,1024]{2,1,0:T(8,128)(2,1)}, u32[]{:S(2)}, u32[]{:S(2)}) async-start(bf16[4,32,1024]{2,1,0:T(8,128)(2,1)} %pad_maximum_fusion.4), calls=%async_computation | async-start | bytes 524288 | tf_op jit(solution)/shard_map/all_to_all | solution.py:326
  22.0 134.6 %collective-permute-start.41 = (bf16[896,1024]{1,0:T(8,128)(2,1)}, bf16[896,1024]{1,0:T(8,128)(2,1)}, u32[]{:S(2)}, u32[]{:S(2)}) collective-permute-start(bf16[896,1024]{1,0:T(8,128)(2,1)} %param.23), channel_id=1, source_target_pairs={{0,2},{5,7},{10,8},{15,13},{16,18},{21,23},{26,24},{31,29}} | collective-permute-start | bytes 5505032 | tf_op jit(solution)/shard_map/ppermute | solution.py:350
  64.0 7.4 %collective-permute-start.9 = (bf16[896,128]{1,0:T(8,128)(2,1)}, bf16[896,128]{1,0:T(8,128)(2,1)}, u32[]{:S(2)}, u32[]{:S(2)}) collective-permute-start(bf16[896,128]{1,0:T(8,128)(2,1)} %broadcast_select_fusion.1), channel_id=1, source_target_pairs={{0,4},{4,12},{12,8},{8,0},{1,5},{5,13},{13,9},{9,1},{2,6},{6,14},{... | collective-permute-start | bytes 688136 | tf_op jit(solution)/shard_map/ppermute | solution.py:273
  65.9 14.1 %collective-permute-start.14 = (bf16[896,128]{1,0:T(8,128)(2,1)}, bf16[896,128]{1,0:T(8,128)(2,1)}, u32[]{:S(2)}, u32[]{:S(2)}) collective-permute-start(bf16[896,128]{1,0:T(8,128)(2,1)} %broadcast_select_fusion.1), channel_id=1, source_target_pairs={{0,16},{16,0},{1,17},{17,1},{2,18},{18,2},{3,19},{19,3},{4,20},{20... | collective-permute-start | bytes 688136 | tf_op jit(solution)/shard_map/ppermute | solution.py:276
  71.4 12.0 %collective-permute-start.10 = (bf16[896,128]{1,0:T(8,128)(2,1)}, bf16[896,128]{1,0:T(8,128)(2,1)S(1)}, u32[]{:S(2)}, u32[]{:S(2)}) collective-permute-start(bf16[896,128]{1,0:T(8,128)(2,1)} %collective-permute-done.9), channel_id=1, source_target_pairs={{0,4},{4,12},{12,8},{8,0},{1,5},{5,13},{13,9},{9,1},{2,6},{6,14},{... | collective-permute-start | bytes 688136 | tf_op jit(solution)/shard_map/ppermute | solution.py:273
  73.7 26.1 %collective-permute-start.1 = (bf16[896,256]{1,0:T(8,128)(2,1)}, bf16[896,256]{1,0:T(8,128)(2,1)S(1)}, u32[]{:S(2)}, u32[]{:S(2)}) collective-permute-start(bf16[896,256]{1,0:T(8,128)(2,1)} %collective-permute-done), channel_id=1, source_target_pairs={{0,4},{4,12},{12,8},{8,0},{1,5},{5,13},{13,9},{9,1},{2,6},{6,14},{... | collective-permute-start | bytes 1376264 | tf_op jit(solution)/shard_map/ppermute | solution.py:273
  78.5 8.4 %collective-permute-start.11 = (bf16[896,128]{1,0:T(8,128)(2,1)}, bf16[896,128]{1,0:T(8,128)(2,1)S(1)}, u32[]{:S(2)}, u32[]{:S(2)}) collective-permute-start(bf16[896,128]{1,0:T(8,128)(2,1)} %collective-permute-done.9), channel_id=1, source_target_pairs={{0,16},{16,0},{1,17},{17,1},{2,18},{18,2},{3,19},{19,3},{4,20},{20... | collective-permute-start | bytes 688136 | tf_op jit(solution)/shard_map/ppermute | solution.py:274
  80.0 19.9 %collective-permute-start.2 = (bf16[896,256]{1,0:T(8,128)(2,1)}, bf16[896,256]{1,0:T(8,128)(2,1)S(1)}, u32[]{:S(2)}, u32[]{:S(2)}) collective-permute-start(bf16[896,256]{1,0:T(8,128)(2,1)} %collective-permute-done), channel_id=1, source_target_pairs={{0,16},{16,0},{1,17},{17,1},{2,18},{18,2},{3,19},{19,3},{4,20},{20... | collective-permute-start | bytes 1376264 | tf_op jit(solution)/shard_map/ppermute | solution.py:274
  86.9 7.1 %collective-permute-start.12 = (bf16[896,128]{1,0:T(8,128)(2,1)S(1)}, bf16[896,128]{1,0:T(8,128)(2,1)S(1)}, u32[]{:S(2)}, u32[]{:S(2)}) collective-permute-start(bf16[896,128]{1,0:T(8,128)(2,1)S(1)} %collective-permute-done.10), channel_id=1, source_target_pairs={{0,4},{4,12},{12,8},{8,0},{1,5},{5,13},{13,9},{9,1},{2,6},{6,14},{... | collective-permute-start | bytes 688136 | tf_op jit(solution)/shard_map/ppermute | solution.py:273
  87.2 12.4 %collective-permute-start.13 = (bf16[896,128]{1,0:T(8,128)(2,1)S(1)}, bf16[896,128]{1,0:T(8,128)(2,1)S(1)}, u32[]{:S(2)}, u32[]{:S(2)}) collective-permute-start(bf16[896,128]{1,0:T(8,128)(2,1)S(1)} %collective-permute-done.10), channel_id=1, source_target_pairs={{0,16},{16,0},{1,17},{17,1},{2,18},{18,2},{3,19},{19,3},{4,20},{20... | collective-permute-start | bytes 688136 | tf_op jit(solution)/shard_map/ppermute | solution.py:274
  87.8 25.9 %copy-start.15 = (f32[128]{0:T(128)S(1)}, f32[128]{0:T(128)}, u32[]{:S(2)}) copy-start(f32[128]{0:T(128)} %get-tuple-element.79) | copy-start | bytes 1540
  87.8 25.9 %copy-start.16 = (f32[128]{0:T(128)S(1)}, f32[128]{0:T(128)}, u32[]{:S(2)}) copy-start(f32[128]{0:T(128)} %get-tuple-element.80) | copy-start | bytes 1540
  99.6 8.7 %collective-permute-start.15 = (bf16[256,384]{1,0:T(8,128)(2,1)S(1)}, bf16[256,384]{1,0:T(8,128)(2,1)S(1)}, u32[]{:S(2)}, u32[]{:S(2)}) collective-permute-start(bf16[256,384]{1,0:T(8,128)(2,1)S(1)} %copy-done.11), channel_id=1, source_target_pairs={{0,4},{4,12},{12,8},{8,0},{1,5},{5,13},{13,9},{9,1},{2,6},{6,14},{... | collective-permute-start | bytes 589832 | tf_op jit(solution)/shard_map/ppermute | solution.py:273
  99.9 27.6 %collective-permute-start.3 = (bf16[896,256]{1,0:T(8,128)(2,1)S(1)}, bf16[896,256]{1,0:T(8,128)(2,1)S(1)}, u32[]{:S(2)}, u32[]{:S(2)}) collective-permute-start(bf16[896,256]{1,0:T(8,128)(2,1)S(1)} %collective-permute-done.1), channel_id=1, source_target_pairs={{0,4},{4,12},{12,8},{8,0},{1,5},{5,13},{13,9},{9,1},{2,6},{6,14},{... | collective-permute-start | bytes 1376264 | tf_op jit(solution)/shard_map/ppermute | solution.py:273
  101.8 25.7 %copy-start.10 = (bf16[256,512]{1,0:T(8,128)(2,1)S(1)}, bf16[256,512]{1,0:T(8,128)(2,1)}, u32[]{:S(2)}) copy-start(bf16[256,512]{1,0:T(8,128)(2,1)} %constant_dynamic-slice_fusion.3) | copy-start | bytes 786436
  102.3 8.6 %collective-permute-start.16 = (bf16[896,128]{1,0:T(8,128)(2,1)S(1)}, bf16[896,128]{1,0:T(8,128)(2,1)S(1)}, u32[]{:S(2)}, u32[]{:S(2)}) collective-permute-start(bf16[896,128]{1,0:T(8,128)(2,1)S(1)} %collective-permute-done.12), channel_id=1, source_target_pairs={{0,16},{16,0},{1,17},{17,1},{2,18},{18,2},{3,19},{19,3},{4,20},{20... | collective-permute-start | bytes 688136 | tf_op jit(solution)/shard_map/ppermute | solution.py:274
  104.1 23.4 %collective-permute-start.4 = (bf16[896,256]{1,0:T(8,128)(2,1)S(1)}, bf16[896,256]{1,0:T(8,128)(2,1)S(1)}, u32[]{:S(2)}, u32[]{:S(2)}) collective-permute-start(bf16[896,256]{1,0:T(8,128)(2,1)S(1)} %collective-permute-done.1), channel_id=1, source_target_pairs={{0,16},{16,0},{1,17},{17,1},{2,18},{18,2},{3,19},{19,3},{4,20},{20... | collective-permute-start | bytes 1376264 | tf_op jit(solution)/shard_map/ppermute | solution.py:274
  108.3 13.4 %collective-permute-start.25 = (bf16[256,384]{1,0:T(8,128)(2,1)S(1)}, bf16[256,384]{1,0:T(8,128)(2,1)S(1)}, u32[]{:S(2)}, u32[]{:S(2)}) collective-permute-start(bf16[256,384]{1,0:T(8,128)(2,1)S(1)} %collective-permute-done.15), channel_id=1, source_target_pairs={{0,16},{16,0},{1,17},{17,1},{2,18},{18,2},{3,19},{19,3},{4,20},{20... | collective-permute-start | bytes 589832 | tf_op jit(solution)/shard_map/ppermute | solution.py:274
  110.9 10.8 %collective-permute-start.24 = (bf16[256,384]{1,0:T(8,128)(2,1)S(1)}, bf16[256,384]{1,0:T(8,128)(2,1)S(1)}, u32[]{:S(2)}, u32[]{:S(2)}) collective-permute-start(bf16[256,384]{1,0:T(8,128)(2,1)S(1)} %collective-permute-done.15), channel_id=1, source_target_pairs={{0,4},{4,12},{12,8},{8,0},{1,5},{5,13},{13,9},{9,1},{2,6},{6,14},{... | collective-permute-start | bytes 589832 | tf_op jit(solution)/shard_map/ppermute | solution.py:273
  121.7 9.4 %collective-permute-start.33 = (bf16[256,384]{1,0:T(8,128)(2,1)S(1)}, bf16[256,384]{1,0:T(8,128)(2,1)S(1)}, u32[]{:S(2)}, u32[]{:S(2)}) collective-permute-start(bf16[256,384]{1,0:T(8,128)(2,1)S(1)} %collective-permute-done.24), channel_id=1, source_target_pairs={{0,4},{4,12},{12,8},{8,0},{1,5},{5,13},{13,9},{9,1},{2,6},{6,14},{... | collective-permute-start | bytes 589832 | tf_op jit(solution)/shard_map/ppermute | solution.py:273
  125.8 27.3 %collective-permute-start.26 = (bf16[256,384]{1,0:T(8,128)(2,1)S(1)}, bf16[256,384]{1,0:T(8,128)(2,1)S(1)}, u32[]{:S(2)}, u32[]{:S(2)}) collective-permute-start(bf16[256,384]{1,0:T(8,128)(2,1)S(1)} %collective-permute-done.24), channel_id=1, source_target_pairs={{0,16},{16,0},{1,17},{17,1},{2,18},{18,2},{3,19},{19,3},{4,20},{20... | collective-permute-start | bytes 589832 | tf_op jit(solution)/shard_map/ppermute | solution.py:274
  127.5 7.5 %collective-permute-start.5 = (bf16[256,512]{1,0:T(8,128)(2,1)S(1)}, bf16[256,512]{1,0:T(8,128)(2,1)S(1)}, u32[]{:S(2)}, u32[]{:S(2)}) collective-permute-start(bf16[256,512]{1,0:T(8,128)(2,1)S(1)} %copy-done.10), channel_id=1, source_target_pairs={{0,4},{4,12},{12,8},{8,0},{1,5},{5,13},{13,9},{9,1},{2,6},{6,14},{... | collective-permute-start | bytes 786440 | tf_op jit(solution)/shard_map/ppermute | solution.py:273
  128.1 15.3 %collective-permute-start.6 = (bf16[896,256]{1,0:T(8,128)(2,1)S(1)}, bf16[896,256]{1,0:T(8,128)(2,1)S(1)}, u32[]{:S(2)}, u32[]{:S(2)}) collective-permute-start(bf16[896,256]{1,0:T(8,128)(2,1)S(1)} %collective-permute-done.3), channel_id=1, source_target_pairs={{0,16},{16,0},{1,17},{17,1},{2,18},{18,2},{3,19},{19,3},{4,20},{20... | collective-permute-start | bytes 1376264 | tf_op jit(solution)/shard_map/ppermute | solution.py:274
  131.1 26.1 %collective-permute-start.34 = (bf16[256,384]{1,0:T(8,128)(2,1)S(1)}, bf16[256,384]{1,0:T(8,128)(2,1)S(1)}, u32[]{:S(2)}, u32[]{:S(2)}) collective-permute-start(bf16[256,384]{1,0:T(8,128)(2,1)S(1)} %collective-permute-done.33), channel_id=1, source_target_pairs={{0,16},{16,0},{1,17},{17,1},{2,18},{18,2},{3,19},{19,3},{4,20},{20... | collective-permute-start | bytes 589832 | tf_op jit(solution)/shard_map/ppermute | solution.py:274
  135.0 30.6 %collective-permute-start.18 = (bf16[256,512]{1,0:T(8,128)(2,1)S(1)}, bf16[256,512]{1,0:T(8,128)(2,1)S(1)}, u32[]{:S(2)}, u32[]{:S(2)}) collective-permute-start(bf16[256,512]{1,0:T(8,128)(2,1)S(1)} %collective-permute-done.5), channel_id=1, source_target_pairs={{0,16},{16,0},{1,17},{17,1},{2,18},{18,2},{3,19},{19,3},{4,20},{20... | collective-permute-start | bytes 786440 | tf_op jit(solution)/shard_map/ppermute | solution.py:274
  151.3 7.6 %collective-permute-start.38 = (bf16[32,512]{1,0:T(8,128)(2,1)S(1)}, bf16[32,512]{1,0:T(8,128)(2,1)S(1)}, u32[]{:S(2)}, u32[]{:S(2)}) collective-permute-start(bf16[32,512]{1,0:T(8,128)(2,1)S(1)} %fusion.25), channel_id=1, source_target_pairs={{8,0},{0,4},{12,8},{4,12},{9,1},{1,5},{13,9},{5,13},{10,2},{2,6},{... | collective-permute-start | bytes 98312 | tf_op jit(solution)/shard_map/ppermute | solution.py:340
  153.1 7.9 %collective-permute-start.40 = (bf16[32,512]{1,0:T(8,128)(2,1)S(1)}, bf16[32,512]{1,0:T(8,128)(2,1)S(1)}, u32[]{:S(2)}, u32[]{:S(2)}) collective-permute-start(bf16[32,512]{1,0:T(8,128)(2,1)S(1)} %fusion.25), channel_id=1, source_target_pairs={{4,0},{12,4},{0,8},{8,12},{5,1},{13,5},{1,9},{9,13},{6,2},{14,6},{... | collective-permute-start | bytes 98312 | tf_op jit(solution)/shard_map/ppermute | solution.py:340
  156.7 5.8 %collective-permute-start.39 = (bf16[32,512]{1,0:T(8,128)(2,1)S(1)}, bf16[32,512]{1,0:T(8,128)(2,1)S(1)}, u32[]{:S(2)}, u32[]{:S(2)}) collective-permute-start(bf16[32,512]{1,0:T(8,128)(2,1)S(1)} %fusion.25), channel_id=1, source_target_pairs={{12,0},{8,4},{4,8},{0,12},{13,1},{9,5},{5,9},{1,13},{14,2},{10,6},... | collective-permute-start | bytes 98312 | tf_op jit(solution)/shard_map/ppermute | solution.py:340
  157.2 56.4 %collective-permute-start.42 = (bf16[896,1024]{1,0:T(8,128)(2,1)S(1)}, bf16[896,1024]{1,0:T(8,128)(2,1)S(1)}, u32[]{:S(2)}, u32[]{:S(2)}) collective-permute-start(bf16[896,1024]{1,0:T(8,128)(2,1)S(1)} %broadcast_select_fusion), channel_id=1, source_target_pairs={{0,1},{2,3},{5,4},{7,6},{10,11},{8,9},{15,14},{13,12},{16,17},{18,... | collective-permute-start | bytes 5505032 | tf_op jit(solution)/shard_map/ppermute | solution.py:354
  159.0 8.4 %collective-permute-start.17 = (bf16[256,512]{1,0:T(8,128)(2,1)S(1)}, bf16[256,512]{1,0:T(8,128)(2,1)S(1)}, u32[]{:S(2)}, u32[]{:S(2)}) collective-permute-start(bf16[256,512]{1,0:T(8,128)(2,1)S(1)} %collective-permute-done.5), channel_id=1, source_target_pairs={{0,4},{4,12},{12,8},{8,0},{1,5},{5,13},{13,9},{9,1},{2,6},{6,14},{... | collective-permute-start | bytes 786440 | tf_op jit(solution)/shard_map/ppermute | solution.py:273
  161.0 11.0 %collective-permute-start.31 = (bf16[256,896]{0,1:T(8,128)(2,1)S(1)}, bf16[256,896]{0,1:T(8,128)(2,1)S(1)}, u32[]{:S(2)}, u32[]{:S(2)}) collective-permute-start(bf16[256,896]{0,1:T(8,128)(2,1)S(1)} %fusion.50), channel_id=1, source_target_pairs={{0,1},{1,0},{2,3},{3,2},{4,5},{5,4},{6,7},{7,6},{8,9},{9,8},{10,11... | collective-permute-start | bytes 1376264 | tf_op jit(solution)/shard_map/ppermute | solution.py:382
  162.5 1.7 collective-permute-start.35
  164.3 47.1 %collective-permute-start.36 = (bf16[256,384]{0,1:T(8,128)(2,1)S(1)}, bf16[256,384]{0,1:T(8,128)(2,1)S(1)}, u32[]{:S(2)}, u32[]{:S(2)}) collective-permute-start(bf16[256,384]{0,1:T(8,128)(2,1)S(1)} %add_convert_fusion.4), channel_id=1, source_target_pairs={{3,1},{2,0},{5,7},{4,6},{10,8},{11,9},{12,14},{13,15},{19,17},{18,... | collective-permute-start | bytes 589832 | tf_op jit(solution)/shard_map/ppermute | solution.py:389
  167.3 11.1 %collective-permute-start.19 = (bf16[256,512]{1,0:T(8,128)(2,1)S(1)}, bf16[256,512]{1,0:T(8,128)(2,1)S(1)}, u32[]{:S(2)}, u32[]{:S(2)}) collective-permute-start(bf16[256,512]{1,0:T(8,128)(2,1)S(1)} %collective-permute-done.17), channel_id=1, source_target_pairs={{0,4},{4,12},{12,8},{8,0},{1,5},{5,13},{13,9},{9,1},{2,6},{6,14},{... | collective-permute-start | bytes 786440 | tf_op jit(solution)/shard_map/ppermute | solution.py:273
  171.9 11.3 %collective-permute-start.29 = (bf16[256,896]{0,1:T(8,128)(2,1)S(1)}, bf16[256,896]{0,1:T(8,128)(2,1)S(1)}, u32[]{:S(2)}, u32[]{:S(2)}) collective-permute-start(bf16[256,896]{0,1:T(8,128)(2,1)S(1)} %fusion.52), channel_id=1, source_target_pairs={{0,1},{1,0},{2,3},{3,2},{4,5},{5,4},{6,7},{7,6},{8,9},{9,8},{10,11... | collective-permute-start | bytes 1376264 | tf_op jit(solution)/shard_map/ppermute | solution.py:382
  172.1 8.7 %collective-permute-start.23 = (bf16[256,512]{1,0:T(8,128)(2,1)S(1)}, bf16[256,512]{1,0:T(8,128)(2,1)S(1)}, u32[]{:S(2)}, u32[]{:S(2)}) collective-permute-start(bf16[256,512]{1,0:T(8,128)(2,1)S(1)} %collective-permute-done.17), channel_id=1, source_target_pairs={{0,16},{16,0},{1,17},{17,1},{2,18},{18,2},{3,19},{19,3},{4,20},{20... | collective-permute-start | bytes 786440 | tf_op jit(solution)/shard_map/ppermute | solution.py:274
  178.5 14.6 %collective-permute-start.32 = (bf16[256,896]{0,1:T(8,128)(2,1)S(1)}, bf16[256,896]{0,1:T(8,128)(2,1)S(1)}, u32[]{:S(2)}, u32[]{:S(2)}) collective-permute-start(bf16[256,896]{0,1:T(8,128)(2,1)S(1)} %add_convert_fusion), channel_id=1, source_target_pairs={{2,0},{3,1},{7,5},{6,4},{8,10},{9,11},{13,15},{12,14},{18,16},{19,... | collective-permute-start | bytes 1376264 | tf_op jit(solution)/shard_map/ppermute | solution.py:389
  180.7 7.9 %collective-permute-start.20 = (bf16[256,512]{1,0:T(8,128)(2,1)S(1)}, bf16[256,512]{1,0:T(8,128)(2,1)S(1)}, u32[]{:S(2)}, u32[]{:S(2)}) collective-permute-start(bf16[256,512]{1,0:T(8,128)(2,1)S(1)} %collective-permute-done.19), channel_id=1, source_target_pairs={{0,16},{16,0},{1,17},{17,1},{2,18},{18,2},{3,19},{19,3},{4,20},{20... | collective-permute-start | bytes 786440 | tf_op jit(solution)/shard_map/ppermute | solution.py:274
  183.2 10.1 %collective-permute-start.27 = (bf16[256,896]{0,1:T(8,128)(2,1)S(1)}, bf16[256,896]{0,1:T(8,128)(2,1)S(1)}, u32[]{:S(2)}, u32[]{:S(2)}) collective-permute-start(bf16[256,896]{0,1:T(8,128)(2,1)S(1)} %fusion.54), channel_id=1, source_target_pairs={{0,1},{1,0},{2,3},{3,2},{4,5},{5,4},{6,7},{7,6},{8,9},{9,8},{10,11... | collective-permute-start | bytes 1376264 | tf_op jit(solution)/shard_map/ppermute | solution.py:382
  188.6 15.1 %collective-permute-start.30 = (bf16[256,896]{0,1:T(8,128)(2,1)S(1)}, bf16[256,896]{0,1:T(8,128)(2,1)S(1)}, u32[]{:S(2)}, u32[]{:S(2)}) collective-permute-start(bf16[256,896]{0,1:T(8,128)(2,1)S(1)} %add_convert_fusion.1), channel_id=1, source_target_pairs={{0,2},{1,3},{6,4},{7,5},{9,11},{8,10},{15,13},{14,12},{16,18},{17,... | collective-permute-start | bytes 1376264 | tf_op jit(solution)/shard_map/ppermute | solution.py:389
  193.1 1.7 collective-permute-start.21
  193.5 17.9 %collective-permute-start.28 = (bf16[256,896]{0,1:T(8,128)(2,1)S(1)}, bf16[256,896]{0,1:T(8,128)(2,1)S(1)}, u32[]{:S(2)}, u32[]{:S(2)}) collective-permute-start(bf16[256,896]{0,1:T(8,128)(2,1)S(1)} %add_convert_fusion.2), channel_id=1, source_target_pairs={{1,3},{0,2},{4,6},{5,7},{11,9},{10,8},{14,12},{15,13},{17,19},{16,... | collective-permute-start | bytes 1376264 | tf_op jit(solution)/shard_map/ppermute | solution.py:389
  194.9 16.7 %collective-permute-start.22 = (bf16[256,512]{0,1:T(8,128)(2,1)S(1)}, bf16[256,512]{0,1:T(8,128)(2,1)S(1)}, u32[]{:S(2)}, u32[]{:S(2)}) collective-permute-start(bf16[256,512]{0,1:T(8,128)(2,1)S(1)} %add_convert_fusion.3), channel_id=1, source_target_pairs={{3,1},{2,0},{5,7},{4,6},{10,8},{11,9},{12,14},{13,15},{19,17},{18,... | collective-permute-start | bytes 786440 | tf_op jit(solution)/shard_map/ppermute | solution.py:389
  212.6 9.0 %collective-permute-start.37 = (bf16[256,896]{0,1:T(8,128)(2,1)}, bf16[256,896]{0,1:T(8,128)(2,1)}, u32[]{:S(2)}, u32[]{:S(2)}) collective-permute-start(bf16[256,896]{0,1:T(8,128)(2,1)} %pad_maximum_fusion.1), channel_id=1, source_target_pairs={{0,1},{1,0},{2,3},{3,2},{4,5},{5,4},{6,7},{7,6},{8,9},{9,8},{10,11... | collective-permute-start | bytes 1376264 | tf_op jit(solution)/shard_map/ppermute | solution.py:416
  215.1 13.3 %all-to-all-start.1 = ((bf16[16,8,256]{2,1,0:T(8,128)(2,1)}), bf16[16,8,256]{2,1,0:T(8,128)(2,1)S(1)}, u32[]{:S(2)}, u32[]{:S(2)}) async-start(bf16[16,8,256]{2,1,0:T(8,128)(2,1)} %bitcast.17), calls=%async_computation.1 | async-start | bytes 131072 | tf_op jit(solution)/shard_map/all_to_all | solution.py:366
  (20 other events, 243.3 us)

commit v2 on v0

--- a/solution.py
+++ b/solution.py
@@ -1,6 +1,8 @@
 import jax
 import jax.numpy as jnp
 from jax import lax
+from jax.experimental import pallas as pl
+from jax.experimental.pallas import tpu as pltpu
 from jax.sharding import PartitionSpec as P
 
 KV_HEADS = 4
@@ -9,6 +11,8 @@
 
 
 rope_base = 1000000.0
+bf16 = jnp.bfloat16
+f32 = jnp.float32
 
 
 def rotate(values, places):
@@ -36,7 +40,7 @@
     return (segment, member, place)
 
 
-def shards(
+def wide_slice_shards(
     hidden,
     lengths,
     list_ids,
@@ -68,16 +72,22 @@
         lax.all_gather(w_query, "dp", axis=0, tiled=True),
         preferred_element_type=jnp.float32,
     )
+    own_cols = jnp.concatenate(
+        [
+            lax.dynamic_slice_in_dim(full_cols, head_group * HD, HD, 1),
+            lax.dynamic_slice_in_dim(full_cols, kv_width + head_group * HD, HD, 1),
+        ],
+        axis=1,
+    )
     keyval_sum = jnp.dot(
         normed,
-        lax.all_gather(full_cols, "dp", axis=0, tiled=True),
+        lax.all_gather(own_cols, "dp", axis=0, tiled=True),
         preferred_element_type=jnp.float32,
     )
-    keyval_sum = keyval_sum + b_keyval.astype(jnp.float32)
-    keys_all = rotate(keyval_sum[:, :kv_width], place).astype(jnp.bfloat16)
-    values_all = keyval_sum[:, kv_width:].astype(jnp.bfloat16)
-    keys = lax.dynamic_slice_in_dim(keys_all, head_group * HD, HD, 1)
-    values = lax.dynamic_slice_in_dim(values_all, head_group * HD, HD, 1)
+    key_bias = lax.dynamic_slice_in_dim(b_keyval, head_group * HD, HD, 0)
+    value_bias = lax.dynamic_slice_in_dim(b_keyval, kv_width + head_group * HD, HD, 0)
+    keys = rotate(keyval_sum[:, :HD] + key_bias.astype(jnp.float32), place).astype(jnp.bfloat16)
+    values = (keyval_sum[:, HD:] + value_bias.astype(jnp.float32)).astype(jnp.bfloat16)
     query = rotate(query_sum + b_query.astype(jnp.float32), place).astype(jnp.bfloat16)
     grouped = query.reshape(token_count, query_cols // HD, HD)
     scores = jnp.einsum("sgd,td->gst", grouped, keys, preferred_element_type=jnp.float32) * HD ** (
@@ -141,9 +151,349 @@
     return (layer_out, residual_sums, list_counts)
 
 
+def prep_kernel(sc, hidden_ref, gain_ref, member_ref, blocks_ref, own_ref, pooled_ref):
+    wide = hidden_ref[...].astype(f32)
+    scale = lax.rsqrt(jnp.mean(wide * wide, axis=1, keepdims=True) + 1e-06)
+    n, _, share = blocks_ref.shape
+    for m in range(n):
+        at = pl.ds(pl.multiple_of(sc[m] * share, 128), share)
+        part = hidden_ref[:, at].astype(f32)
+        blocks_ref[m] = (part * scale * gain_ref[:, at]).astype(bf16)
+    own = hidden_ref[:, pl.ds(pl.multiple_of(sc[4] * share, 128), share)]
+    own_ref[...] = own
+    total = jnp.dot(member_ref[...], own, preferred_element_type=f32)
+
+    @pl.when(pl.program_id(0) == 0)
+    def _():
+        pooled_ref[...] = jnp.zeros_like(pooled_ref)
+
+    pooled_ref[...] += total
+
+
+def prepare(scalars, hidden, gain, member, n):
+    tokens, width = hidden.shape
+    share = width // n
+    captions = member.shape[0]
+    rows = 128
+    return pl.pallas_call(
+        prep_kernel,
+        grid_spec=pltpu.PrefetchScalarGridSpec(
+            num_scalar_prefetch=1,
+            grid=(tokens // rows,),
+            in_specs=[
+                pl.BlockSpec((rows, width), lambda i, s: (i, 0)),
+                pl.BlockSpec((1, width), lambda i, s: (0, 0)),
+                pl.BlockSpec((captions, rows), lambda i, s: (0, i)),
+            ],
+            out_specs=[
+                pl.BlockSpec((n, rows, share), lambda i, s: (0, i, 0)),
+                pl.BlockSpec((rows, share), lambda i, s: (i, 0)),
+                pl.BlockSpec((captions, share), lambda i, s: (0, 0)),
+            ],
+        ),
+        out_shape=[
+            jax.ShapeDtypeStruct((n, tokens, share), bf16),
+            jax.ShapeDtypeStruct((tokens, share), bf16),
+            jax.ShapeDtypeStruct((captions, share), f32),
+        ],
+        compiler_params=pltpu.CompilerParams(vmem_limit_bytes=32 * 1024 * 1024),
+        cost_estimate=pl.CostEstimate(
+            flops=8 * tokens * width, bytes_accessed=4 * tokens * width, transcendentals=0
+        ),
+    )(scalars, hidden, gain[None, :], member)
+
+
+def attention_kernel(
+    sc,
+    own_ref,
+    oth_ref,
+    bq_ref,
+    bkv_ref,
+    cos_ref,
+    sin_ref,
+    seg_col,
+    seg_row,
+    member_ref,
+    inverse_ref,
+    hits_ref,
+    out_ref,
+    lists_ref,
+):
+    def turn(x, cosine, sine):
+        return (x * cosine + pltpu.roll(x, HD // 2, 1) * sine).astype(bf16)
+
+    t, c, g = sc[4], sc[5], sc[6]
+    tokens = own_ref.shape[0]
+    wide = own_ref.shape[1] - HD
+    heads = wide // HD
+    kv_width = bkv_ref.shape[1] // 2
+    at_key = pl.ds(pl.multiple_of(t * HD, HD), HD)
+    at_value = pl.ds(pl.multiple_of(kv_width + t * HD, HD), HD)
+    first, second = own_ref[:, wide:], oth_ref[:, wide:]
+    keys = jnp.where(g == 0, first, second) + bkv_ref[:, at_key]
+    values = (jnp.where(g == 0, second, first) + bkv_ref[:, at_value]).astype(bf16)
+    keys = turn(keys, cos_ref[...], sin_ref[...])
+    rows = 128
+    per_half = tokens // 2 // rows
+    pooled = jnp.zeros((member_ref.shape[0], 2 * wide), f32)
+    for i in range(tokens // rows):
+        at = pl.ds(i * rows, rows)
+        cosine, sine = cos_ref[at, :], sin_ref[at, :]
+        allowed = seg_col[at, :] == seg_row[...]
+        slot = jnp.bitwise_xor(c, i // per_half)
+        to = pl.ds((i % per_half) * rows, rows)
+        out = []
+        for part, ref in enumerate((own_ref, oth_ref)):
+            for h in range(heads):
+                lo = h * HD
+                bias_at = pl.ds(
+                    pl.multiple_of(jnp.bitwise_xor(g, part) * wide + lo, HD), HD
+                )
+                query = turn(ref[at, lo : lo + HD] + bq_ref[:, bias_at], cosine, sine)
+                scores = lax.dot_general(
+                    query, keys, (((1,), (1,)), ((), ())), preferred_element_type=f32
+                ) * HD ** (-0.5)
+                scores = jnp.where(allowed, scores, -1e30)
+                top = jnp.max(scores, axis=1, keepdims=True)
+                weights = jnp.exp(scores - top)
+                probs = (weights / jnp.sum(weights, axis=1, keepdims=True)).astype(bf16)
+                out.append(jnp.dot(probs, values, preferred_element_type=f32).astype(bf16))
+        out = jnp.concatenate(out, axis=1)
+        out_ref[slot, to, :] = out
+        pooled = pooled + jnp.dot(member_ref[:, at], out, preferred_element_type=f32)
+    pooled = (pooled * inverse_ref[...]).astype(bf16)
+    lists_ref[...] = jnp.dot(hits_ref[...], pooled, preferred_element_type=f32).astype(bf16)
+
+
+def attend(scalars, own, oth, bq, bkv, cosine, sine, segment, member, inverse, hits):
+    tokens = own.shape[0]
+    query_cols = 2 * (own.shape[1] - HD)
+    vmem = pl.BlockSpec(memory_space=pltpu.VMEM)
+    return pl.pallas_call(
+        attention_kernel,
+        in_specs=[pl.BlockSpec(memory_space=pltpu.SMEM)] + [vmem] * 11,
+        out_specs=[vmem] * 2,
+        out_shape=[
+            jax.ShapeDtypeStruct((2, tokens // 2, query_cols), bf16),
+            jax.ShapeDtypeStruct((hits.shape[0], query_cols), bf16),
+        ],
+        compiler_params=pltpu.CompilerParams(vmem_limit_bytes=32 * 1024 * 1024),
+        cost_estimate=pl.CostEstimate(
+            flops=4 * tokens * tokens * query_cols,
+            bytes_accessed=8 * 1024 * 1024,
+            transcendentals=tokens * tokens * query_cols // HD,
+        ),
+    )(
+        scalars,
+        own,
+        oth,
+        bq[None, :],
+        bkv[None, :],
+        cosine,
+        sine,
+        segment[:, None],
+        segment[None, :],
+        member,
+        inverse,
+        hits,
+    )
+
+
+def folded_ring(n):
+    return [0] + list(range(1, n, 2)) + list(range(2 * ((n - 1) // 2), 0, -2))
+
+
+def after(value, *earlier):
+    return lax.optimization_barrier((value, *earlier))[0]
+
+
+def shards(
+    hidden,
+    lengths,
+    list_ids,
+    list_slot,
+    gain,
+    w_query,
+    b_query,
+    w_keyval,
+    b_keyval,
+    w_out,
+    w_pool,
+    centroids,
+):
+    tokens, width = hidden.shape
+    captions = lengths.shape[1]
+    n_dp, n_tp = lax.axis_size("dp"), lax.axis_size("tp")
+    share = width // n_dp
+    ring = folded_ring(n_dp)
+    place_in = {v: i for i, v in enumerate(ring)}
+    source_of = [[ring[(place_in[d] - m) % n_dp] for m in range(n_dp)] for d in range(n_dp)]
+    forward = [(ring[i], ring[(i + 1) % n_dp]) for i in range(n_dp)]
+    backward = [(b, a) for a, b in forward]
+    swap = [(0, 1), (1, 0)]
+    core = [(i, i ^ 1) for i in range(n_tp)]
+    across = [(i, i ^ 2) for i in range(n_tp)]
+    table = []
+    for gg in range(2):
+        for d in range(n_dp):
+            for tt in range(n_tp):
+                chip = [source_of[d][m] // 2 == tt // 2 for m in range(n_dp)]
+                mine = tt in (source_of[d][0], source_of[d][2])
+                table.append(
+                    [*source_of[d], tt, tt % 2, gg, int(chip[0]), int(chip[1]), int(mine), int(tt == d), d]
+                )
+    scalars = lax.dynamic_slice_in_dim(
+        jnp.array(table, jnp.int32), lax.axis_index(("groups", "dp", "tp")), 1, 0
+    )[0]
+    g, t, z = lax.axis_index("groups"), lax.axis_index("tp"), lax.axis_index("dp")
+    first_group = g == 0
+    here_0, here_1, mine_a = scalars[7] == 1, scalars[8] == 1, scalars[9] == 1
+
+    q_half = w_query.shape[1] // 2
+    o_half = w_out.shape[0] // 2
+    per_dev = w_keyval.shape[1] // HD
+    rounds = [[] for _ in range(per_dev)]
+    for gg in range(2):
+        for tt in range(n_tp):
+            col = gg * KV_HEADS + tt
+            rounds[col % per_dev].append((gg * n_tp + col // per_dev, gg * n_tp + tt))
+    came = [
+        lax.ppermute(w_keyval[:, r * HD : (r + 1) * HD], ("groups", "tp"), rounds[r])
+        for r in range(per_dev)
+    ]
+    kv_own = came[0]
+    for r in range(1, per_dev):
+        kv_own = jnp.where(t % per_dev == r, came[r], kv_own)
+    o_own = jnp.where(first_group, w_out[:o_half], w_out[o_half:])
+    o_oth = jnp.where(first_group, w_out[o_half:], w_out[:o_half])
+    q_own = jnp.where(first_group, w_query[:, :q_half], w_query[:, q_half:])
+    q_oth = jnp.where(first_group, w_query[:, q_half:], w_query[:, :q_half])
+    qk_own = jnp.concatenate([q_own, kv_own], axis=1)
+    cut = share // 256 * 128
+
+    o_f = lax.ppermute(o_own, "dp", forward)
+    qk_f = lax.ppermute(qk_own, "dp", forward)
+    qk_r = lax.ppermute(qk_own, "dp", backward)
+    kv_y = lax.ppermute(kv_own, "groups", swap)
+    o_fy = lax.ppermute(o_f, "groups", swap)
+    qk_fy = lax.ppermute(qk_f, "groups", swap)
+    qk_s = lax.ppermute(after(qk_f, o_fy), "dp", forward)
+    qk_ry = lax.ppermute(qk_r, "groups", swap)
+    o_r = lax.ppermute(after(o_own, qk_r), "dp", backward)
+    qk_sy = lax.ppermute(qk_s, "groups", swap)
+    o_sa = lax.ppermute(after(o_f[:, :cut], qk_s), "dp", forward)
+    o_ry = lax.ppermute(o_r, "groups", swap)
+    o_sb = lax.ppermute(after(o_f[:, cut:], o_r), "dp", forward)
+    o_say = lax.ppermute(o_sa, "groups", swap)
+    o_sby = lax.ppermute(o_sb, "groups", swap)
+
+    segment, member, place = positions_of(lengths[0], tokens, captions)
+    member = member.astype(bf16)
+    freq = rope_base ** (-(2.0 / HD) * jnp.arange(HD // 2, dtype=f32))
+    angle = place.astype(f32)[:, None] * freq[None, :]
+    cosine, sine = jnp.cos(angle), jnp.sin(angle)
+    cosine = jnp.concatenate([cosine, cosine], axis=1)
+    sine = jnp.concatenate([-sine, sine], axis=1)
+    blocks, own_input, pooled_hidden = prepare(scalars, hidden, gain, member, n_dp)
+    inverse = 1.0 / lengths[0].astype(f32)[:, None]
+    pooled_hidden = (pooled_hidden * inverse).astype(bf16)
+    lists_total = list_slot.shape[0]
+    slot = jnp.sum(
+        jnp.where(
+            list_ids.reshape(-1)[:, None] == jnp.arange(lists_total, dtype=jnp.int32)[None, :],
+            list_slot[None, :],
+            0,
+        ),
+        axis=1,
+        dtype=jnp.int32,
+    )
+    hits = (jnp.arange(lists_total, dtype=jnp.int32)[:, None] == slot[None, :]).astype(bf16)
+    local_counts = jnp.sum(hits.astype(f32), axis=1)
+    hidden_lists = jnp.dot(hits, pooled_hidden, preferred_element_type=f32)
+
+    def dot(a, b):
+        return jnp.dot(a, b, preferred_element_type=f32)
+
+    qk_oth = jnp.concatenate([q_oth, kv_y], axis=1)
+    sum_own = dot(blocks[0], qk_own) + dot(blocks[1], qk_f)
+    sum_own = sum_own + dot(blocks[3], qk_r) + dot(blocks[2], qk_s)
+    sum_oth = dot(blocks[0], qk_oth) + dot(blocks[1], qk_fy)
+    sum_oth = sum_oth + dot(blocks[3], qk_ry) + dot(blocks[2], qk_sy)
+    attn, attn_lists = attend(
+        scalars,
+        sum_own,
+        sum_oth,
+        b_query.astype(f32),
+        b_keyval.astype(f32),
+        cosine,
+        sine,
+        segment,
+        member,
+        inverse,
+        hits,
+    )
+
+    lists_sum = attn_lists.astype(f32)
+    for m in range(1, n_dp):
+        pairs = [(source_of[d][m], d) for d in range(n_dp)]
+        lists_sum = lists_sum + lax.ppermute(attn_lists, "dp", pairs).astype(f32)
+    lists_sum = lists_sum.astype(bf16)
+    plane = (dot(lists_sum[:, :q_half], o_own) + dot(lists_sum[:, q_half:], o_oth)).astype(bf16)
+    plane = plane.astype(f32) + lax.ppermute(plane, "tp", core).astype(f32)
+    plane16 = plane.astype(bf16)
+    plane = plane + lax.ppermute(plane16, "tp", across).astype(f32)
+    plane = (jnp.where(t == z, plane, 0.0) + hidden_lists).astype(bf16)
+    vec_lists = dot(plane, w_pool).astype(bf16)
+    lists_own, cols = centroids.shape
+    late = vec_lists.reshape(n_dp, lists_own, n_tp, cols).transpose(0, 2, 1, 3)
+    late = jnp.concatenate(
+        [
+            late,
+            jnp.broadcast_to(
+                local_counts.astype(bf16).reshape(n_dp, 1, lists_own, 1),
+                (n_dp, n_tp, lists_own, HD),
+            ),
+        ],
+        axis=3,
+    ).reshape(n_dp * n_tp, lists_own, cols + HD)
+    late = lax.all_to_all(late, ("dp", "tp"), split_axis=0, concat_axis=0, tiled=True)
+    late = late.reshape(n_dp, n_tp, lists_own, cols + HD).astype(f32)
+    totals = jnp.sum(late[..., :cols], axis=(0, 1))
+    counts = jnp.sum(late[:, 0, :, cols], axis=0)
+    residual_sums = totals - counts[:, None] * centroids
+    list_counts = counts.astype(jnp.int32)
+
+    def project(rows, own, oth):
+        return (dot(rows[:, :q_half], own) + dot(rows[:, q_half:], oth)).astype(bf16)
+
+    def reduce_pair(weights_a, weights_b, a_here):
+        sent = jnp.concatenate([project(attn[1], *weights_a), project(attn[1], *weights_b)], axis=1)
+        came = lax.ppermute(sent, "tp", core).astype(f32)
+        n = weights_a[0].shape[1]
+        sum_a = project(attn[0], *weights_a).astype(f32) + came[:, :n]
+        sum_b = project(attn[0], *weights_b).astype(f32) + came[:, n:]
+        stays = jnp.where(a_here, sum_a, sum_b)
+        goes = jnp.where(a_here, sum_b, sum_a).astype(bf16)
+        return stays + lax.ppermute(goes, "tp", across).astype(f32)
+
+    block_b = reduce_pair((o_f, o_fy), (o_r, o_ry), here_1)
+    block_aa = reduce_pair((o_own[:, :cut], o_oth[:, :cut]), (o_sa, o_say), here_0)
+    block_ab = reduce_pair((o_own[:, cut:], o_oth[:, cut:]), (o_sb, o_sby), here_0)
+    block_a = jnp.concatenate([block_aa, block_ab], axis=1)
+    keep = jnp.where(mine_a, block_a, block_b)
+    give = jnp.where(mine_a, block_b, block_a).astype(bf16)
+    got = lax.ppermute(give, "tp", core).astype(f32)
+    low = t % 2 == 0
+    summed = jnp.concatenate([jnp.where(low, keep, got), jnp.where(low, got, keep)], axis=0)
+    layer_out = (own_input.astype(f32) + summed).astype(bf16)
+    return (layer_out, residual_sums, list_counts)
+
+
 def solution(mesh):
+    sizes = mesh.shape
+    square = sizes["groups"] == 2 and sizes["dp"] == 4 and sizes["tp"] == 4
     return jax.shard_map(
-        shards,
+        shards if square else wide_slice_shards,
         mesh=mesh,
         in_specs=(
             P(("groups", "dp"), None),

time: 410 us -> 195 us (0.48)
  waiting for transfers between devices: 317 us -> 72.5 us
  starting transfers between devices: 4.84 us -> 41.9 us
  between operations: 14.4 us -> 3.3 us
  Pallas kernels: 0 us -> 10.1 us
  blocking collectives: 9.94 us -> 0 us
  other arithmetic: 19.7 us -> 27 us
  local copies, waits for them, and re-layouts: 17.3 us -> 11 us
    all_gather x4 -> x0, waiting for transfers between devices: 267 us -> none  [the longest x1 125 us: shards(): lax.all_gather(full_cols, 'dp', axis=0, tiled=True)]
    ppermute x0 -> x29, waiting for transfers between devices: none -> 72.5 us  [the longest x1 25.1 us: shards(): qk_sy = lax.ppermute(qk_s, 'groups', swap)]
    ppermute x0 -> x29, starting transfers between devices: none -> 36.2 us  [the longest x2 6.56 us: shards(): lax.ppermute(w_keyval[:, r * HD:(r + 1) * HD], ('groups', 'tp'), rounds[r])]
    unnamed x7 -> x0, waiting for transfers between devices: 35 us -> none
    pallas_call x0 -> x2, Pallas kernels: none -> 10.1 us  [the longest x1 7.17 us: attend(): pl.pallas_call(attention_kernel, in_specs=[pl.BlockSpec(memory_space=pltp...]
    all_to_all x1 -> x0, blocking collectives: 9.94 us -> none  [shards(): lax.all_to_all(send_rows, 'dp', split_axis=0, concat_axis=0, tiled=True)]
    reduce_scatter x1 -> x0, waiting for transfers between devices: 9.36 us -> none  [shards(): lax.psum_scatter(pooled_part.astype(jnp.bfloat16), 'tp', scatter_dimensio...]
    select_n x0 -> x4, other arithmetic: none -> 6.97 us  [the longest x1 2.03 us: shards(): o_oth = jnp.where(first_group, w_out[o_half:], w_out[:o_half])]
  transfers between devices with their start and end apart: 7 -> 30, of which waited for: 7 -> 8; matrix products, arithmetic and copies ran while one was open for 10% -> 29% of each run, Pallas kernels for 0% -> 5%
where the time goes in v2:
time: 195 us; the launch traced here: 194 us
  waiting for transfers between devices  72.5 us (37%)
  starting transfers between devices  41.9 us (21%)
  matrix products  27.7 us (14%)
  other arithmetic  27 us (14%)
  local copies, waits for them, and re-layouts  11 us (6%)
  Pallas kernels  10.1 us (5%)
  between operations  3.3 us (2%)
    dot_general x35, matrix products, dot(): return jnp.dot(a, b, preferred_element_type=f32)  27.7 us
    ppermute x1, waiting for transfers between devices, shards(): qk_sy = lax.ppermute(qk_s, 'groups', swap)  25.1 us
    ppermute x3, waiting for transfers between devices, reduce_pair(): return stays + lax.ppermute(goes, 'tp', across).astype(f32)  13.8 us
    ppermute x1, waiting for transfers between devices, shards(): qk_f = lax.ppermute(qk_own, 'dp', forward)  13.7 us
    ppermute x1, waiting for transfers between devices, shards(): o_r = lax.ppermute(after(o_own, qk_r), 'dp', backward)  13.4 us
    pallas_call x1, Pallas kernels, attend(): pl.pallas_call(attention_kernel, in_specs=[pl.BlockSpec(memory_space=pltp...  7.17 us
    ppermute x2, starting transfers between devices, shards(): lax.ppermute(w_keyval[:, r * HD:(r + 1) * HD], ('groups', 'tp'), rounds[r])  6.56 us
    all_to_all x1, starting transfers between devices, shards(): lax.all_to_all(late, ('dp', 'tp'), split_axis=0, concat_axis=0, tiled=True)  5.66 us
  transfers between devices with their start and end apart: 30, of which 8 were waited for; matrix products, arithmetic and copies ran while one was open for 29% of the time, Pallas kernels for 5%

profile of v2, /device:TPU:0, one launch (start us, length us, event | category | flops | bytes accessed | tf_op | source)
XLA Modules:
  0.0 193.5 jit_solution(12244582869401776071)
XLA Ops:
  0.7 2.0 %fusion.119 = (bf16[896,128]{1,0:T(8,128)(2,1)}, bf16[896,128]{1,0:T(8,128)(2,1)}) fusion(bf16[896,256]{1,0:T(8,128)(2,1)} %param.20), kind=kLoop, calls=%fused_computation.180 | loop fusion | bytes 917504 | tf_op jit(solution)/shard_map/slice | solution.py:361
  2.7 3.1 %collective-permute-start = (bf16[896,128]{1,0:T(8,128)(2,1)}, bf16[896,128]{1,0:T(8,128)(2,1)}, u32[]{:S(2)}, u32[]{:S(2)}) collective-permute-start(bf16[896,128]{1,0:T(8,128)(2,1)} %get-tuple-element.32), channel_id=1, source_target_pairs={{0,1},{1,3},{18,17},{19,19},{4,5},{5,7},{22,21},{23,23},{8,9},{9,1... | collective-permute-start | bytes 688136 | tf_op jit(solution)/shard_map/ppermute | solution.py:361
  5.7 3.5 %collective-permute-start.1 = (bf16[896,128]{1,0:T(8,128)(2,1)}, bf16[896,128]{1,0:T(8,128)(2,1)}, u32[]{:S(2)}, u32[]{:S(2)}) collective-permute-start(bf16[896,128]{1,0:T(8,128)(2,1)} %get-tuple-element.31), channel_id=1, source_target_pairs={{0,0},{1,2},{18,16},{19,18},{4,4},{5,6},{22,20},{23,22},{8,8},{9,1... | collective-permute-start | bytes 688136 | tf_op jit(solution)/shard_map/ppermute | solution.py:361
  9.2 2.0 %broadcast_select_fusion = (bf16[256,896]{1,0:T(8,128)(2,1)}, bf16[256,896]{1,0:T(8,128)(2,1)S(1)}) fusion(pred[]{:T(512)S(6)} %eq.82, bf16[512,896]{1,0:T(8,128)(2,1)} %param.22), kind=kLoop, calls=%fused_computation.82 | loop fusion | flops 458752 | bytes 1835009 | tf_op jit(solution)/shard_map/jit(_where)/select_n | solution.py:368
  11.3 2.4 %collective-permute-start.4 = (bf16[256,896]{1,0:T(8,128)(2,1)S(1)}, bf16[256,896]{1,0:T(8,128)(2,1)}, u32[]{:S(2)}, u32[]{:S(2)}) collective-permute-start(bf16[256,896]{1,0:T(8,128)(2,1)S(1)} %get-tuple-element.17), channel_id=1, source_target_pairs={{0,4},{4,12},{12,8},{8,0},{1,5},{5,13},{13,9},{9,1},{2,6},{6,14},{... | collective-permute-start | bytes 1376264 | tf_op jit(solution)/shard_map/ppermute | solution.py:374
  14.1 2.0 %broadcast_select_fusion.2 = (bf16[896,256]{1,0:T(8,128)(2,1)}, bf16[896,256]{1,0:T(8,128)(2,1)S(1)}) fusion(pred[]{:T(512)S(6)} %eq.82, bf16[896,512]{1,0:T(8,128)(2,1)} %param.18), kind=kLoop, calls=%fused_computation.84 | loop fusion | flops 458752 | bytes 1835009 | tf_op jit(solution)/shard_map/jit(_where)/select_n | solution.py:370
  17.0 1.8 fusion.69
  19.9 1.7 broadcast_select_fusion.4
  21.6 1.9 pad_maximum_fusion.2
  23.4 2.6 %collective-permute-start.2 = (bf16[896,384]{1,0:T(8,128)(2,1)}, bf16[896,384]{1,0:T(8,128)(2,1)}, u32[]{:S(2)}, u32[]{:S(2)}) collective-permute-start(bf16[896,384]{1,0:T(8,128)(2,1)} %pad_maximum_fusion.2), channel_id=1, source_target_pairs={{0,4},{4,12},{12,8},{8,0},{1,5},{5,13},{13,9},{9,1},{2,6},{6,14},{... | collective-permute-start | bytes 2064392 | tf_op jit(solution)/shard_map/ppermute | solution.py:375
  27.0 1.2 constant_dynamic-slice_fusion
  28.2 2.0 %collective-permute-start.7 = (bf16[896,128]{1,0:T(8,128)(2,1)}, bf16[896,128]{1,0:T(8,128)(2,1)}, u32[]{:S(2)}, u32[]{:S(2)}) collective-permute-start(bf16[896,128]{1,0:T(8,128)(2,1)} %broadcast_select_fusion.4), channel_id=1, source_target_pairs={{0,16},{16,0},{1,17},{17,1},{2,18},{18,2},{3,19},{19,3},{4,20},{20... | collective-permute-start | bytes 688136 | tf_op jit(solution)/shard_map/ppermute | solution.py:377
  34.8 2.0 %copy-done.1 = bf16[512,3584]{1,0:T(8,128)(2,1)S(1)} copy-done((bf16[512,3584]{1,0:T(8,128)(2,1)S(1)}, bf16[512,3584]{1,0:T(8,128)(2,1)}, u32[]{:S(2)}) %copy-start.1) | copy-done | bytes 3670040
  38.2 2.9 %shard_map.148 = (bf16[4,512,896]{2,1,0:T(8,128)(2,1)S(1)}, bf16[512,896]{1,0:T(8,128)(2,1)S(1)}, f32[32,896]{1,0:T(8,128)S(1)}) custom-call(s32[12]{0:T(128)S(1)} %copy-done.10, bf16[512,3584]{1,0:T(8,128)(2,1)S(1)} %copy-done.1, f32[1,3584]{1,0:T(1,128)S(1)} %broadcast_in_dim.67.gain_ref, bf16[32,512]{1,0:T(8,128)(2,1)S(1)} %copy-done.2), custom_call_target="tpu_custom_call" | custom-call | flops 14680064 | bytes 7340032 | tf_op jit(solution)/shard_map/pallas_call | solution.py:178
  41.2 13.7 %collective-permute-done.2 = bf16[896,384]{1,0:T(8,128)(2,1)} collective-permute-done((bf16[896,384]{1,0:T(8,128)(2,1)}, bf16[896,384]{1,0:T(8,128)(2,1)}, u32[]{:S(2)}, u32[]{:S(2)}) %collective-permute-start.2) | collective-permute-done | bytes 688160 | tf_op jit(solution)/shard_map/ppermute | solution.py:375
  54.9 1.7 fusion.37
  58.5 3.0 %collective-permute-start.15 = (bf16[256,896]{1,0:T(8,128)(2,1)S(1)}, bf16[256,896]{1,0:T(8,128)(2,1)S(1)}, u32[]{:S(2)}, u32[]{:S(2)}) collective-permute-start(bf16[256,896]{1,0:T(8,128)(2,1)S(1)} %copy-done.14), channel_id=1, source_target_pairs={{4,0},{12,4},{8,12},{0,8},{5,1},{13,5},{9,13},{1,9},{6,2},{14,6},{... | collective-permute-start | bytes 1376264 | tf_op jit(solution)/shard_map/ppermute | solution.py:382
  61.5 2.0 %collective-permute-start.9 = (bf16[896,384]{1,0:T(8,128)(2,1)}, bf16[896,384]{1,0:T(8,128)(2,1)S(1)}, u32[]{:S(2)}, u32[]{:S(2)}) collective-permute-start(bf16[896,384]{1,0:T(8,128)(2,1)} %collective-permute-done.3), channel_id=1, source_target_pairs={{0,16},{16,0},{1,17},{17,1},{2,18},{18,2},{3,19},{19,3},{4,20},{20... | collective-permute-start | bytes 2064392 | tf_op jit(solution)/shard_map/ppermute | solution.py:381
  63.5 1.8 fusion.32
  65.3 1.8 fusion.35
  67.1 13.4 %collective-permute-done.15 = bf16[256,896]{1,0:T(8,128)(2,1)S(1)} collective-permute-done((bf16[256,896]{1,0:T(8,128)(2,1)S(1)}, bf16[256,896]{1,0:T(8,128)(2,1)S(1)}, u32[]{:S(2)}, u32[]{:S(2)}) %collective-permute-start.15) | collective-permute-done | bytes 458784 | tf_op jit(solution)/shard_map/ppermute | solution.py:382
  81.2 2.0 %collective-permute-start.10 = (bf16[896,384]{1,0:T(8,128)(2,1)S(1)}, bf16[896,384]{1,0:T(8,128)(2,1)S(1)}, u32[]{:S(2)}, u32[]{:S(2)}) collective-permute-start(bf16[896,384]{1,0:T(8,128)(2,1)S(1)} %collective-permute-done.6), channel_id=1, source_target_pairs={{0,16},{16,0},{1,17},{17,1},{2,18},{18,2},{3,19},{19,3},{4,20},{20... | collective-permute-start | bytes 2064392 | tf_op jit(solution)/shard_map/ppermute | solution.py:383
  83.9 1.7 fusion.3.own_ref
  85.5 3.3 %collective-permute-start.11 = (bf16[256,384]{1,0:T(8,128)(2,1)S(1)}, bf16[256,384]{1,0:T(8,128)(2,1)S(1)}, u32[]{:S(2)}, u32[]{:S(2)}) collective-permute-start(bf16[256,384]{1,0:T(8,128)(2,1)S(1)} %slice.187), channel_id=1, source_target_pairs={{0,4},{4,12},{12,8},{8,0},{1,5},{5,13},{13,9},{9,1},{2,6},{6,14},{... | collective-permute-start | bytes 589832 | tf_op jit(solution)/shard_map/ppermute | solution.py:384
  90.6 3.3 %collective-permute-done.11 = bf16[256,384]{1,0:T(8,128)(2,1)S(1)} collective-permute-done((bf16[256,384]{1,0:T(8,128)(2,1)S(1)}, bf16[256,384]{1,0:T(8,128)(2,1)S(1)}, u32[]{:S(2)}, u32[]{:S(2)}) %collective-permute-start.11) | collective-permute-done | bytes 196640 | tf_op jit(solution)/shard_map/ppermute | solution.py:384
  93.9 25.1 %collective-permute-done.10 = bf16[896,384]{1,0:T(8,128)(2,1)S(1)} collective-permute-done((bf16[896,384]{1,0:T(8,128)(2,1)S(1)}, bf16[896,384]{1,0:T(8,128)(2,1)S(1)}, u32[]{:S(2)}, u32[]{:S(2)}) %collective-permute-start.10) | collective-permute-done | bytes 688160 | tf_op jit(solution)/shard_map/ppermute | solution.py:383
  120.4 7.2 %shard_map.149 = (bf16[2,256,512]{2,1,0:T(8,128)(2,1)S(1)}, bf16[32,512]{1,0:T(8,128)(2,1)S(1)}) custom-call(s32[12]{0:T(128)S(1)} %copy-done.10, f32[512,384]{1,0:T(8,128)S(1)} %fusion.3.own_ref, f32[512,384]{1,0:T(8,128)S(1)} %fusion.1.oth_ref, f32[1,512]{1,0:T(1,128)S(1)} %bitcast.75, f32[1,1024]{1,0:T(1,128)S(1)} %bitcast.74, ...), custom_call_target="tpu_custom_call" | custom-call | flops 536870912 | bytes 8388608 | tf_op jit(solution)/shard_map/pallas_call | solution.py:272
  127.8 2.0 %collective-permute-start.25 = (bf16[32,512]{1,0:T(8,128)(2,1)S(1)}, bf16[32,512]{1,0:T(8,128)(2,1)S(1)}, u32[]{:S(2)}, u32[]{:S(2)}) collective-permute-start(bf16[32,512]{1,0:T(8,128)(2,1)S(1)} %get-tuple-element.19), channel_id=1, source_target_pairs={{12,0},{8,4},{4,8},{0,12},{13,1},{9,5},{5,9},{1,13},{14,2},{10,6},... | collective-permute-start | bytes 98312 | tf_op jit(solution)/shard_map/ppermute | solution.py:439
  130.7 1.3 fusion.84
  133.4 1.3 fusion.7
  138.4 2.2 %fusion.100 = f32[256,896]{1,0:T(8,128)} fusion(bf16[256,896]{1,0:T(8,128)(2,1)} %collective-permute-done.4, bf16[256,512]{1,0:T(8,128)(2,1)S(1)} %get-tuple-element.30), kind=kOutput, calls=%fused_computation.150 | convolution fusion | flops 117440512 | bytes 1507328 | tf_op jit(solution)/shard_map/dot_general | solution.py:415
  141.9 1.2 fusion.98
  146.8 2.7 %collective-permute-start.28 = (bf16[32,896]{1,0:T(8,128)(2,1)S(1)}, bf16[32,896]{1,0:T(8,128)(2,1)S(1)}, u32[]{:S(2)}, u32[]{:S(2)}) collective-permute-start(bf16[32,896]{1,0:T(8,128)(2,1)S(1)} %fusion.68), channel_id=1, source_target_pairs={{0,2},{1,3},{2,0},{3,1},{4,6},{5,7},{6,4},{7,5},{8,10},{9,11},{10,... | collective-permute-start | bytes 172040 | tf_op jit(solution)/shard_map/ppermute | solution.py:444
  149.8 2.1 %collective-permute-done.28 = bf16[32,896]{1,0:T(8,128)(2,1)S(1)} collective-permute-done((bf16[32,896]{1,0:T(8,128)(2,1)S(1)}, bf16[32,896]{1,0:T(8,128)(2,1)S(1)}, u32[]{:S(2)}, u32[]{:S(2)}) %collective-permute-start.28) | collective-permute-done | bytes 57376 | tf_op jit(solution)/shard_map/ppermute | solution.py:444
  152.5 2.1 %convolution_convert_fusion = bf16[32,1024]{1,0:T(8,128)(2,1)} fusion(bf16[896,1024]{1,0:T(8,128)(2,1)S(1)} %copy-done, bf16[32,896]{1,0:T(8,128)(2,1)} %copy-done.34, bf16[32,896]{1,0:T(8,128)(2,1)} %copy-done.31, bf16[32,896]{1,0:T(8,128)(2,1)} %copy-done.29, f32[32,896]{1,0:T(8,128)S(1)} %copy-done.4, f32[32]{0:T(128)S(1)} %copy-done.42, pred[]{:T(512)S(6)} %eq.93, ...), kind=kOutput, calls=%fused_computation.45 | convolution fusion | flops 60875776 | bytes 2187521 | tf_op jit(solution)/shard_map/dot_general | solution.py:415
  154.7 1.5 pad_maximum_fusion.7
  156.2 5.7 %all-to-all-start = ((bf16[16,8,384]{2,1,0:T(8,128)(2,1)}), bf16[16,8,384]{2,1,0:T(8,128)(2,1)}, u32[]{:S(2)}, u32[]{:S(2)}) async-start(bf16[16,8,384]{2,1,0:T(8,128)(2,1)} %bitcast.19), calls=%async_computation | async-start | bytes 196608 | tf_op jit(solution)/shard_map/all_to_all | solution.py:459
  163.0 1.3 slice_add_fusion.1
  164.6 1.9 %collective-permute-start.14 = (bf16[256,384]{1,0:T(8,128)(2,1)S(1)}, bf16[256,384]{1,0:T(8,128)(2,1)S(1)}, u32[]{:S(2)}, u32[]{:S(2)}) collective-permute-start(bf16[256,384]{1,0:T(8,128)(2,1)S(1)} %get-tuple-element.43), channel_id=1, source_target_pairs={{0,2},{1,3},{2,0},{3,1},{4,6},{5,7},{6,4},{7,5},{8,10},{9,11},{10,... | collective-permute-start | bytes 589832 | tf_op jit(solution)/shard_map/ppermute | solution.py:477
  166.6 1.1 convert_element_type.193
  168.5 1.3 convert_element_type.202
  169.9 1.4 fusion.6
  171.7 1.9 collective-permute-start.22
  173.6 4.6 %collective-permute-done.19 = bf16[256,512]{1,0:T(8,128)(2,1)S(1)} collective-permute-done((bf16[256,512]{1,0:T(8,128)(2,1)S(1)}, bf16[256,512]{1,0:T(8,128)(2,1)S(1)}, u32[]{:S(2)}, u32[]{:S(2)}) %collective-permute-start.19) | collective-permute-done | bytes 262176 | tf_op jit(solution)/shard_map/ppermute | solution.py:477
  178.4 9.2 %collective-permute-done.22 = bf16[256,896]{1,0:T(8,128)(2,1)S(1)} collective-permute-done((bf16[256,896]{1,0:T(8,128)(2,1)S(1)}, bf16[256,896]{1,0:T(8,128)(2,1)S(1)}, u32[]{:S(2)}, u32[]{:S(2)}) %collective-permute-start.22) | collective-permute-done | bytes 458784 | tf_op jit(solution)/shard_map/ppermute | solution.py:477
  187.6 1.3 select_convert_fusion
  191.1 1.3 convert_select_fusion.1
  192.4 1.1 fusion
  (192 shorter events, 30.7 us)
Async XLA Ops:
  0.6 151.9 %copy-start = (bf16[896,1024]{1,0:T(8,128)(2,1)S(1)}, bf16[896,1024]{1,0:T(8,128)(2,1)}, u32[]{:S(2)}) copy-start(bf16[896,1024]{1,0:T(8,128)(2,1)} %param.23) | copy-start | bytes 5505028
  0.6 13.0 %copy-start.43 = (s32[1,32]{1,0:T(1,128)S(1)}, s32[1,32]{1,0:T(1,128)}, u32[]{:S(2)}) copy-start(s32[1,32]{1,0:T(1,128)} %param.14) | copy-start | bytes 388
  2.7 17.2 %collective-permute-start = (bf16[896,128]{1,0:T(8,128)(2,1)}, bf16[896,128]{1,0:T(8,128)(2,1)}, u32[]{:S(2)}, u32[]{:S(2)}) collective-permute-start(bf16[896,128]{1,0:T(8,128)(2,1)} %get-tuple-element.32), channel_id=1, source_target_pairs={{0,1},{1,3},{18,17},{19,19},{4,5},{5,7},{22,21},{23,23},{8,9},{9,1... | collective-permute-start | bytes 688136 | tf_op jit(solution)/shard_map/ppermute | solution.py:361
  5.7 14.2 %collective-permute-start.1 = (bf16[896,128]{1,0:T(8,128)(2,1)}, bf16[896,128]{1,0:T(8,128)(2,1)}, u32[]{:S(2)}, u32[]{:S(2)}) collective-permute-start(bf16[896,128]{1,0:T(8,128)(2,1)} %get-tuple-element.31), channel_id=1, source_target_pairs={{0,0},{1,2},{18,16},{19,18},{4,4},{5,6},{22,20},{23,22},{8,8},{9,1... | collective-permute-start | bytes 688136 | tf_op jit(solution)/shard_map/ppermute | solution.py:361
  9.2 6.9 %copy-start.45 = (s32[1,32]{1,0:T(1,128)S(1)}, s32[1,32]{1,0:T(1,128)}, u32[]{:S(2)}) copy-start(s32[1,32]{1,0:T(1,128)} %param.15) | copy-start | bytes 388
  11.3 12.2 %copy-start.13 = (bf16[256,896]{1,0:T(8,128)(2,1)}, bf16[256,896]{1,0:T(8,128)(2,1)S(1)}, u32[]{:S(2)}) copy-start(bf16[256,896]{1,0:T(8,128)(2,1)S(1)} %get-tuple-element.17) | copy-start | bytes 1376260
  11.3 15.0 %collective-permute-start.4 = (bf16[256,896]{1,0:T(8,128)(2,1)S(1)}, bf16[256,896]{1,0:T(8,128)(2,1)}, u32[]{:S(2)}, u32[]{:S(2)}) collective-permute-start(bf16[256,896]{1,0:T(8,128)(2,1)S(1)} %get-tuple-element.17), channel_id=1, source_target_pairs={{0,4},{4,12},{12,8},{8,0},{1,5},{5,13},{13,9},{9,1},{2,6},{6,14},{... | collective-permute-start | bytes 1376264 | tf_op jit(solution)/shard_map/ppermute | solution.py:374
  14.0 16.9 %copy-start.5 = (s32[512]{0:T(512)}, s32[512]{0:T(512)S(1)}, u32[]{:S(2)}) copy-start(s32[512]{0:T(512)S(1)} %convert_reduce_fusion) | copy-start | bytes 6148
  16.0 10.0 %copy-start.15 = (bf16[896,256]{1,0:T(8,128)(2,1)}, bf16[896,256]{1,0:T(8,128)(2,1)S(1)}, u32[]{:S(2)}) copy-start(bf16[896,256]{1,0:T(8,128)(2,1)S(1)} %get-tuple-element.28) | copy-start | bytes 1376260
  16.3 10.0 %copy-start.37 = (s32[32]{0:T(128)}, s32[32]{0:T(128)S(1)}, u32[]{:S(2)}) copy-start(s32[32]{0:T(128)S(1)} %select_reduce_fusion.1) | copy-start | bytes 388
  18.7 12.2 %copy-start.35 = (f32[3584]{0:T(1024)S(1)}, f32[3584]{0:T(1024)}, u32[]{:S(2)}) copy-start(f32[3584]{0:T(1024)} %param.17) | copy-start | bytes 43012
  19.9 11.2 %copy-start.39 = (bf16[1024]{0:T(1024)(128)(2,1)S(1)}, bf16[1024]{0:T(1024)(128)(2,1)}, u32[]{:S(2)}) copy-start(bf16[1024]{0:T(1024)(128)(2,1)} %param.21) | copy-start | bytes 6148
  19.9 11.8 %copy-start.40 = (bf16[512]{0:T(512)(128)(2,1)S(1)}, bf16[512]{0:T(512)(128)(2,1)}, u32[]{:S(2)}) copy-start(bf16[512]{0:T(512)(128)(2,1)} %param.19) | copy-start | bytes 3076
  23.4 31.5 %collective-permute-start.2 = (bf16[896,384]{1,0:T(8,128)(2,1)}, bf16[896,384]{1,0:T(8,128)(2,1)}, u32[]{:S(2)}, u32[]{:S(2)}) collective-permute-start(bf16[896,384]{1,0:T(8,128)(2,1)} %pad_maximum_fusion.2), channel_id=1, source_target_pairs={{0,4},{4,12},{12,8},{8,0},{1,5},{5,13},{13,9},{9,1},{2,6},{6,14},{... | collective-permute-start | bytes 2064392 | tf_op jit(solution)/shard_map/ppermute | solution.py:375
  26.3 28.6 %collective-permute-start.5 = (bf16[256,896]{1,0:T(8,128)(2,1)}, bf16[256,896]{1,0:T(8,128)(2,1)}, u32[]{:S(2)}, u32[]{:S(2)}) collective-permute-start(bf16[256,896]{1,0:T(8,128)(2,1)} %collective-permute-done.4), channel_id=1, source_target_pairs={{0,16},{16,0},{1,17},{17,1},{2,18},{18,2},{3,19},{19,3},{4,20},{20... | collective-permute-start | bytes 1376264 | tf_op jit(solution)/shard_map/ppermute | solution.py:378
  26.5 32.1 %collective-permute-start.3 = (bf16[896,384]{1,0:T(8,128)(2,1)}, bf16[896,384]{1,0:T(8,128)(2,1)}, u32[]{:S(2)}, u32[]{:S(2)}) collective-permute-start(bf16[896,384]{1,0:T(8,128)(2,1)} %pad_maximum_fusion.2), channel_id=1, source_target_pairs={{4,0},{12,4},{8,12},{0,8},{5,1},{13,5},{9,13},{1,9},{6,2},{14,6},{... | collective-permute-start | bytes 2064392 | tf_op jit(solution)/shard_map/ppermute | solution.py:376
  28.2 26.7 %collective-permute-start.7 = (bf16[896,128]{1,0:T(8,128)(2,1)}, bf16[896,128]{1,0:T(8,128)(2,1)}, u32[]{:S(2)}, u32[]{:S(2)}) collective-permute-start(bf16[896,128]{1,0:T(8,128)(2,1)} %broadcast_select_fusion.4), channel_id=1, source_target_pairs={{0,16},{16,0},{1,17},{17,1},{2,18},{18,2},{3,19},{19,3},{4,20},{20... | collective-permute-start | bytes 688136 | tf_op jit(solution)/shard_map/ppermute | solution.py:377
  38.2 16.7 %copy-start.30 = (bf16[896,256]{1,0:T(8,128)(2,1)S(1)}, bf16[896,256]{1,0:T(8,128)(2,1)}, u32[]{:S(2)}) copy-start(bf16[896,256]{1,0:T(8,128)(2,1)} %get-tuple-element.27) | copy-start | bytes 1376260
  41.1 17.4 %copy-start.3 = (f32[32,896]{1,0:T(8,128)}, f32[32,896]{1,0:T(8,128)S(1)}, u32[]{:S(2)}) copy-start(f32[32,896]{1,0:T(8,128)S(1)} %get-tuple-element.20) | copy-start | bytes 344068
  54.9 26.3 %collective-permute-start.6 = (bf16[896,384]{1,0:T(8,128)(2,1)}, bf16[896,384]{1,0:T(8,128)(2,1)S(1)}, u32[]{:S(2)}, u32[]{:S(2)}) collective-permute-start(bf16[896,384]{1,0:T(8,128)(2,1)} %collective-permute-done.2), channel_id=1, source_target_pairs={{0,4},{4,12},{12,8},{8,0},{1,5},{5,13},{13,9},{9,1},{2,6},{6,14},{... | collective-permute-start | bytes 2064392 | tf_op jit(solution)/shard_map/ppermute | solution.py:380
  58.5 22.0 %collective-permute-start.15 = (bf16[256,896]{1,0:T(8,128)(2,1)S(1)}, bf16[256,896]{1,0:T(8,128)(2,1)S(1)}, u32[]{:S(2)}, u32[]{:S(2)}) collective-permute-start(bf16[256,896]{1,0:T(8,128)(2,1)S(1)} %copy-done.14), channel_id=1, source_target_pairs={{4,0},{12,4},{8,12},{0,8},{5,1},{13,5},{9,13},{1,9},{6,2},{14,6},{... | collective-permute-start | bytes 1376264 | tf_op jit(solution)/shard_map/ppermute | solution.py:382
  61.5 24.0 %collective-permute-start.8 = (bf16[896,384]{1,0:T(8,128)(2,1)}, bf16[896,384]{1,0:T(8,128)(2,1)S(1)}, u32[]{:S(2)}, u32[]{:S(2)}) collective-permute-start(bf16[896,384]{1,0:T(8,128)(2,1)} %collective-permute-done.2), channel_id=1, source_target_pairs={{0,16},{16,0},{1,17},{17,1},{2,18},{18,2},{3,19},{19,3},{4,20},{20... | collective-permute-start | bytes 2064392 | tf_op jit(solution)/shard_map/ppermute | solution.py:379
  61.5 58.2 %collective-permute-start.9 = (bf16[896,384]{1,0:T(8,128)(2,1)}, bf16[896,384]{1,0:T(8,128)(2,1)S(1)}, u32[]{:S(2)}, u32[]{:S(2)}) collective-permute-start(bf16[896,384]{1,0:T(8,128)(2,1)} %collective-permute-done.3), channel_id=1, source_target_pairs={{0,16},{16,0},{1,17},{17,1},{2,18},{18,2},{3,19},{19,3},{4,20},{20... | collective-permute-start | bytes 2064392 | tf_op jit(solution)/shard_map/ppermute | solution.py:381
  67.1 16.8 %copy-start.16 = (bf16[896,256]{1,0:T(8,128)(2,1)S(1)}, bf16[896,256]{1,0:T(8,128)(2,1)}, u32[]{:S(2)}) copy-start(bf16[896,256]{1,0:T(8,128)(2,1)} %copy-done.15) | copy-start | bytes 1376260
  80.5 10.1 %collective-permute-start.16 = (bf16[256,512]{1,0:T(8,128)(2,1)S(1)}, bf16[256,512]{1,0:T(8,128)(2,1)S(1)}, u32[]{:S(2)}, u32[]{:S(2)}) collective-permute-start(bf16[256,512]{1,0:T(8,128)(2,1)S(1)} %slice.192), channel_id=1, source_target_pairs={{0,4},{4,12},{12,8},{8,0},{1,5},{5,13},{13,9},{9,1},{2,6},{6,14},{... | collective-permute-start | bytes 786440 | tf_op jit(solution)/shard_map/ppermute | solution.py:386
  81.2 53.6 %collective-permute-start.20 = (bf16[256,896]{1,0:T(8,128)(2,1)S(1)}, bf16[256,896]{1,0:T(8,128)(2,1)S(1)}, u32[]{:S(2)}, u32[]{:S(2)}) collective-permute-start(bf16[256,896]{1,0:T(8,128)(2,1)S(1)} %collective-permute-done.15), channel_id=1, source_target_pairs={{0,16},{16,0},{1,17},{17,1},{2,18},{18,2},{3,19},{19,3},{4,20},{20... | collective-permute-start | bytes 1376264 | tf_op jit(solution)/shard_map/ppermute | solution.py:385
  81.2 37.8 %collective-permute-start.10 = (bf16[896,384]{1,0:T(8,128)(2,1)S(1)}, bf16[896,384]{1,0:T(8,128)(2,1)S(1)}, u32[]{:S(2)}, u32[]{:S(2)}) collective-permute-start(bf16[896,384]{1,0:T(8,128)(2,1)S(1)} %collective-permute-done.6), channel_id=1, source_target_pairs={{0,16},{16,0},{1,17},{17,1},{2,18},{18,2},{3,19},{19,3},{4,20},{20... | collective-permute-start | bytes 2064392 | tf_op jit(solution)/shard_map/ppermute | solution.py:383
  85.5 8.3 %collective-permute-start.11 = (bf16[256,384]{1,0:T(8,128)(2,1)S(1)}, bf16[256,384]{1,0:T(8,128)(2,1)S(1)}, u32[]{:S(2)}, u32[]{:S(2)}) collective-permute-start(bf16[256,384]{1,0:T(8,128)(2,1)S(1)} %slice.187), channel_id=1, source_target_pairs={{0,4},{4,12},{12,8},{8,0},{1,5},{5,13},{13,9},{9,1},{2,6},{6,14},{... | collective-permute-start | bytes 589832 | tf_op jit(solution)/shard_map/ppermute | solution.py:384
  90.6 52.6 %collective-permute-start.17 = (bf16[256,512]{1,0:T(8,128)(2,1)S(1)}, bf16[256,512]{1,0:T(8,128)(2,1)S(1)}, u32[]{:S(2)}, u32[]{:S(2)}) collective-permute-start(bf16[256,512]{1,0:T(8,128)(2,1)S(1)} %collective-permute-done.16), channel_id=1, source_target_pairs={{0,16},{16,0},{1,17},{17,1},{2,18},{18,2},{3,19},{19,3},{4,20},{20... | collective-permute-start | bytes 786440 | tf_op jit(solution)/shard_map/ppermute | solution.py:388
  93.9 43.4 %collective-permute-start.12 = (bf16[256,384]{1,0:T(8,128)(2,1)S(1)}, bf16[256,384]{1,0:T(8,128)(2,1)S(1)}, u32[]{:S(2)}, u32[]{:S(2)}) collective-permute-start(bf16[256,384]{1,0:T(8,128)(2,1)S(1)} %collective-permute-done.11), channel_id=1, source_target_pairs={{0,16},{16,0},{1,17},{17,1},{2,18},{18,2},{3,19},{19,3},{4,20},{20... | collective-permute-start | bytes 589832 | tf_op jit(solution)/shard_map/ppermute | solution.py:387
  127.6 17.2 %collective-permute-start.24 = (bf16[32,512]{1,0:T(8,128)(2,1)S(1)}, bf16[32,512]{1,0:T(8,128)(2,1)S(1)}, u32[]{:S(2)}, u32[]{:S(2)}) collective-permute-start(bf16[32,512]{1,0:T(8,128)(2,1)S(1)} %get-tuple-element.19), channel_id=1, source_target_pairs={{8,0},{0,4},{12,8},{4,12},{9,1},{1,5},{13,9},{5,13},{10,2},{2,6},{... | collective-permute-start | bytes 98312 | tf_op jit(solution)/shard_map/ppermute | solution.py:439
  127.8 17.0 %collective-permute-start.25 = (bf16[32,512]{1,0:T(8,128)(2,1)S(1)}, bf16[32,512]{1,0:T(8,128)(2,1)S(1)}, u32[]{:S(2)}, u32[]{:S(2)}) collective-permute-start(bf16[32,512]{1,0:T(8,128)(2,1)S(1)} %get-tuple-element.19), channel_id=1, source_target_pairs={{12,0},{8,4},{4,8},{0,12},{13,1},{9,5},{5,9},{1,13},{14,2},{10,6},... | collective-permute-start | bytes 98312 | tf_op jit(solution)/shard_map/ppermute | solution.py:439
  134.7 10.1 %collective-permute-start.26 = (bf16[32,512]{1,0:T(8,128)(2,1)S(1)}, bf16[32,512]{1,0:T(8,128)(2,1)S(1)}, u32[]{:S(2)}, u32[]{:S(2)}) collective-permute-start(bf16[32,512]{1,0:T(8,128)(2,1)S(1)} %get-tuple-element.19), channel_id=1, source_target_pairs={{4,0},{12,4},{0,8},{8,12},{5,1},{13,5},{1,9},{9,13},{6,2},{14,6},{... | collective-permute-start | bytes 98312 | tf_op jit(solution)/shard_map/ppermute | solution.py:439
  137.3 31.2 %collective-permute-start.21 = (bf16[256,1792]{1,0:T(8,128)(2,1)}, bf16[256,1792]{1,0:T(8,128)(2,1)}, u32[]{:S(2)}, u32[]{:S(2)}) collective-permute-start(bf16[256,1792]{1,0:T(8,128)(2,1)} %pad_maximum_fusion.1), channel_id=1, source_target_pairs={{0,1},{1,0},{2,3},{3,2},{4,5},{5,4},{6,7},{7,6},{8,9},{9,8},{10,11... | collective-permute-start | bytes 2752520 | tf_op jit(solution)/shard_map/ppermute | solution.py:471
  143.2 18.7 %collective-permute-start.13 = (bf16[256,768]{1,0:T(8,128)(2,1)}, bf16[256,768]{1,0:T(8,128)(2,1)}, u32[]{:S(2)}, u32[]{:S(2)}) collective-permute-start(bf16[256,768]{1,0:T(8,128)(2,1)} %pad_maximum_fusion.4), channel_id=1, source_target_pairs={{0,1},{1,0},{2,3},{3,2},{4,5},{5,4},{6,7},{7,6},{8,9},{9,8},{10,11... | collective-permute-start | bytes 1179656 | tf_op jit(solution)/shard_map/ppermute | solution.py:471
  143.9 8.6 %copy-start.4 = (f32[32,896]{1,0:T(8,128)S(1)}, f32[32,896]{1,0:T(8,128)}, u32[]{:S(2)}) copy-start(f32[32,896]{1,0:T(8,128)} %copy-done.3) | copy-start | bytes 344068
  143.9 8.6 %copy-start.38 = (s32[32]{0:T(128)S(1)}, s32[32]{0:T(128)}, u32[]{:S(2)}) copy-start(s32[32]{0:T(128)} %copy-done.37) | copy-start | bytes 388
  143.9 8.6 %copy-start.42 = (f32[32]{0:T(128)S(1)}, f32[32]{0:T(128)}, u32[]{:S(2)}) copy-start(f32[32]{0:T(128)} %fusion.115) | copy-start | bytes 388
  144.8 21.8 %collective-permute-start.18 = (bf16[256,1024]{1,0:T(8,128)(2,1)}, bf16[256,1024]{1,0:T(8,128)(2,1)}, u32[]{:S(2)}, u32[]{:S(2)}) collective-permute-start(bf16[256,1024]{1,0:T(8,128)(2,1)} %pad_maximum_fusion.3), channel_id=1, source_target_pairs={{0,1},{1,0},{2,3},{3,2},{4,5},{5,4},{6,7},{7,6},{8,9},{9,8},{10,11... | collective-permute-start | bytes 1572872 | tf_op jit(solution)/shard_map/ppermute | solution.py:471
  145.2 9.4 %copy-start.41 = (bf16[4,8]{1,0:T(4,128)(2,1)S(1)}, bf16[4,8]{1,0:T(4,128)(2,1)}, u32[]{:S(2)}) copy-start(bf16[4,8]{1,0:T(4,128)(2,1)} %broadcast_in_dim.79) | copy-start | bytes 196
  145.3 1.6 collective-permute-start.27
  146.8 5.0 %collective-permute-start.28 = (bf16[32,896]{1,0:T(8,128)(2,1)S(1)}, bf16[32,896]{1,0:T(8,128)(2,1)S(1)}, u32[]{:S(2)}, u32[]{:S(2)}) collective-permute-start(bf16[32,896]{1,0:T(8,128)(2,1)S(1)} %fusion.68), channel_id=1, source_target_pairs={{0,2},{1,3},{2,0},{3,1},{4,6},{5,7},{6,4},{7,5},{8,10},{9,11},{10,... | collective-permute-start | bytes 172040 | tf_op jit(solution)/shard_map/ppermute | solution.py:444
  156.2 32.6 %all-to-all-start = ((bf16[16,8,384]{2,1,0:T(8,128)(2,1)}), bf16[16,8,384]{2,1,0:T(8,128)(2,1)}, u32[]{:S(2)}, u32[]{:S(2)}) async-start(bf16[16,8,384]{2,1,0:T(8,128)(2,1)} %bitcast.19), calls=%async_computation | async-start | bytes 196608 | tf_op jit(solution)/shard_map/all_to_all | solution.py:459
  164.6 8.9 %collective-permute-start.14 = (bf16[256,384]{1,0:T(8,128)(2,1)S(1)}, bf16[256,384]{1,0:T(8,128)(2,1)S(1)}, u32[]{:S(2)}, u32[]{:S(2)}) collective-permute-start(bf16[256,384]{1,0:T(8,128)(2,1)S(1)} %get-tuple-element.43), channel_id=1, source_target_pairs={{0,2},{1,3},{2,0},{3,1},{4,6},{5,7},{6,4},{7,5},{8,10},{9,11},{10,... | collective-permute-start | bytes 589832 | tf_op jit(solution)/shard_map/ppermute | solution.py:477
  168.3 10.0 %collective-permute-start.19 = (bf16[256,512]{1,0:T(8,128)(2,1)S(1)}, bf16[256,512]{1,0:T(8,128)(2,1)S(1)}, u32[]{:S(2)}, u32[]{:S(2)}) collective-permute-start(bf16[256,512]{1,0:T(8,128)(2,1)S(1)} %get-tuple-element.41), channel_id=1, source_target_pairs={{0,2},{1,3},{2,0},{3,1},{4,6},{5,7},{6,4},{7,5},{8,10},{9,11},{10,... | collective-permute-start | bytes 786440 | tf_op jit(solution)/shard_map/ppermute | solution.py:477
  171.7 15.9 %collective-permute-start.22 = (bf16[256,896]{1,0:T(8,128)(2,1)S(1)}, bf16[256,896]{1,0:T(8,128)(2,1)S(1)}, u32[]{:S(2)}, u32[]{:S(2)}) collective-permute-start(bf16[256,896]{1,0:T(8,128)(2,1)S(1)} %get-tuple-element.45), channel_id=1, source_target_pairs={{0,2},{1,3},{2,0},{3,1},{4,6},{5,7},{6,4},{7,5},{8,10},{9,11},{10,... | collective-permute-start | bytes 1376264 | tf_op jit(solution)/shard_map/ppermute | solution.py:477
  173.6 15.2 %copy-start.19 = (f32[256,384]{1,0:T(8,128)}, f32[256,384]{1,0:T(8,128)S(1)}, u32[]{:S(2)}) copy-start(f32[256,384]{1,0:T(8,128)S(1)} %convert_add_fusion.2) | copy-start | bytes 1179652
  188.8 2.3 %collective-permute-start.23 = (bf16[256,896]{1,0:T(8,128)(2,1)}, bf16[256,896]{1,0:T(8,128)(2,1)}, u32[]{:S(2)}, u32[]{:S(2)}) collective-permute-start(bf16[256,896]{1,0:T(8,128)(2,1)} %get-tuple-element.21), channel_id=1, source_target_pairs={{0,1},{1,0},{2,3},{3,2},{4,5},{5,4},{6,7},{7,6},{8,9},{9,8},{10,11... | collective-permute-start | bytes 1376264 | tf_op jit(solution)/shard_map/ppermute | solution.py:485
  (28 other events, 75.9 us)

commit v3 on v0

--- a/solution.py
+++ b/solution.py
@@ -1,6 +1,11 @@
+import functools
+
 import jax
 import jax.numpy as jnp
+import numpy as np
 from jax import lax
+from jax.experimental import pallas as pl
+from jax.experimental.pallas import tpu as pltpu
 from jax.sharding import PartitionSpec as P
 
 KV_HEADS = 4
@@ -9,6 +14,8 @@
 
 
 rope_base = 1000000.0
+bf16 = jnp.bfloat16
+f32 = jnp.float32
 
 
 def rotate(values, places):
@@ -36,7 +43,7 @@
     return (segment, member, place)
 
 
-def shards(
+def wide_slice_shards(
     hidden,
     lengths,
     list_ids,
@@ -68,16 +75,22 @@
         lax.all_gather(w_query, "dp", axis=0, tiled=True),
         preferred_element_type=jnp.float32,
     )
+    own_cols = jnp.concatenate(
+        [
+            lax.dynamic_slice_in_dim(full_cols, head_group * HD, HD, 1),
+            lax.dynamic_slice_in_dim(full_cols, kv_width + head_group * HD, HD, 1),
+        ],
+        axis=1,
+    )
     keyval_sum = jnp.dot(
         normed,
-        lax.all_gather(full_cols, "dp", axis=0, tiled=True),
+        lax.all_gather(own_cols, "dp", axis=0, tiled=True),
         preferred_element_type=jnp.float32,
     )
-    keyval_sum = keyval_sum + b_keyval.astype(jnp.float32)
-    keys_all = rotate(keyval_sum[:, :kv_width], place).astype(jnp.bfloat16)
-    values_all = keyval_sum[:, kv_width:].astype(jnp.bfloat16)
-    keys = lax.dynamic_slice_in_dim(keys_all, head_group * HD, HD, 1)
-    values = lax.dynamic_slice_in_dim(values_all, head_group * HD, HD, 1)
+    key_bias = lax.dynamic_slice_in_dim(b_keyval, head_group * HD, HD, 0)
+    value_bias = lax.dynamic_slice_in_dim(b_keyval, kv_width + head_group * HD, HD, 0)
+    keys = rotate(keyval_sum[:, :HD] + key_bias.astype(jnp.float32), place).astype(jnp.bfloat16)
+    values = (keyval_sum[:, HD:] + value_bias.astype(jnp.float32)).astype(jnp.bfloat16)
     query = rotate(query_sum + b_query.astype(jnp.float32), place).astype(jnp.bfloat16)
     grouped = query.reshape(token_count, query_cols // HD, HD)
     scores = jnp.einsum("sgd,td->gst", grouped, keys, preferred_element_type=jnp.float32) * HD ** (
@@ -141,9 +154,559 @@
     return (layer_out, residual_sums, list_counts)
 
 
+VMEM = pl.BlockSpec(memory_space=pltpu.VMEM)
+SMEM = pl.BlockSpec(memory_space=pltpu.SMEM)
+T, GROUP, KEEP_0, KEEP_1, MINE_A, KEY_FROM, VALUE_FROM = range(4, 11)
+
+
+def dot(a, b):
+    return jnp.dot(a, b, preferred_element_type=f32)
+
+
+def turn(x, cosine, sine):
+    return x * cosine + pltpu.roll(x, HD // 2, 1) * sine
+
+
+def lanes(start, size):
+    return pl.ds(pl.multiple_of(start, 128), size)
+
+
+def call(kernel, outs, flops, scalars, *args):
+    moved = sum(a.size * a.dtype.itemsize for a in (*args, *outs))
+    return pl.pallas_call(
+        kernel,
+        in_specs=[SMEM] + [VMEM] * len(args),
+        out_specs=[VMEM] * len(outs),
+        out_shape=outs,
+        compiler_params=pltpu.CompilerParams(vmem_limit_bytes=60 * 1024 * 1024),
+        cost_estimate=pl.CostEstimate(flops=flops, bytes_accessed=moved, transcendentals=0),
+    )(scalars, *args)
+
+
+def places_kernel(
+    freq, lengths, ids, slots, cos_ref, sin_ref, seg_col, seg_row, member_ref, inverse_ref, hits_ref, counts_ref
+):
+    i32 = jnp.int32
+    tokens = cos_ref.shape[0]
+    captions = lengths.shape[1]
+    lists = slots.shape[1]
+    row = lengths[...]
+    square = (captions, captions)
+    down = lax.broadcasted_iota(i32, square, 0)
+    along = lax.broadcasted_iota(i32, square, 1)
+    wide_row = jnp.broadcast_to(row, square)
+    col = jnp.sum(jnp.where(down == along, wide_row, 0), axis=1, keepdims=True)
+    end_col = jnp.sum(jnp.where(along <= down, wide_row, 0), axis=1, keepdims=True)
+    start_col = end_col - col
+    end_row = jnp.sum(jnp.where(down <= along, jnp.broadcast_to(col, square), 0), axis=0, keepdims=True)
+    start_row = end_row - row
+    inverse_ref[...] = 1.0 / col.astype(f32)
+    index = lax.broadcasted_iota(i32, (captions, tokens), 1)
+    member_ref[...] = jnp.where((index >= start_col) & (index < end_col), 1.0, 0.0).astype(bf16)
+    seg_row[...] = jnp.sum(jnp.where(index >= end_col, 1, 0), axis=0, keepdims=True)
+    index = lax.broadcasted_iota(i32, (tokens, captions), 0)
+    seg_col[...] = jnp.sum(jnp.where(index >= end_row, 1, 0), axis=1, keepdims=True)
+    inside = (index >= start_row) & (index < end_row)
+    place = jnp.sum(jnp.where(inside, index - start_row, 0), axis=1, keepdims=True)
+    angle = place.astype(f32) * freq[...]
+    cos_ref[...] = jnp.cos(angle)
+    sine = jnp.sin(angle)
+    lane = lax.broadcasted_iota(i32, (tokens, HD), 1)
+    sin_ref[...] = jnp.where(lane < HD // 2, -sine, sine)
+    square = (lists, lists)
+    down = lax.broadcasted_iota(i32, square, 0)
+    along = lax.broadcasted_iota(i32, square, 1)
+    slot_col = jnp.sum(
+        jnp.where(down == along, jnp.broadcast_to(slots[...], square), 0), axis=1, keepdims=True
+    )
+    down = lax.broadcasted_iota(i32, (lists, captions), 0)
+    slot_row = jnp.sum(jnp.where(ids[...] == down, slot_col, 0), axis=0, keepdims=True)
+    hits = jnp.where(down == slot_row, 1.0, 0.0)
+    hits_ref[...] = hits.astype(bf16)
+    counts_ref[...] = jnp.sum(hits, axis=1, keepdims=True)
+
+
+def places(lengths, list_ids, list_slot, tokens):
+    captions, lists = lengths.shape[1], list_slot.shape[0]
+    freq = rope_base ** (-(2.0 / HD) * (np.arange(HD) % (HD // 2)))
+    shape = jax.ShapeDtypeStruct
+    return pl.pallas_call(
+        places_kernel,
+        in_specs=[VMEM] * 4,
+        out_specs=[VMEM] * 8,
+        out_shape=[
+            shape((tokens, HD), f32),
+            shape((tokens, HD), f32),
+            shape((tokens, 1), jnp.int32),
+            shape((1, tokens), jnp.int32),
+            shape((captions, tokens), bf16),
+            shape((captions, 1), f32),
+            shape((lists, captions), bf16),
+            shape((lists, 1), f32),
+        ],
+        compiler_params=pltpu.CompilerParams(vmem_limit_bytes=60 * 1024 * 1024),
+        cost_estimate=pl.CostEstimate(
+            flops=64 * tokens * HD, bytes_accessed=tokens * HD * 8, transcendentals=2 * tokens * HD
+        ),
+    )(jnp.asarray(freq, f32)[None, :], lengths, list_ids, list_slot[None, :])
+
+
+def prep_kernel(sc, hidden_ref, gain_ref, member_ref, *outs):
+    *block_refs, own_ref, pooled_ref = outs
+    wide = hidden_ref[...].astype(f32)
+    scale = lax.rsqrt(jnp.mean(wide * wide, axis=1, keepdims=True) + 1e-06)
+    share = own_ref.shape[1]
+    for m, ref in enumerate(block_refs):
+        at = lanes(sc[m] * share, share)
+        ref[...] = (hidden_ref[:, at].astype(f32) * scale * gain_ref[:, at]).astype(bf16)
+    own = hidden_ref[:, lanes(sc[T] * share, share)]
+    own_ref[...] = own
+
+    @pl.when(pl.program_id(0) == 0)
+    def _():
+        pooled_ref[...] = jnp.zeros_like(pooled_ref)
+
+    pooled_ref[...] += dot(member_ref[...], own)
+
+
+def prepare(scalars, hidden, gain, member, n):
+    tokens, width = hidden.shape
+    share = width // n
+    captions = member.shape[0]
+    rows = 128
+    stripe = pl.BlockSpec((rows, share), lambda i, s: (i, 0))
+    return pl.pallas_call(
+        prep_kernel,
+        grid_spec=pltpu.PrefetchScalarGridSpec(
+            num_scalar_prefetch=1,
+            grid=(tokens // rows,),
+            in_specs=[
+                pl.BlockSpec((rows, width), lambda i, s: (i, 0)),
+                pl.BlockSpec((1, width), lambda i, s: (0, 0)),
+                pl.BlockSpec((captions, rows), lambda i, s: (0, i)),
+            ],
+            out_specs=[stripe] * (n + 1) + [pl.BlockSpec((captions, share), lambda i, s: (0, 0))],
+        ),
+        out_shape=[jax.ShapeDtypeStruct((tokens, share), bf16)] * (n + 1)
+        + [jax.ShapeDtypeStruct((captions, share), f32)],
+        compiler_params=pltpu.CompilerParams(vmem_limit_bytes=60 * 1024 * 1024),
+        cost_estimate=pl.CostEstimate(
+            flops=8 * tokens * width, bytes_accessed=4 * tokens * width, transcendentals=0
+        ),
+    )(scalars, hidden, gain[None, :], member)
+
+
+def keyval_kernel(sc, b0, b1, b2, b3, w, r1, r2, r3, y1, y2, y3, bias, cos_ref, sin_ref, out_ref):
+    g, t = sc[GROUP], sc[T]
+    base = dot(b0[...], w[...])
+    own = dot(b1[...], r1[...]) + dot(b2[...], r2[...]) + dot(b3[...], r3[...])
+    oth = dot(b1[...], y1[...]) + dot(b2[...], y2[...]) + dot(b3[...], y3[...])
+    heads = w.shape[1] // HD
+    keyed = t * heads < KV_HEADS
+    for h in range(heads):
+        at = slice(h * HD, (h + 1) * HD)
+        x = base[:, at] + jnp.where(g == h, own, oth)
+        x = x + bias[:, lanes((t * heads + h) * HD, HD)].astype(f32)
+        out_ref[:, at] = jnp.where(keyed, turn(x, cos_ref[...], sin_ref[...]), x).astype(bf16)
+
+
+def query_kernel(sc, b0, b1, b2, b3, w, r1, r2, r3, y1, y3, own_ref, oth_ref):
+    g = sc[GROUP]
+    half = own_ref.shape[1]
+    own = dot(b0[...], w[:, lanes(g * half, half)]) + dot(b1[...], r1[...])
+    own_ref[...] = own + dot(b2[...], r2[...]) + dot(b3[...], r3[...])
+    oth = dot(b0[...], w[:, lanes((1 - g) * half, half)]) + dot(b1[...], y1[...])
+    oth_ref[...] = oth + dot(b3[...], y3[...])
+
+
+def attention_kernel(
+    sc,
+    own_ref,
+    oth_ref,
+    b2,
+    y2,
+    bq_ref,
+    x0,
+    x1,
+    x2,
+    cos_ref,
+    sin_ref,
+    seg_col,
+    seg_row,
+    member_ref,
+    inverse_ref,
+    hits_ref,
+    out_ref,
+    lists_ref,
+    query_ref,
+):
+    t, g = sc[T], sc[GROUP]
+    tokens, wide = own_ref.shape
+    heads = wide // HD
+    here = lanes((t % (x0.shape[1] // HD)) * HD, HD)
+
+    def pick(origin):
+        return jnp.where(
+            origin == 0, x0[:, here], jnp.where(origin == 1, x1[:, here], x2[:, here])
+        )
+
+    keys, values = pick(sc[KEY_FROM]), pick(sc[VALUE_FROM])
+    query_ref[...] = oth_ref[...] + dot(b2[...], y2[...])
+    rows = 128
+    pooled = jnp.zeros((member_ref.shape[0], 2 * wide), f32)
+    for i in range(tokens // rows):
+        at = pl.ds(i * rows, rows)
+        lo_key, hi_key = max(0, (i - 1) * rows), min(tokens, (i + 2) * rows)
+        cosine, sine = cos_ref[at, :], sin_ref[at, :]
+        allowed = seg_col[at, :] == seg_row[:, lo_key:hi_key]
+        out = []
+        for part, ref in enumerate((own_ref, query_ref)):
+            for h in range(heads):
+                lo = h * HD
+                bias = bq_ref[:, lanes(jnp.bitwise_xor(g, part) * wide + lo, HD)].astype(f32)
+                query = turn(ref[at, lo : lo + HD] + bias, cosine, sine).astype(bf16)
+                scores = lax.dot_general(
+                    query,
+                    keys[lo_key:hi_key],
+                    (((1,), (1,)), ((), ())),
+                    preferred_element_type=f32,
+                ) * HD ** (-0.5)
+                scores = jnp.where(allowed, scores, -1e30)
+                top = jnp.max(scores, axis=1, keepdims=True)
+                weights = jnp.exp(scores - top)
+                probs = (weights / jnp.sum(weights, axis=1, keepdims=True)).astype(bf16)
+                out.append(dot(probs, values[lo_key:hi_key]).astype(bf16))
+        out = jnp.concatenate(out, axis=1)
+        out_ref[at, :] = out
+        pooled = pooled + dot(member_ref[:, at], out)
+    pooled = (pooled * inverse_ref[...]).astype(bf16)
+    lists_ref[...] = dot(hits_ref[...], pooled).astype(bf16)
+
+
+def attend(scalars, own, *rest):
+    tokens, wide = own.shape
+    lists = rest[-1].shape[0]
+    outs = [
+        jax.ShapeDtypeStruct((tokens, 2 * wide), bf16),
+        jax.ShapeDtypeStruct((lists, 2 * wide), bf16),
+    ]
+    return pl.pallas_call(
+        attention_kernel,
+        in_specs=[SMEM] + [VMEM] * (1 + len(rest)),
+        out_specs=[VMEM] * 2,
+        out_shape=outs,
+        scratch_shapes=[pltpu.VMEM((tokens, wide), f32)],
+        compiler_params=pltpu.CompilerParams(vmem_limit_bytes=60 * 1024 * 1024),
+        cost_estimate=pl.CostEstimate(
+            flops=8 * tokens * tokens * wide,
+            bytes_accessed=8 * 1024 * 1024,
+            transcendentals=tokens * tokens * 2 * wide // HD,
+        ),
+    )(scalars, own, *rest)
+
+
+def project(attn, weights, ref):
+    half = attn.shape[1] // 2
+    first, second = weights()
+    ref[...] = (dot(attn[:, :half], first) + dot(attn[:, half:], second)).astype(bf16)
+
+
+def project_two(keep, attn, first, second, sent, kept):
+    @pl.when(keep == 1)
+    def _():
+        project(attn, first, kept)
+        project(attn, second, sent)
+
+    @pl.when(keep == 0)
+    def _():
+        project(attn, second, kept)
+        project(attn, first, sent)
+
+
+def project_own_kernel(sc, attn, w, own_b, oth_b, sent, kept):
+    half = attn.shape[1] // 2
+    g = sc[GROUP]
+
+    def stored():
+        return (
+            w[pl.ds(pl.multiple_of(g * half, half), half), :],
+            w[pl.ds(pl.multiple_of((1 - g) * half, half), half), :],
+        )
+
+    project_two(sc[KEEP_0], attn, stored, lambda: (own_b[...], oth_b[...]), sent, kept)
+
+
+def project_kernel(lo, hi, sc, attn, own_a, oth_a, own_b, oth_b, sent, kept):
+    project_two(
+        sc[KEEP_1],
+        attn,
+        lambda: (own_a[:, lo:hi], oth_a[:, lo:hi]),
+        lambda: (own_b[...], oth_b[...]),
+        sent,
+        kept,
+    )
+
+
+def add_kernel(sc, kept, came, total):
+    total[...] = (kept[...].astype(f32) + came[...].astype(f32)).astype(bf16)
+
+
+def finish_kernel(sc, own, ta, ca, tb0, cb0, tb1, cb1, out):
+    cut = tb0.shape[1]
+    mine = sc[MINE_A] == 1
+    for lo, hi, t, c in ((0, cut, tb0, cb0), (cut, own.shape[1], tb1, cb1)):
+        a = ta[:, lo:hi].astype(f32) + ca[:, lo:hi].astype(f32)
+        b = t[...].astype(f32) + c[...].astype(f32)
+        out[:, lo:hi] = (own[:, lo:hi].astype(f32) + jnp.where(mine, a, b)).astype(bf16)
+
+
+def folded_ring(n):
+    return [0] + list(range(1, n, 2)) + list(range(2 * ((n - 1) // 2), 0, -2))
+
+
+def after(value, *earlier):
+    return lax.optimization_barrier((value, *earlier))[0]
+
+
+def shards(
+    hidden,
+    lengths,
+    list_ids,
+    list_slot,
+    gain,
+    w_query,
+    b_query,
+    w_keyval,
+    b_keyval,
+    w_out,
+    w_pool,
+    centroids,
+):
+    tokens, width = hidden.shape
+    captions = lengths.shape[1]
+    n_dp, n_tp = lax.axis_size("dp"), lax.axis_size("tp")
+    share = width // n_dp
+    ring = folded_ring(n_dp)
+    place_in = {v: i for i, v in enumerate(ring)}
+    source_of = [[ring[(place_in[d] - m) % n_dp] for m in range(n_dp)] for d in range(n_dp)]
+    forward = [(ring[i], ring[(i + 1) % n_dp]) for i in range(n_dp)]
+    backward = [(b, a) for a, b in forward]
+    swap = [(0, 1), (1, 0)]
+    core = [(i, i ^ 1) for i in range(n_tp)]
+    across = [(i, i ^ 2) for i in range(n_tp)]
+    per_dev = w_keyval.shape[1] // HD
+    rounds = [[], []]
+    origin = []
+    for tt in range(n_tp):
+        for source in (tt // per_dev, (KV_HEADS + tt) // per_dev):
+            if source == tt:
+                origin.append(0)
+                continue
+            for k, pairs in enumerate(rounds):
+                if all(a != source and b != tt for a, b in pairs):
+                    pairs.append((source, tt))
+                    origin.append(k + 1)
+                    break
+    table = []
+    for gg in range(2):
+        for d in range(n_dp):
+            for tt in range(n_tp):
+                stays = [int(source_of[d][m] % 2 == tt % 2) for m in range(2)]
+                mine = int(tt in (source_of[d][0], source_of[d][2]))
+                table.append(
+                    [*source_of[d], tt, gg, *stays, mine, *origin[2 * tt : 2 * tt + 2]]
+                )
+    scalars = lax.dynamic_slice_in_dim(
+        jnp.array(table, jnp.int32),
+        lax.axis_index(("groups", "dp", "tp")),
+        1,
+        0,
+        allow_negative_indices=False,
+    )[0]
+    g, t, z = lax.axis_index("groups"), lax.axis_index("tp"), lax.axis_index("dp")
+
+    def own_half(w, axis):
+        size = w.shape[axis] // 2
+        return lax.dynamic_slice_in_dim(w, g * size, size, axis, allow_negative_indices=False)
+
+    cosine, sine, seg_col, seg_row, member, inverse, hits, local_counts = places(
+        lengths, list_ids, list_slot, tokens
+    )
+
+    kv_own = own_half(w_keyval, 1)
+    q_own = own_half(w_query, 1)
+    o_own = own_half(w_out, 0)
+    cut = share // 256 * 128 + 128
+
+    own = {"k": kv_own, "q": q_own, "o": o_own, "a": o_own[:, :cut], "b": o_own[:, cut:]}
+    stages = [["k1", "k3"], ["q1", "k2"], ["q3"], ["q2"], ["o1"], ["o2"], ["a3", "b3"]]
+    lag = 3
+    ring_of, swapped = {}, {}
+
+    def run_stage(i, *ties):
+        ties = list(ties)
+        if i >= 1:
+            ties += [ring_of[key] for key in stages[i - 1]]
+        if lag <= i < len(stages) - 1:
+            ties += [swapped[key] for key in stages[i - lag]]
+        for key in stages[i]:
+            piece = ring_of[key[0] + "1"] if key[1] == "2" else own[key[0]]
+            pairs = backward if key[1] == "3" else forward
+            ring_of[key] = lax.ppermute(after(piece, *ties) if ties else piece, "dp", pairs)
+        for key in stages[i]:
+            swapped[key] = lax.ppermute(ring_of[key], "groups", swap)
+
+    run_stage(0)
+    run_stage(1, cosine)
+    *blocks, own_input, pooled_hidden = prepare(
+        scalars, after(hidden, swapped["k1"], swapped["k3"]), gain, member, n_dp
+    )
+    run_stage(2, blocks[0])
+    run_stage(3)
+    run_stage(4)
+    hidden_lists = dot(hits, (pooled_hidden * inverse).astype(bf16))
+
+    shape = jax.ShapeDtypeStruct
+    work = 2 * tokens * width
+    (kv_mine,) = call(
+        keyval_kernel,
+        [shape((tokens, w_keyval.shape[1]), bf16)],
+        work * w_keyval.shape[1],
+        scalars,
+        *blocks,
+        w_keyval,
+        *[r["k%d" % m] for r in (ring_of, swapped) for m in range(1, n_dp)],
+        b_keyval[None, :],
+        cosine,
+        sine,
+    )
+    kv_came = [lax.ppermute(kv_mine, "tp", pairs) for pairs in rounds]
+    run_stage(5, *kv_came)
+    q_half = w_query.shape[1] // 2
+    sum_own, sum_oth = call(
+        query_kernel,
+        [shape((tokens, q_half), f32)] * 2,
+        work * q_half * 2,
+        scalars,
+        *blocks,
+        w_query,
+        *[ring_of[key] for key in ("q1", "q2", "q3")],
+        *[swapped[key] for key in ("q1", "q3")],
+    )
+    run_stage(6, sum_own)
+    attn, attn_lists = attend(
+        scalars,
+        after(sum_own, ring_of["o1"]),
+        sum_oth,
+        blocks[2],
+        swapped["q2"],
+        b_query[None, :],
+        kv_mine,
+        *kv_came,
+        cosine,
+        sine,
+        seg_col,
+        seg_row,
+        member,
+        inverse,
+        hits,
+    )
+
+    def project_pair(kernel, n, attn, *weights):
+        sent, kept = call(
+            kernel,
+            [shape((tokens, n), bf16)] * 2,
+            4 * tokens * q_half * 2 * n,
+            scalars,
+            attn,
+            *weights,
+        )
+        return sent, kept, lax.ppermute(sent, "tp", core)
+
+    def exchange(kept, came, m):
+        (total,) = call(
+            add_kernel, [shape(kept.shape, bf16)], kept.size, scalars, kept, came
+        )
+        pairs = []
+        for d in range(n_dp):
+            for block in (source_of[d][m], source_of[d][m + 2]):
+                pairs.append((d * n_tp + (block ^ 2), d * n_tp + block))
+        return total, lax.ppermute(total, ("dp", "tp"), pairs)
+
+    def both(key):
+        return ring_of[key], swapped[key]
+
+    sent_a, kept_a, came_a = project_pair(
+        project_own_kernel, share, attn, w_out, *both("o2")
+    )
+    block_a = exchange(kept_a, after(came_a, swapped["a3"]), 0)
+
+    attn_lists = after(attn_lists, ring_of["b3"])
+    lists_sum = attn_lists.astype(f32)
+    for m in range(1, n_dp):
+        pairs = [(source_of[d][m], d) for d in range(n_dp)]
+        lists_sum = lists_sum + lax.ppermute(attn_lists, "dp", pairs).astype(f32)
+    lists_sum = after(lists_sum.astype(bf16), sent_a)
+    first = jnp.where(g == 0, lists_sum[:, :q_half], lists_sum[:, q_half:])
+    second = jnp.where(g == 0, lists_sum[:, q_half:], lists_sum[:, :q_half])
+    plane = dot(jnp.concatenate([first, second], axis=1), w_out).astype(bf16)
+    plane = plane.astype(f32) + lax.ppermute(plane, "tp", core).astype(f32)
+    plane16 = after(plane.astype(bf16), block_a[0])
+    crossed = lax.ppermute(plane16, "tp", across)
+    rows = after(attn, block_a[0], plane16)
+    sent_b0, kept_b0, came_b0 = project_pair(
+        functools.partial(project_kernel, 0, cut), cut, rows, *both("o1"), *both("a3")
+    )
+    plane = after(plane, sent_b0)
+    plane = plane + crossed.astype(f32)
+    plane = (jnp.where(t == z, plane, 0.0) + hidden_lists).astype(bf16)
+    vec_lists = dot(plane, w_pool).astype(bf16)
+    lists_own, cols = centroids.shape
+    late = vec_lists.reshape(n_dp, lists_own, n_tp, cols).transpose(0, 2, 1, 3)
+    late = jnp.concatenate(
+        [
+            late,
+            jnp.broadcast_to(
+                local_counts.astype(bf16).reshape(n_dp, 1, lists_own, 1),
+                (n_dp, n_tp, lists_own, HD),
+            ),
+        ],
+        axis=3,
+    ).reshape(n_dp * n_tp, lists_own, cols + HD)
+    late = lax.all_to_all(late, ("dp", "tp"), split_axis=0, concat_axis=0, tiled=True)
+    late = late.reshape(n_dp, n_tp, lists_own, cols + HD).astype(f32)
+    totals = jnp.sum(late[..., :cols], axis=(0, 1))
+    counts = jnp.sum(late[:, 0, :, cols], axis=0)
+    residual_sums = totals - counts[:, None] * centroids
+    list_counts = counts.astype(jnp.int32)
+    block_b0 = exchange(kept_b0, after(came_b0, swapped["b3"]), 1)
+    rows = after(rows, block_b0[0], vec_lists)
+    _, kept_b1, came_b1 = project_pair(
+        functools.partial(project_kernel, cut, share),
+        share - cut,
+        rows,
+        *both("o1"),
+        *both("b3"),
+    )
+    block_b1 = exchange(kept_b1, came_b1, 1)
+    (layer_out,) = call(
+        finish_kernel,
+        [shape((tokens, share), bf16)],
+        tokens * share,
+        scalars,
+        own_input,
+        *block_a,
+        *block_b0,
+        *block_b1,
+    )
+    return (layer_out, residual_sums, list_counts)
+
+
 def solution(mesh):
+    sizes = mesh.shape
+    square = sizes["groups"] == 2 and sizes["dp"] == 4 and sizes["tp"] == 4
     return jax.shard_map(
-        shards,
+        shards if square else wide_slice_shards,
         mesh=mesh,
         in_specs=(
             P(("groups", "dp"), None),

time: 410 us -> 179 us (0.44)
  waiting for transfers between devices: 317 us -> 57.8 us
  Pallas kernels: 0 us -> 50.7 us
  starting transfers between devices: 4.84 us -> 53.5 us
  matrix products: 26.5 us -> 1.75 us
  other arithmetic: 19.7 us -> 2.27 us
  between operations: 14.4 us -> 0.9 us
  blocking collectives: 9.94 us -> 0 us
  local copies, waits for them, and re-layouts: 17.3 us -> 10.9 us
    all_gather x4 -> x0, waiting for transfers between devices: 267 us -> none  [the longest x1 125 us: shards(): lax.all_gather(full_cols, 'dp', axis=0, tiled=True)]
    ppermute x0 -> x33, waiting for transfers between devices: none -> 57.8 us  [the longest x10 25.9 us: run_stage(): lax.ppermute(after(piece, *ties) if ties else piece, 'dp', pairs)]
    pallas_call x0 -> x12, Pallas kernels: none -> 50.7 us  [the longest x9 32.6 us: call(): pl.pallas_call(kernel, in_specs=[SMEM] + [VMEM] * len(args), out_specs=[V...]
    ppermute x0 -> x33, starting transfers between devices: none -> 46.7 us  [the longest x10 17 us: run_stage(): lax.ppermute(after(piece, *ties) if ties else piece, 'dp', pairs)]
    unnamed x7 -> x0, waiting for transfers between devices: 35 us -> none
    dot_general x8 -> x2, matrix products: 26.5 us -> 1.75 us  [dot(): return jnp.dot(a, b, preferred_element_type=f32)]
    all_to_all x1 -> x0, blocking collectives: 9.94 us -> none  [shards(): lax.all_to_all(send_rows, 'dp', split_axis=0, concat_axis=0, tiled=True)]
    reduce_scatter x1 -> x0, waiting for transfers between devices: 9.36 us -> none  [shards(): lax.psum_scatter(pooled_part.astype(jnp.bfloat16), 'tp', scatter_dimensio...]
  transfers between devices with their start and end apart: 7 -> 34, of which waited for: 7 -> 15; matrix products, arithmetic and copies ran while one was open for 10% -> 5% of each run, Pallas kernels for 0% -> 25%
where the time goes in v3:
time: 179 us; the launch traced here: 178 us
  waiting for transfers between devices  57.8 us (32%)
  starting transfers between devices  53.5 us (30%)
  Pallas kernels  50.7 us (28%)
  local copies, waits for them, and re-layouts  10.9 us (6%)
  other arithmetic  2.27 us (1%)
    pallas_call x9, Pallas kernels, call(): pl.pallas_call(kernel, in_specs=[SMEM] + [VMEM] * len(args), out_specs=[V...  32.6 us
    ppermute x10, waiting for transfers between devices, run_stage(): lax.ppermute(after(piece, *ties) if ties else piece, 'dp', pairs)  25.9 us
    ppermute x10, waiting for transfers between devices, run_stage(): swapped[key] = lax.ppermute(ring_of[key], 'groups', swap)  17.8 us
    ppermute x10, starting transfers between devices, run_stage(): lax.ppermute(after(piece, *ties) if ties else piece, 'dp', pairs)  17 us
    ppermute x10, starting transfers between devices, run_stage(): swapped[key] = lax.ppermute(ring_of[key], 'groups', swap)  12.5 us
    pallas_call x1, Pallas kernels, attend(): pl.pallas_call(attention_kernel, in_specs=[SMEM] + [VMEM] * (1 + len(rest...  8.57 us
    ppermute x3, starting transfers between devices, exchange(): return (total, lax.ppermute(total, ('dp', 'tp'), pairs))  7.69 us
    all_to_all x1, starting transfers between devices, shards(): lax.all_to_all(late, ('dp', 'tp'), split_axis=0, concat_axis=0, tiled=True)  6.83 us
  transfers between devices with their start and end apart: 34, of which 15 were waited for; matrix products, arithmetic and copies ran while one was open for 5% of the time, Pallas kernels for 25%

profile of v3, /device:TPU:0, one launch (start us, length us, event | category | flops | bytes accessed | tf_op | source)
XLA Modules:
  0.0 177.9 jit_solution(17613495751018716440)
XLA Ops:
  1.7 3.1 %collective-permute-start = (bf16[896,128]{1,0:T(8,128)(2,1)S(1)}, bf16[896,128]{1,0:T(8,128)(2,1)S(1)}, u32[]{:S(2)}, u32[]{:S(2)}) collective-permute-start(bf16[896,128]{1,0:T(8,128)(2,1)S(1)} %constant_dynamic-slice_fusion.3), channel_id=1, source_target_pairs={{0,4},{4,12},{12,8},{8,0},{1,5},{5,13},{13,9},{9,1},{2,6},{6,14},{... | collective-permute-start | bytes 688136 | tf_op jit(solution)/shard_map/ppermute | solution.py:555
  5.9 2.9 %shard_map.157 = (f32[512,128]{1,0:T(8,128)}, f32[512,128]{1,0:T(8,128)}, s32[512,1]{1,0:T(8,128)}, s32[1,512]{1,0:T(1,128)}, bf16[32,512]{1,0:T(8,128)(2,1)}, /...) custom-call(f32[1,128]{1,0:T(1,128)} %constant.33.freq, s32[1,32]{1,0:T(1,128)} %lengths.1, s32[1,32]{1,0:T(1,128)} %ids.1, ...), custom_call_target="tpu_custom_call" | custom-call | flops 4194304 | bytes 524288 | tf_op jit(solution)/shard_map/pallas_call | solution.py:233
  9.9 1.6 collective-permute-done.r1
  11.5 4.8 %collective-permute-done.2.r3 = bf16[896,128]{1,0:T(8,128)(2,1)S(1)} collective-permute-done((bf16[896,128]{1,0:T(8,128)(2,1)S(1)}, bf16[896,128]{1,0:T(8,128)(2,1)S(1)}, u32[]{:S(2)}, u32[]{:S(2)}) %collective-permute-start.2) | collective-permute-done | bytes 229408 | tf_op jit(solution)/shard_map/ppermute | solution.py:555
  16.4 1.7 collective-permute-start.4
  18.1 1.5 collective-permute-start.1
  20.1 2.6 %collective-permute-start.5 = (bf16[896,128]{1,0:T(8,128)(2,1)S(1)}, bf16[896,128]{1,0:T(8,128)(2,1)}, u32[]{:S(2)}, u32[]{:S(2)}) collective-permute-start(bf16[896,128]{1,0:T(8,128)(2,1)S(1)} %collective-permute-done.r1), channel_id=1, source_target_pairs={{0,4},{4,12},{12,8},{8,0},{1,5},{5,13},{13,9},{9,1},{2,6},{6,14},{... | collective-permute-start | bytes 688136 | tf_op jit(solution)/shard_map/ppermute | solution.py:555
  22.7 1.3 broadcast_in_dim.27.gain_ref
  25.2 1.4 collective-permute-done.1.y1
  26.6 2.6 %collective-permute-done.3.y3 = bf16[896,128]{1,0:T(8,128)(2,1)S(1)} collective-permute-done((bf16[896,128]{1,0:T(8,128)(2,1)S(1)}, bf16[896,128]{1,0:T(8,128)(2,1)S(1)}, u32[]{:S(2)}, u32[]{:S(2)}) %collective-permute-start.3) | collective-permute-done | bytes 229408 | tf_op jit(solution)/shard_map/ppermute | solution.py:557
  29.9 6.5 %shard_map.158 = (bf16[512,896]{1,0:T(8,128)(2,1)}, bf16[512,896]{1,0:T(8,128)(2,1)}, bf16[512,896]{1,0:T(8,128)(2,1)}, bf16[512,896]{1,0:T(8,128)(2,1)}, bf16[512,896]{1,0:T(8,128)(2,1)}, /*index=5*/f32[32,896]{1,0:T(8,128)}) custom-call(s32[11]{0:T(128)} %fusion.8.sc, bf16[512,3584]{1,0:T(8,128)(2,1)} %hidden_ref, f32[1,3584]{1,0:T(1,128)} %broadcast_in_dim.27.gain_ref, ...), custom_call_target="tpu_custom_call" | custom-call | flops 14680064 | bytes 7340032 | tf_op jit(solution)/shard_map/pallas_call | solution.py:278
  36.5 2.3 %collective-permute-start.6 = (bf16[896,256]{1,0:T(8,128)(2,1)S(1)}, bf16[896,256]{1,0:T(8,128)(2,1)}, u32[]{:S(2)}, u32[]{:S(2)}) collective-permute-start(bf16[896,256]{1,0:T(8,128)(2,1)S(1)} %constant_dynamic-slice_fusion.2), channel_id=1, source_target_pairs={{4,0},{12,4},{8,12},{0,8},{5,1},{13,5},{9,13},{1,9},{6,2},{14,6},{... | collective-permute-start | bytes 1376264 | tf_op jit(solution)/shard_map/ppermute | solution.py:555
  38.8 1.6 collective-permute-start.8
  40.3 8.6 %collective-permute-done.6.r3 = bf16[896,256]{1,0:T(8,128)(2,1)} collective-permute-done((bf16[896,256]{1,0:T(8,128)(2,1)S(1)}, bf16[896,256]{1,0:T(8,128)(2,1)}, u32[]{:S(2)}, u32[]{:S(2)}) %collective-permute-start.6) | collective-permute-done | bytes 458784 | tf_op jit(solution)/shard_map/ppermute | solution.py:555
  48.9 1.6 collective-permute-start.10
  51.1 6.6 %collective-permute-done.10.y2 = bf16[896,128]{1,0:T(8,128)(2,1)S(1)} collective-permute-done((bf16[896,128]{1,0:T(8,128)(2,1)}, bf16[896,128]{1,0:T(8,128)(2,1)S(1)}, u32[]{:S(2)}, u32[]{:S(2)}) %collective-permute-start.10) | collective-permute-done | bytes 229408 | tf_op jit(solution)/shard_map/ppermute | solution.py:557
  57.7 2.7 %collective-permute-done.7.r2 = bf16[896,256]{1,0:T(8,128)(2,1)S(1)} collective-permute-done((bf16[896,256]{1,0:T(8,128)(2,1)}, bf16[896,256]{1,0:T(8,128)(2,1)S(1)}, u32[]{:S(2)}, u32[]{:S(2)}) %collective-permute-start.7) | collective-permute-done | bytes 458784 | tf_op jit(solution)/shard_map/ppermute | solution.py:555
  61.2 5.4 %shard_map.160.x0 = bf16[512,256]{1,0:T(8,128)(2,1)} custom-call(s32[11]{0:T(128)} %fusion.8.sc, bf16[512,896]{1,0:T(8,128)(2,1)} %get-tuple-element.48.b0, bf16[512,896]{1,0:T(8,128)(2,1)} %get-tuple-element.49.b1, bf16[512,896]{1,0:T(8,128)(2,1)} %get-tuple-element.50.b2, bf16[512,896]{1,0:T(8,128)(2,1)} %get-tuple-element.51.b3, bf16[896,256]{1,0:T(8,128)(2,1)} %w.4, ...), custom_call_target="tpu_custom_call" | custom-call | flops 939524096 | bytes 6293504 | tf_op jit(solution)/shard_map/pallas_call | solution.py:176
  66.6 1.9 %collective-permute-start.13 = (bf16[512,256]{1,0:T(8,128)(2,1)}, bf16[512,256]{1,0:T(8,128)(2,1)S(1)}, u32[]{:S(2)}, u32[]{:S(2)}) collective-permute-start(bf16[512,256]{1,0:T(8,128)(2,1)} %shard_map.160.x0), channel_id=1, source_target_pairs={{2,0},{0,1},{1,2},{6,4},{4,5},{5,6},{10,8},{8,9},{9,10},{14,12},{1... | collective-permute-start | bytes 786440 | tf_op jit(solution)/shard_map/ppermute | solution.py:583
  69.2 5.9 %collective-permute-done.13.x1 = bf16[512,256]{1,0:T(8,128)(2,1)S(1)} collective-permute-done((bf16[512,256]{1,0:T(8,128)(2,1)}, bf16[512,256]{1,0:T(8,128)(2,1)S(1)}, u32[]{:S(2)}, u32[]{:S(2)}) %collective-permute-start.13) | collective-permute-done | bytes 262176 | tf_op jit(solution)/shard_map/ppermute | solution.py:583
  75.8 2.7 %collective-permute-start.15 = (bf16[256,896]{1,0:T(8,128)(2,1)}, bf16[256,896]{1,0:T(8,128)(2,1)}, u32[]{:S(2)}, u32[]{:S(2)}) collective-permute-start(bf16[256,896]{1,0:T(8,128)(2,1)} %collective-permute-done.11.own_a), channel_id=1, source_target_pairs={{0,4},{4,12},{12,8},{8,0},{1,5},{5,13},{13,9},{9,1},{2,6},{6,14},{... | collective-permute-start | bytes 1376264 | tf_op jit(solution)/shard_map/ppermute | solution.py:555
  78.5 1.6 collective-permute-start.12
  80.1 8.1 %collective-permute-done.15.own_b = bf16[256,896]{1,0:T(8,128)(2,1)} collective-permute-done((bf16[256,896]{1,0:T(8,128)(2,1)}, bf16[256,896]{1,0:T(8,128)(2,1)}, u32[]{:S(2)}, u32[]{:S(2)}) %collective-permute-start.15) | collective-permute-done | bytes 458784 | tf_op jit(solution)/shard_map/ppermute | solution.py:555
  88.2 1.6 collective-permute-start.16
  90.5 6.0 %shard_map.159 = (f32[512,256]{1,0:T(8,128)}, f32[512,256]{1,0:T(8,128)}) custom-call(s32[11]{0:T(128)} %fusion.8.sc, bf16[512,896]{1,0:T(8,128)(2,1)} %get-tuple-element.48.b0, bf16[512,896]{1,0:T(8,128)(2,1)} %get-tuple-element.49.b1, bf16[512,896]{1,0:T(8,128)(2,1)} %get-tuple-element.50.b2, bf16[512,896]{1,0:T(8,128)(2,1)} %get-tuple-element.51.b3, ...), custom_call_target="tpu_custom_call" | custom-call | flops 1879048192 | bytes 7929856 | tf_op jit(solution)/shard_map/pallas_call | solution.py:176
  96.5 2.0 %collective-permute-start.21 = (bf16[256,384]{1,0:T(8,128)(2,1)}, bf16[256,384]{1,0:T(8,128)(2,1)}, u32[]{:S(2)}, u32[]{:S(2)}) collective-permute-start(bf16[256,384]{1,0:T(8,128)(2,1)} %dynamic-slice.1), channel_id=1, source_target_pairs={{4,0},{12,4},{8,12},{0,8},{5,1},{13,5},{9,13},{1,9},{6,2},{14,6},{... | collective-permute-start | bytes 589832 | tf_op jit(solution)/shard_map/ppermute | solution.py:555
  100.4 8.6 %shard_map.161 = (bf16[512,512]{1,0:T(8,128)(2,1)}, bf16[32,512]{1,0:T(8,128)(2,1)}) custom-call(s32[11]{0:T(128)} %fusion.8.sc, f32[512,256]{1,0:T(8,128)} %get-tuple-element.59.own_ref, f32[512,256]{1,0:T(8,128)} %get-tuple-element.60.oth_ref, bf16[512,896]{1,0:T(8,128)(2,1)} %get-tuple-element.50.b2, bf16[896,256]{1,0:T(8,128)(2,1)} %copy-done.7, ...), custom_call_target="tpu_custom_call" | custom-call | flops 536870912 | bytes 8388608 | tf_op jit(solution)/shard_map/pallas_call | solution.py:393
  109.0 1.5 collective-permute-start.18
  110.5 1.4 collective-permute-start.24
  111.9 1.5 collective-permute-start.23
  113.4 4.4 %shard_map.162 = (bf16[512,896]{1,0:T(8,128)(2,1)}, bf16[512,896]{1,0:T(8,128)(2,1)}) custom-call(s32[11]{0:T(128)} %fusion.8.sc, bf16[512,512]{1,0:T(8,128)(2,1)} %get-tuple-element.83.attn, bf16[512,896]{1,0:T(8,128)(2,1)} %w.5, bf16[256,896]{1,0:T(8,128)(2,1)} %collective-permute-done.15.own_b, bf16[256,896]{1,0:T(8,128)(2,1)} %collective-permute-done.16.oth_b), custom_call_target="tpu_custom_call" | custom-call | flops 939524096 | bytes 4194304 | tf_op jit(solution)/shard_map/pallas_call | solution.py:176
  119.7 1.6 collective-permute-done.22
  121.8 1.6 collective-permute-start.19
  123.5 7.2 %collective-permute-done.19.oth_b = bf16[256,512]{1,0:T(8,128)(2,1)S(1)} collective-permute-done((bf16[256,512]{1,0:T(8,128)(2,1)}, bf16[256,512]{1,0:T(8,128)(2,1)S(1)}, u32[]{:S(2)}, u32[]{:S(2)}) %collective-permute-start.19) | collective-permute-done | bytes 262176 | tf_op jit(solution)/shard_map/ppermute | solution.py:557
  131.7 2.6 %shard_map.163.ta = bf16[512,896]{1,0:T(8,128)(2,1)} custom-call(s32[11]{0:T(128)} %fusion.8.sc, bf16[512,896]{1,0:T(8,128)(2,1)} %get-tuple-element.68.kept, bf16[512,896]{1,0:T(8,128)(2,1)} %copy-done.5), custom_call_target="tpu_custom_call" | custom-call | flops 458752 | bytes 2752512 | tf_op jit(solution)/shard_map/pallas_call | solution.py:176
  134.3 3.2 %shard_map.164 = (bf16[512,512]{1,0:T(8,128)(2,1)}, bf16[512,512]{1,0:T(8,128)(2,1)}) custom-call(s32[11]{0:T(128)} %fusion.8.sc, bf16[512,512]{1,0:T(8,128)(2,1)} %get-tuple-element.83.attn, bf16[256,896]{1,0:T(8,128)(2,1)} %collective-permute-done.11.own_a, bf16[256,896]{1,0:T(8,128)(2,1)} %collective-permute-done.26.oth_a, ...), custom_call_target="tpu_custom_call" | custom-call | flops 536870912 | bytes 3014656 | tf_op jit(solution)/shard_map/pallas_call | solution.py:176
  137.7 3.2 %collective-permute-start.30 = (bf16[32,896]{1,0:T(8,128)(2,1)S(1)}, bf16[32,896]{1,0:T(8,128)(2,1)S(1)}, u32[]{:S(2)}, u32[]{:S(2)}) collective-permute-start(bf16[32,896]{1,0:T(8,128)(2,1)S(1)} %get-tuple-element.76), channel_id=1, source_target_pairs={{0,2},{1,3},{2,0},{3,1},{4,6},{5,7},{6,4},{7,5},{8,10},{9,11},{10,... | collective-permute-start | bytes 172040 | tf_op jit(solution)/shard_map/ppermute | solution.py:655
  141.1 1.5 collective-permute-start.28
  142.7 1.3 collective-permute-start.20
  144.0 1.5 convolution_convert_fusion
  146.2 6.8 %all-to-all-start = ((bf16[16,8,384]{2,1,0:T(8,128)(2,1)}), bf16[16,8,384]{2,1,0:T(8,128)(2,1)S(1)}, u32[]{:S(2)}, u32[]{:S(2)}) async-start(bf16[16,8,384]{2,1,0:T(8,128)(2,1)} %bitcast.4), calls=%async_computation | async-start | bytes 196608 | tf_op jit(solution)/shard_map/all_to_all | solution.py:676
  153.9 2.1 %shard_map.165.tb0 = bf16[512,512]{1,0:T(8,128)(2,1)} custom-call(s32[11]{0:T(128)} %fusion.8.sc, bf16[512,512]{1,0:T(8,128)(2,1)} %get-tuple-element.78.kept, bf16[512,512]{1,0:T(8,128)(2,1)} %copy-done.6), custom_call_target="tpu_custom_call" | custom-call | flops 262144 | bytes 1572864 | tf_op jit(solution)/shard_map/pallas_call | solution.py:176
  156.0 3.1 %shard_map.166 = (bf16[512,384]{1,0:T(8,128)(2,1)}, bf16[512,384]{1,0:T(8,128)(2,1)}) custom-call(s32[11]{0:T(128)} %fusion.8.sc, bf16[512,512]{1,0:T(8,128)(2,1)} %get-tuple-element.83.attn, bf16[256,896]{1,0:T(8,128)(2,1)} %collective-permute-done.11.own_a, bf16[256,896]{1,0:T(8,128)(2,1)} %collective-permute-done.26.oth_a, ...), custom_call_target="tpu_custom_call" | custom-call | flops 402653184 | bytes 2621440 | tf_op jit(solution)/shard_map/pallas_call | solution.py:176
  159.5 4.4 %collective-permute-start.29 = (bf16[512,512]{1,0:T(8,128)(2,1)S(1)}, bf16[512,512]{1,0:T(8,128)(2,1)}, u32[]{:S(2)}, u32[]{:S(2)}) collective-permute-start(bf16[512,512]{1,0:T(8,128)(2,1)S(1)} %copy-done.4), channel_id=1, source_target_pairs={{0,2},{3,1},{6,4},{5,7},{9,11},{10,8},{15,13},{12,14},{16,18},{19,... | collective-permute-start | bytes 1572872 | tf_op jit(solution)/shard_map/ppermute | solution.py:634
  163.9 2.0 %shard_map.167.tb1 = bf16[512,384]{1,0:T(8,128)(2,1)} custom-call(s32[11]{0:T(128)} %fusion.8.sc, bf16[512,384]{1,0:T(8,128)(2,1)} %get-tuple-element.84.kept, bf16[512,384]{1,0:T(8,128)(2,1)} %collective-permute-done.31.came), custom_call_target="tpu_custom_call" | custom-call | flops 196608 | bytes 1179648 | tf_op jit(solution)/shard_map/pallas_call | solution.py:176
  165.9 2.0 %collective-permute-start.32 = (bf16[512,384]{1,0:T(8,128)(2,1)}, bf16[512,384]{1,0:T(8,128)(2,1)}, u32[]{:S(2)}, u32[]{:S(2)}) collective-permute-start(bf16[512,384]{1,0:T(8,128)(2,1)} %shard_map.167.tb1), channel_id=1, source_target_pairs={{0,2},{3,1},{6,4},{5,7},{9,11},{10,8},{15,13},{12,14},{16,18},{19,... | collective-permute-start | bytes 1179656 | tf_op jit(solution)/shard_map/ppermute | solution.py:634
  169.8 4.3 %collective-permute-done.32.cb1 = bf16[512,384]{1,0:T(8,128)(2,1)} collective-permute-done((bf16[512,384]{1,0:T(8,128)(2,1)}, bf16[512,384]{1,0:T(8,128)(2,1)}, u32[]{:S(2)}, u32[]{:S(2)}) %collective-permute-start.32) | collective-permute-done | bytes 393248 | tf_op jit(solution)/shard_map/ppermute | solution.py:634
  174.1 3.8 %shard_map.168 = bf16[512,896]{1,0:T(8,128)(2,1)} custom-call(s32[11]{0:T(128)} %fusion.8.sc, bf16[512,896]{1,0:T(8,128)(2,1)} %get-tuple-element.47.own, bf16[512,896]{1,0:T(8,128)(2,1)} %shard_map.163.ta, bf16[512,896]{1,0:T(8,128)(2,1)} %collective-permute-done.20.ca, bf16[512,512]{1,0:T(8,128)(2,1)} %shard_map.165.tb0, ...), custom_call_target="tpu_custom_call" | custom-call | flops 458752 | bytes 5505024 | tf_op jit(solution)/shard_map/pallas_call | solution.py:176
  (106 shorter events, 18.5 us)
Async XLA Ops:
  0.6 143.3 %copy-start = (bf16[896,1024]{1,0:T(8,128)(2,1)S(1)}, bf16[896,1024]{1,0:T(8,128)(2,1)}, u32[]{:S(2)}) copy-start(bf16[896,1024]{1,0:T(8,128)(2,1)} %param.24) | copy-start | bytes 5505028
  1.7 9.8 %collective-permute-start = (bf16[896,128]{1,0:T(8,128)(2,1)S(1)}, bf16[896,128]{1,0:T(8,128)(2,1)S(1)}, u32[]{:S(2)}, u32[]{:S(2)}) collective-permute-start(bf16[896,128]{1,0:T(8,128)(2,1)S(1)} %constant_dynamic-slice_fusion.3), channel_id=1, source_target_pairs={{0,4},{4,12},{12,8},{8,0},{1,5},{5,13},{13,9},{9,1},{2,6},{6,14},{... | collective-permute-start | bytes 688136 | tf_op jit(solution)/shard_map/ppermute | solution.py:555
  4.8 11.5 %collective-permute-start.2 = (bf16[896,128]{1,0:T(8,128)(2,1)S(1)}, bf16[896,128]{1,0:T(8,128)(2,1)S(1)}, u32[]{:S(2)}, u32[]{:S(2)}) collective-permute-start(bf16[896,128]{1,0:T(8,128)(2,1)S(1)} %constant_dynamic-slice_fusion.3), channel_id=1, source_target_pairs={{4,0},{12,4},{8,12},{0,8},{5,1},{13,5},{9,13},{1,9},{6,2},{14,6},{... | collective-permute-start | bytes 688136 | tf_op jit(solution)/shard_map/ppermute | solution.py:555
  11.5 24.9 %copy-start.10 = (bf16[896,128]{1,0:T(8,128)(2,1)}, bf16[896,128]{1,0:T(8,128)(2,1)S(1)}, u32[]{:S(2)}) copy-start(bf16[896,128]{1,0:T(8,128)(2,1)S(1)} %collective-permute-done.r1) | copy-start | bytes 688132
  16.4 12.9 %copy-start.11 = (bf16[896,128]{1,0:T(8,128)(2,1)}, bf16[896,128]{1,0:T(8,128)(2,1)S(1)}, u32[]{:S(2)}) copy-start(bf16[896,128]{1,0:T(8,128)(2,1)S(1)} %collective-permute-done.2.r3) | copy-start | bytes 688132
  16.4 20.1 %collective-permute-start.4 = (bf16[896,256]{1,0:T(8,128)(2,1)S(1)}, bf16[896,256]{1,0:T(8,128)(2,1)}, u32[]{:S(2)}, u32[]{:S(2)}) collective-permute-start(bf16[896,256]{1,0:T(8,128)(2,1)S(1)} %constant_dynamic-slice_fusion.2), channel_id=1, source_target_pairs={{0,4},{4,12},{12,8},{8,0},{1,5},{5,13},{13,9},{9,1},{2,6},{6,14},{... | collective-permute-start | bytes 1376264 | tf_op jit(solution)/shard_map/ppermute | solution.py:555
  18.1 8.5 %collective-permute-start.1 = (bf16[896,128]{1,0:T(8,128)(2,1)S(1)}, bf16[896,128]{1,0:T(8,128)(2,1)S(1)}, u32[]{:S(2)}, u32[]{:S(2)}) collective-permute-start(bf16[896,128]{1,0:T(8,128)(2,1)S(1)} %collective-permute-done.r1), channel_id=1, source_target_pairs={{0,16},{16,0},{1,17},{17,1},{2,18},{18,2},{3,19},{19,3},{4,20},{20... | collective-permute-start | bytes 688136 | tf_op jit(solution)/shard_map/ppermute | solution.py:557
  19.6 9.6 %collective-permute-start.3 = (bf16[896,128]{1,0:T(8,128)(2,1)S(1)}, bf16[896,128]{1,0:T(8,128)(2,1)S(1)}, u32[]{:S(2)}, u32[]{:S(2)}) collective-permute-start(bf16[896,128]{1,0:T(8,128)(2,1)S(1)} %collective-permute-done.2.r3), channel_id=1, source_target_pairs={{0,16},{16,0},{1,17},{17,1},{2,18},{18,2},{3,19},{19,3},{4,20},{20... | collective-permute-start | bytes 688136 | tf_op jit(solution)/shard_map/ppermute | solution.py:557
  20.1 16.3 %collective-permute-start.5 = (bf16[896,128]{1,0:T(8,128)(2,1)S(1)}, bf16[896,128]{1,0:T(8,128)(2,1)}, u32[]{:S(2)}, u32[]{:S(2)}) collective-permute-start(bf16[896,128]{1,0:T(8,128)(2,1)S(1)} %collective-permute-done.r1), channel_id=1, source_target_pairs={{0,4},{4,12},{12,8},{8,0},{1,5},{5,13},{13,9},{9,1},{2,6},{6,14},{... | collective-permute-start | bytes 688136 | tf_op jit(solution)/shard_map/ppermute | solution.py:555
  29.9 20.6 %copy-start.1 = (bf16[512,896]{1,0:T(8,128)(2,1)S(1)}, bf16[512,896]{1,0:T(8,128)(2,1)}, u32[]{:S(2)}) copy-start(bf16[512,896]{1,0:T(8,128)(2,1)} %w.5) | copy-start | bytes 2752516
  29.9 30.5 %copy-start.20 = (bf16[1024]{0:T(1024)(128)(2,1)S(1)}, bf16[1024]{0:T(1024)(128)(2,1)}, u32[]{:S(2)}) copy-start(bf16[1024]{0:T(1024)(128)(2,1)} %param.22) | copy-start | bytes 6148
  36.5 12.5 %collective-permute-start.6 = (bf16[896,256]{1,0:T(8,128)(2,1)S(1)}, bf16[896,256]{1,0:T(8,128)(2,1)}, u32[]{:S(2)}, u32[]{:S(2)}) collective-permute-start(bf16[896,256]{1,0:T(8,128)(2,1)S(1)} %constant_dynamic-slice_fusion.2), channel_id=1, source_target_pairs={{4,0},{12,4},{8,12},{0,8},{5,1},{13,5},{9,13},{1,9},{6,2},{14,6},{... | collective-permute-start | bytes 1376264 | tf_op jit(solution)/shard_map/ppermute | solution.py:555
  38.8 18.9 %collective-permute-start.8 = (bf16[896,256]{1,0:T(8,128)(2,1)}, bf16[896,256]{1,0:T(8,128)(2,1)S(1)}, u32[]{:S(2)}, u32[]{:S(2)}) collective-permute-start(bf16[896,256]{1,0:T(8,128)(2,1)} %collective-permute-done.4.r1), channel_id=1, source_target_pairs={{0,16},{16,0},{1,17},{17,1},{2,18},{18,2},{3,19},{19,3},{4,20},{20... | collective-permute-start | bytes 1376264 | tf_op jit(solution)/shard_map/ppermute | solution.py:557
  48.9 11.5 %collective-permute-start.7 = (bf16[896,256]{1,0:T(8,128)(2,1)}, bf16[896,256]{1,0:T(8,128)(2,1)S(1)}, u32[]{:S(2)}, u32[]{:S(2)}) collective-permute-start(bf16[896,256]{1,0:T(8,128)(2,1)} %collective-permute-done.4.r1), channel_id=1, source_target_pairs={{0,4},{4,12},{12,8},{8,0},{1,5},{5,13},{13,9},{9,1},{2,6},{6,14},{... | collective-permute-start | bytes 1376264 | tf_op jit(solution)/shard_map/ppermute | solution.py:555
  48.9 8.8 %collective-permute-start.10 = (bf16[896,128]{1,0:T(8,128)(2,1)}, bf16[896,128]{1,0:T(8,128)(2,1)S(1)}, u32[]{:S(2)}, u32[]{:S(2)}) collective-permute-start(bf16[896,128]{1,0:T(8,128)(2,1)} %collective-permute-done.5.r2), channel_id=1, source_target_pairs={{0,16},{16,0},{1,17},{17,1},{2,18},{18,2},{3,19},{19,3},{4,20},{20... | collective-permute-start | bytes 688136 | tf_op jit(solution)/shard_map/ppermute | solution.py:557
  50.6 24.5 %collective-permute-start.9 = (bf16[896,256]{1,0:T(8,128)(2,1)}, bf16[896,256]{1,0:T(8,128)(2,1)}, u32[]{:S(2)}, u32[]{:S(2)}) collective-permute-start(bf16[896,256]{1,0:T(8,128)(2,1)} %collective-permute-done.6.r3), channel_id=1, source_target_pairs={{0,16},{16,0},{1,17},{17,1},{2,18},{18,2},{3,19},{19,3},{4,20},{20... | collective-permute-start | bytes 1376264 | tf_op jit(solution)/shard_map/ppermute | solution.py:557
  60.4 14.7 %collective-permute-start.11 = (bf16[256,896]{1,0:T(8,128)(2,1)S(1)}, bf16[256,896]{1,0:T(8,128)(2,1)}, u32[]{:S(2)}, u32[]{:S(2)}) collective-permute-start(bf16[256,896]{1,0:T(8,128)(2,1)S(1)} %constant_dynamic-slice_fusion.1), channel_id=1, source_target_pairs={{0,4},{4,12},{12,8},{8,0},{1,5},{5,13},{13,9},{9,1},{2,6},{6,14},{... | collective-permute-start | bytes 1376264 | tf_op jit(solution)/shard_map/ppermute | solution.py:555
  66.6 8.5 %collective-permute-start.13 = (bf16[512,256]{1,0:T(8,128)(2,1)}, bf16[512,256]{1,0:T(8,128)(2,1)S(1)}, u32[]{:S(2)}, u32[]{:S(2)}) collective-permute-start(bf16[512,256]{1,0:T(8,128)(2,1)} %shard_map.160.x0), channel_id=1, source_target_pairs={{2,0},{0,1},{1,2},{6,4},{4,5},{5,6},{10,8},{8,9},{9,10},{14,12},{1... | collective-permute-start | bytes 786440 | tf_op jit(solution)/shard_map/ppermute | solution.py:583
  68.5 6.6 %collective-permute-start.14 = (bf16[512,256]{1,0:T(8,128)(2,1)}, bf16[512,256]{1,0:T(8,128)(2,1)S(1)}, u32[]{:S(2)}, u32[]{:S(2)}) collective-permute-start(bf16[512,256]{1,0:T(8,128)(2,1)} %shard_map.160.x0), channel_id=1, source_target_pairs={{2,1},{3,2},{1,3},{6,5},{7,6},{5,7},{10,9},{11,10},{9,11},{14,13},... | collective-permute-start | bytes 786440 | tf_op jit(solution)/shard_map/ppermute | solution.py:583
  75.0 21.5 %copy-start.8 = (bf16[512,256]{1,0:T(8,128)(2,1)}, bf16[512,256]{1,0:T(8,128)(2,1)S(1)}, u32[]{:S(2)}) copy-start(bf16[512,256]{1,0:T(8,128)(2,1)S(1)} %collective-permute-done.13.x1) | copy-start | bytes 786436
  75.8 12.4 %collective-permute-start.15 = (bf16[256,896]{1,0:T(8,128)(2,1)}, bf16[256,896]{1,0:T(8,128)(2,1)}, u32[]{:S(2)}, u32[]{:S(2)}) collective-permute-start(bf16[256,896]{1,0:T(8,128)(2,1)} %collective-permute-done.11.own_a), channel_id=1, source_target_pairs={{0,4},{4,12},{12,8},{8,0},{1,5},{5,13},{13,9},{9,1},{2,6},{6,14},{... | collective-permute-start | bytes 1376264 | tf_op jit(solution)/shard_map/ppermute | solution.py:555
  78.5 21.1 %collective-permute-start.12 = (bf16[896,256]{1,0:T(8,128)(2,1)}, bf16[896,256]{1,0:T(8,128)(2,1)S(1)}, u32[]{:S(2)}, u32[]{:S(2)}) collective-permute-start(bf16[896,256]{1,0:T(8,128)(2,1)} %copy-done.22), channel_id=1, source_target_pairs={{0,16},{16,0},{1,17},{17,1},{2,18},{18,2},{3,19},{19,3},{4,20},{20... | collective-permute-start | bytes 1376264 | tf_op jit(solution)/shard_map/ppermute | solution.py:557
  88.2 25.2 %collective-permute-start.16 = (bf16[256,896]{1,0:T(8,128)(2,1)}, bf16[256,896]{1,0:T(8,128)(2,1)}, u32[]{:S(2)}, u32[]{:S(2)}) collective-permute-start(bf16[256,896]{1,0:T(8,128)(2,1)} %collective-permute-done.15.own_b), channel_id=1, source_target_pairs={{0,16},{16,0},{1,17},{17,1},{2,18},{18,2},{3,19},{19,3},{4,20},{20... | collective-permute-start | bytes 1376264 | tf_op jit(solution)/shard_map/ppermute | solution.py:557
  90.5 8.1 %copy-start.21 = (bf16[512]{0:T(512)(128)(2,1)S(1)}, bf16[512]{0:T(512)(128)(2,1)}, u32[]{:S(2)}) copy-start(bf16[512]{0:T(512)(128)(2,1)} %param.20) | copy-start | bytes 3076
  96.5 13.9 %collective-permute-start.21 = (bf16[256,384]{1,0:T(8,128)(2,1)}, bf16[256,384]{1,0:T(8,128)(2,1)}, u32[]{:S(2)}, u32[]{:S(2)}) collective-permute-start(bf16[256,384]{1,0:T(8,128)(2,1)} %dynamic-slice.1), channel_id=1, source_target_pairs={{4,0},{12,4},{8,12},{0,8},{5,1},{13,5},{9,13},{1,9},{6,2},{14,6},{... | collective-permute-start | bytes 589832 | tf_op jit(solution)/shard_map/ppermute | solution.py:555
  99.2 35.1 %collective-permute-start.26 = (bf16[256,896]{1,0:T(8,128)(2,1)}, bf16[256,896]{1,0:T(8,128)(2,1)}, u32[]{:S(2)}, u32[]{:S(2)}) collective-permute-start(bf16[256,896]{1,0:T(8,128)(2,1)} %collective-permute-done.11.own_a), channel_id=1, source_target_pairs={{0,16},{16,0},{1,17},{17,1},{2,18},{18,2},{3,19},{19,3},{4,20},{20... | collective-permute-start | bytes 1376264 | tf_op jit(solution)/shard_map/ppermute | solution.py:557
  109.0 12.4 %copy-start.17 = (bf16[32,512]{1,0:T(8,128)(2,1)S(1)}, bf16[32,512]{1,0:T(8,128)(2,1)}, u32[]{:S(2)}) copy-start(bf16[32,512]{1,0:T(8,128)(2,1)} %get-tuple-element.74) | copy-start | bytes 98308
  109.0 12.8 %collective-permute-start.18 = (bf16[256,512]{1,0:T(8,128)(2,1)S(1)}, bf16[256,512]{1,0:T(8,128)(2,1)}, u32[]{:S(2)}, u32[]{:S(2)}) collective-permute-start(bf16[256,512]{1,0:T(8,128)(2,1)S(1)} %constant_dynamic-slice_fusion), channel_id=1, source_target_pairs={{4,0},{12,4},{8,12},{0,8},{5,1},{13,5},{9,13},{1,9},{6,2},{14,6},{... | collective-permute-start | bytes 786440 | tf_op jit(solution)/shard_map/ppermute | solution.py:555
  110.5 8.4 %collective-permute-start.24 = (bf16[32,512]{1,0:T(8,128)(2,1)}, bf16[32,512]{1,0:T(8,128)(2,1)S(1)}, u32[]{:S(2)}, u32[]{:S(2)}) collective-permute-start(bf16[32,512]{1,0:T(8,128)(2,1)} %get-tuple-element.74), channel_id=1, source_target_pairs={{4,0},{12,4},{0,8},{8,12},{5,1},{13,5},{1,9},{9,13},{6,2},{14,6},{... | collective-permute-start | bytes 98312 | tf_op jit(solution)/shard_map/ppermute | solution.py:648
  111.9 7.8 %collective-permute-start.23 = (bf16[32,512]{1,0:T(8,128)(2,1)}, bf16[32,512]{1,0:T(8,128)(2,1)S(1)}, u32[]{:S(2)}, u32[]{:S(2)}) collective-permute-start(bf16[32,512]{1,0:T(8,128)(2,1)} %get-tuple-element.74), channel_id=1, source_target_pairs={{12,0},{8,4},{4,8},{0,12},{13,1},{9,5},{5,9},{1,13},{14,2},{10,6},... | collective-permute-start | bytes 98312 | tf_op jit(solution)/shard_map/ppermute | solution.py:648
  113.4 8.0 %collective-permute-start.22 = (bf16[32,512]{1,0:T(8,128)(2,1)}, bf16[32,512]{1,0:T(8,128)(2,1)S(1)}, u32[]{:S(2)}, u32[]{:S(2)}) collective-permute-start(bf16[32,512]{1,0:T(8,128)(2,1)} %get-tuple-element.74), channel_id=1, source_target_pairs={{8,0},{0,4},{12,8},{4,12},{9,1},{1,5},{13,9},{5,13},{10,2},{2,6},{... | collective-permute-start | bytes 98312 | tf_op jit(solution)/shard_map/ppermute | solution.py:648
  113.4 8.0 %copy-start.2 = (bf16[512,896]{1,0:T(8,128)(2,1)S(1)}, bf16[512,896]{1,0:T(8,128)(2,1)}, u32[]{:S(2)}) copy-start(bf16[512,896]{1,0:T(8,128)(2,1)} %w.5) | copy-start | bytes 2752516
  118.8 11.9 %collective-permute-start.17 = (bf16[512,896]{1,0:T(8,128)(2,1)}, bf16[512,896]{1,0:T(8,128)(2,1)S(1)}, u32[]{:S(2)}, u32[]{:S(2)}) collective-permute-start(bf16[512,896]{1,0:T(8,128)(2,1)} %get-tuple-element.69), channel_id=1, source_target_pairs={{0,1},{1,0},{2,3},{3,2},{4,5},{5,4},{6,7},{7,6},{8,9},{9,8},{10,11... | collective-permute-start | bytes 2752520 | tf_op jit(solution)/shard_map/ppermute | solution.py:624
  121.7 1.8 collective-permute-start.25
  121.8 8.9 %collective-permute-start.19 = (bf16[256,512]{1,0:T(8,128)(2,1)}, bf16[256,512]{1,0:T(8,128)(2,1)S(1)}, u32[]{:S(2)}, u32[]{:S(2)}) collective-permute-start(bf16[256,512]{1,0:T(8,128)(2,1)} %collective-permute-done.18.own_b), channel_id=1, source_target_pairs={{0,16},{16,0},{1,17},{17,1},{2,18},{18,2},{3,19},{19,3},{4,20},{20... | collective-permute-start | bytes 786440 | tf_op jit(solution)/shard_map/ppermute | solution.py:557
  131.7 5.9 %copy-start.15 = (f32[32,1]{1,0:T(8,128)S(1)}, f32[32,1]{1,0:T(8,128)}, u32[]{:S(2)}) copy-start(f32[32,1]{1,0:T(8,128)} %get-tuple-element.64.inverse_ref) | copy-start | bytes 388
  131.7 9.2 %copy-start.18 = (f32[32,1]{1,0:T(8,128)S(1)}, f32[32,1]{1,0:T(8,128)}, u32[]{:S(2)}) copy-start(f32[32,1]{1,0:T(8,128)} %get-tuple-element.86) | copy-start | bytes 388
  131.7 12.3 %copy-start.16 = (bf16[32,32]{1,0:T(8,128)(2,1)S(1)}, bf16[32,32]{1,0:T(8,128)(2,1)}, u32[]{:S(2)}) copy-start(bf16[32,32]{1,0:T(8,128)(2,1)} %get-tuple-element.65.hits_ref) | copy-start | bytes 6148
  134.3 8.3 %copy-start.3 = (bf16[512,896]{1,0:T(8,128)(2,1)S(1)}, bf16[512,896]{1,0:T(8,128)(2,1)}, u32[]{:S(2)}) copy-start(bf16[512,896]{1,0:T(8,128)(2,1)} %shard_map.163.ta) | copy-start | bytes 2752516
  137.6 15.5 %collective-permute-start.27 = (bf16[512,512]{1,0:T(8,128)(2,1)}, bf16[512,512]{1,0:T(8,128)(2,1)S(1)}, u32[]{:S(2)}, u32[]{:S(2)}) collective-permute-start(bf16[512,512]{1,0:T(8,128)(2,1)} %get-tuple-element.79), channel_id=1, source_target_pairs={{0,1},{1,0},{2,3},{3,2},{4,5},{5,4},{6,7},{7,6},{8,9},{9,8},{10,11... | collective-permute-start | bytes 1572872 | tf_op jit(solution)/shard_map/ppermute | solution.py:624
  137.7 6.3 %collective-permute-start.30 = (bf16[32,896]{1,0:T(8,128)(2,1)S(1)}, bf16[32,896]{1,0:T(8,128)(2,1)S(1)}, u32[]{:S(2)}, u32[]{:S(2)}) collective-permute-start(bf16[32,896]{1,0:T(8,128)(2,1)S(1)} %get-tuple-element.76), channel_id=1, source_target_pairs={{0,2},{1,3},{2,0},{3,1},{4,6},{5,7},{6,4},{7,5},{8,10},{9,11},{10,... | collective-permute-start | bytes 172040 | tf_op jit(solution)/shard_map/ppermute | solution.py:655
  141.1 11.9 %collective-permute-start.28 = (bf16[256,384]{1,0:T(8,128)(2,1)}, bf16[256,384]{1,0:T(8,128)(2,1)}, u32[]{:S(2)}, u32[]{:S(2)}) collective-permute-start(bf16[256,384]{1,0:T(8,128)(2,1)} %collective-permute-done.21.own_b), channel_id=1, source_target_pairs={{0,16},{16,0},{1,17},{17,1},{2,18},{18,2},{3,19},{19,3},{4,20},{20... | collective-permute-start | bytes 589832 | tf_op jit(solution)/shard_map/ppermute | solution.py:557
  142.7 26.6 %collective-permute-start.20 = (bf16[512,896]{1,0:T(8,128)(2,1)S(1)}, bf16[512,896]{1,0:T(8,128)(2,1)}, u32[]{:S(2)}, u32[]{:S(2)}) collective-permute-start(bf16[512,896]{1,0:T(8,128)(2,1)S(1)} %copy-done.3), channel_id=1, source_target_pairs={{2,0},{1,3},{7,5},{4,6},{8,10},{11,9},{13,15},{14,12},{18,16},{17,... | collective-permute-start | bytes 2752520 | tf_op jit(solution)/shard_map/ppermute | solution.py:634
  146.2 17.7 %all-to-all-start = ((bf16[16,8,384]{2,1,0:T(8,128)(2,1)}), bf16[16,8,384]{2,1,0:T(8,128)(2,1)S(1)}, u32[]{:S(2)}, u32[]{:S(2)}) async-start(bf16[16,8,384]{2,1,0:T(8,128)(2,1)} %bitcast.4), calls=%async_computation | async-start | bytes 196608 | tf_op jit(solution)/shard_map/all_to_all | solution.py:676
  156.0 12.6 %copy-start.19 = (f32[8,256]{1,0:T(8,128)S(1)}, f32[8,256]{1,0:T(8,128)}, u32[]{:S(2)}) copy-start(f32[8,256]{1,0:T(8,128)} %param.25) | copy-start | bytes 24580
  159.1 4.8 %collective-permute-start.31 = (bf16[512,384]{1,0:T(8,128)(2,1)}, bf16[512,384]{1,0:T(8,128)(2,1)}, u32[]{:S(2)}, u32[]{:S(2)}) collective-permute-start(bf16[512,384]{1,0:T(8,128)(2,1)} %get-tuple-element.85), channel_id=1, source_target_pairs={{0,1},{1,0},{2,3},{3,2},{4,5},{5,4},{6,7},{7,6},{8,9},{9,8},{10,11... | collective-permute-start | bytes 1179656 | tf_op jit(solution)/shard_map/ppermute | solution.py:624
  159.5 10.2 %collective-permute-start.29 = (bf16[512,512]{1,0:T(8,128)(2,1)S(1)}, bf16[512,512]{1,0:T(8,128)(2,1)}, u32[]{:S(2)}, u32[]{:S(2)}) collective-permute-start(bf16[512,512]{1,0:T(8,128)(2,1)S(1)} %copy-done.4), channel_id=1, source_target_pairs={{0,2},{3,1},{6,4},{5,7},{9,11},{10,8},{15,13},{12,14},{16,18},{19,... | collective-permute-start | bytes 1572872 | tf_op jit(solution)/shard_map/ppermute | solution.py:634
  165.9 8.2 %collective-permute-start.32 = (bf16[512,384]{1,0:T(8,128)(2,1)}, bf16[512,384]{1,0:T(8,128)(2,1)}, u32[]{:S(2)}, u32[]{:S(2)}) collective-permute-start(bf16[512,384]{1,0:T(8,128)(2,1)} %shard_map.167.tb1), channel_id=1, source_target_pairs={{0,2},{3,1},{6,4},{5,7},{9,11},{10,8},{15,13},{12,14},{16,18},{19,... | collective-permute-start | bytes 1179656 | tf_op jit(solution)/shard_map/ppermute | solution.py:634
  (11 other events, 21.4 us)

commit v4 on v3

--- a/solution.py
+++ b/solution.py
@@ -156,7 +156,8 @@
 
 VMEM = pl.BlockSpec(memory_space=pltpu.VMEM)
 SMEM = pl.BlockSpec(memory_space=pltpu.SMEM)
-T, GROUP, KEEP_0, KEEP_1, MINE_A, KEY_FROM, VALUE_FROM = range(4, 11)
+T, GROUP, KEEP_0, KEEP_1, MINE_A, KEY_FROM, VALUE_FROM, SEND_1, SEND_2 = range(4, 13)
+TAIL = 20
 
 
 def dot(a, b):
@@ -171,14 +172,14 @@
     return pl.ds(pl.multiple_of(start, 128), size)
 
 
-def call(kernel, outs, flops, scalars, *args):
+def call(kernel, outs, flops, scalars, *args, vmem=60):
     moved = sum(a.size * a.dtype.itemsize for a in (*args, *outs))
     return pl.pallas_call(
         kernel,
         in_specs=[SMEM] + [VMEM] * len(args),
         out_specs=[VMEM] * len(outs),
         out_shape=outs,
-        compiler_params=pltpu.CompilerParams(vmem_limit_bytes=60 * 1024 * 1024),
+        compiler_params=pltpu.CompilerParams(vmem_limit_bytes=vmem * 1024 * 1024),
         cost_estimate=pl.CostEstimate(flops=flops, bytes_accessed=moved, transcendentals=0),
     )(scalars, *args)
 
@@ -296,27 +297,31 @@
     )(scalars, hidden, gain[None, :], member)
 
 
-def keyval_kernel(sc, b0, b1, b2, b3, w, r1, r2, r3, y1, y2, y3, bias, cos_ref, sin_ref, out_ref):
+def projection_kernel(sc, b0, b1, b2, b3, wk, wq, r1, r2, r3, y1, y3, kv_ref, own_ref, oth_ref):
+    g = sc[GROUP]
+    half = own_ref.shape[1]
+    own = dot(b1[...], r1[...]) + dot(b2[...], r2[...]) + dot(b3[...], r3[...])
+    oth = dot(b1[...], y1[...]) + dot(b3[...], y3[...])
+    base = dot(b0[...], wk[...])
+    for h in range(wk.shape[1] // HD):
+        at = slice(h * HD, (h + 1) * HD)
+        kv_ref[:, at] = base[:, at] + jnp.where(g == h, own[:, :HD], oth[:, :HD])
+    own_ref[...] = own[:, HD:] + dot(b0[...], wq[:, lanes(g * half, half)])
+    oth_ref[...] = oth[:, HD:] + dot(b0[...], wq[:, lanes((1 - g) * half, half)])
+
+
+def keyval_kernel(sc, kv_ref, b2, y2, bias, cos_ref, sin_ref, out_ref, send_1, send_2):
     g, t = sc[GROUP], sc[T]
-    base = dot(b0[...], w[...])
-    own = dot(b1[...], r1[...]) + dot(b2[...], r2[...]) + dot(b3[...], r3[...])
-    oth = dot(b1[...], y1[...]) + dot(b2[...], y2[...]) + dot(b3[...], y3[...])
-    heads = w.shape[1] // HD
+    last = dot(b2[...], y2[:, :HD])
+    heads = kv_ref.shape[1] // HD
     keyed = t * heads < KV_HEADS
     for h in range(heads):
         at = slice(h * HD, (h + 1) * HD)
-        x = base[:, at] + jnp.where(g == h, own, oth)
+        x = kv_ref[:, at] + jnp.where(g == h, 0.0, last)
         x = x + bias[:, lanes((t * heads + h) * HD, HD)].astype(f32)
         out_ref[:, at] = jnp.where(keyed, turn(x, cos_ref[...], sin_ref[...]), x).astype(bf16)
-
-
-def query_kernel(sc, b0, b1, b2, b3, w, r1, r2, r3, y1, y3, own_ref, oth_ref):
-    g = sc[GROUP]
-    half = own_ref.shape[1]
-    own = dot(b0[...], w[:, lanes(g * half, half)]) + dot(b1[...], r1[...])
-    own_ref[...] = own + dot(b2[...], r2[...]) + dot(b3[...], r3[...])
-    oth = dot(b0[...], w[:, lanes((1 - g) * half, half)]) + dot(b1[...], y1[...])
-    oth_ref[...] = oth + dot(b3[...], y3[...])
+    send_1[...] = out_ref[:, lanes(sc[SEND_1] * HD, HD)]
+    send_2[...] = out_ref[:, lanes(sc[SEND_2] * HD, HD)]
 
 
 def attention_kernel(
@@ -347,11 +352,11 @@
 
     def pick(origin):
         return jnp.where(
-            origin == 0, x0[:, here], jnp.where(origin == 1, x1[:, here], x2[:, here])
+            origin == 0, x0[:, here], jnp.where(origin == 1, x1[...], x2[...])
         )
 
     keys, values = pick(sc[KEY_FROM]), pick(sc[VALUE_FROM])
-    query_ref[...] = oth_ref[...] + dot(b2[...], y2[...])
+    query_ref[...] = oth_ref[...] + dot(b2[...], y2[:, HD:])
     rows = 128
     pooled = jnp.zeros((member_ref.shape[0], 2 * wide), f32)
     for i in range(tokens // rows):
@@ -407,8 +412,12 @@
 
 def project(attn, weights, ref):
     half = attn.shape[1] // 2
-    first, second = weights()
-    ref[...] = (dot(attn[:, :half], first) + dot(attn[:, half:], second)).astype(bf16)
+    left, right = attn[:, :half], attn[:, half:]
+    lo = 0
+    for first, second in weights():
+        hi = lo + first.shape[1]
+        ref[:, lo:hi] = (dot(left, first) + dot(right, second)).astype(bf16)
+        lo = hi
 
 
 def project_two(keep, attn, first, second, sent, kept):
@@ -428,20 +437,22 @@
     g = sc[GROUP]
 
     def stored():
-        return (
-            w[pl.ds(pl.multiple_of(g * half, half), half), :],
-            w[pl.ds(pl.multiple_of((1 - g) * half, half), half), :],
-        )
-
-    project_two(sc[KEEP_0], attn, stored, lambda: (own_b[...], oth_b[...]), sent, kept)
-
-
-def project_kernel(lo, hi, sc, attn, own_a, oth_a, own_b, oth_b, sent, kept):
+        return [
+            (
+                w[pl.ds(pl.multiple_of(g * half, half), half), :],
+                w[pl.ds(pl.multiple_of((1 - g) * half, half), half), :],
+            )
+        ]
+
+    project_two(sc[KEEP_0], attn, stored, lambda: [(own_b[...], oth_b[...])], sent, kept)
+
+
+def project_kernel(sc, attn, own_a, oth_a, own_b, oth_b, own_c, oth_c, sent, kept):
     project_two(
         sc[KEEP_1],
         attn,
-        lambda: (own_a[:, lo:hi], oth_a[:, lo:hi]),
-        lambda: (own_b[...], oth_b[...]),
+        lambda: [(own_a[...], oth_a[...])],
+        lambda: [(own_b[...], oth_b[...]), (own_c[...], oth_c[...])],
         sent,
         kept,
     )
@@ -451,13 +462,14 @@
     total[...] = (kept[...].astype(f32) + came[...].astype(f32)).astype(bf16)
 
 
-def finish_kernel(sc, own, ta, ca, tb0, cb0, tb1, cb1, out):
-    cut = tb0.shape[1]
-    mine = sc[MINE_A] == 1
-    for lo, hi, t, c in ((0, cut, tb0, cb0), (cut, own.shape[1], tb1, cb1)):
-        a = ta[:, lo:hi].astype(f32) + ca[:, lo:hi].astype(f32)
-        b = t[...].astype(f32) + c[...].astype(f32)
-        out[:, lo:hi] = (own[:, lo:hi].astype(f32) + jnp.where(mine, a, b)).astype(bf16)
+def finish_kernel(sc, own, ta, ca, tb, cb, out):
+    @pl.when(sc[MINE_A] == 1)
+    def _():
+        out[...] = (own[...].astype(f32) + (ta[...].astype(f32) + ca[...].astype(f32))).astype(bf16)
+
+    @pl.when(sc[MINE_A] == 0)
+    def _():
+        out[...] = (own[...].astype(f32) + (tb[...].astype(f32) + cb[...].astype(f32))).astype(bf16)
 
 
 def folded_ring(n):
@@ -496,15 +508,18 @@
     across = [(i, i ^ 2) for i in range(n_tp)]
     per_dev = w_keyval.shape[1] // HD
     rounds = [[], []]
+    sends = [[0] * n_tp, [0] * n_tp]
     origin = []
     for tt in range(n_tp):
-        for source in (tt // per_dev, (KV_HEADS + tt) // per_dev):
+        for head in (tt, KV_HEADS + tt):
+            source = head // per_dev
             if source == tt:
                 origin.append(0)
                 continue
             for k, pairs in enumerate(rounds):
                 if all(a != source and b != tt for a, b in pairs):
                     pairs.append((source, tt))
+                    sends[k][source] = head % per_dev
                     origin.append(k + 1)
                     break
     table = []
@@ -514,7 +529,7 @@
                 stays = [int(source_of[d][m] % 2 == tt % 2) for m in range(2)]
                 mine = int(tt in (source_of[d][0], source_of[d][2]))
                 table.append(
-                    [*source_of[d], tt, gg, *stays, mine, *origin[2 * tt : 2 * tt + 2]]
+                    [*source_of[d], tt, gg, *stays, mine, *origin[2 * tt : 2 * tt + 2], sends[0][tt], sends[1][tt]]
                 )
     scalars = lax.dynamic_slice_in_dim(
         jnp.array(table, jnp.int32),
@@ -533,70 +548,69 @@
         lengths, list_ids, list_slot, tokens
     )
 
-    kv_own = own_half(w_keyval, 1)
-    q_own = own_half(w_query, 1)
+    kq_own = jnp.concatenate([own_half(w_keyval, 1), own_half(w_query, 1)], axis=1)
     o_own = own_half(w_out, 0)
     cut = share // 256 * 128 + 128
 
-    own = {"k": kv_own, "q": q_own, "o": o_own, "a": o_own[:, :cut], "b": o_own[:, cut:]}
-    stages = [["k1", "k3"], ["q1", "k2"], ["q3"], ["q2"], ["o1"], ["o2"], ["a3", "b3"]]
-    lag = 3
+    own = {"q": kq_own, "o": o_own, "a": o_own[:, :cut], "b": o_own[:, cut:]}
+    stages = [["q1"], ["q3"], ["q2"], ["o1", "a3"], ["o2", "b3"]]
+    lag = 2
     ring_of, swapped = {}, {}
 
-    def run_stage(i, *ties):
+    def run_stage(i, *ties, swap_ties=()):
         ties = list(ties)
         if i >= 1:
             ties += [ring_of[key] for key in stages[i - 1]]
-        if lag <= i < len(stages) - 1:
+        if i >= lag:
             ties += [swapped[key] for key in stages[i - lag]]
         for key in stages[i]:
             piece = ring_of[key[0] + "1"] if key[1] == "2" else own[key[0]]
             pairs = backward if key[1] == "3" else forward
             ring_of[key] = lax.ppermute(after(piece, *ties) if ties else piece, "dp", pairs)
         for key in stages[i]:
-            swapped[key] = lax.ppermute(ring_of[key], "groups", swap)
+            came = ring_of[key]
+            if swap_ties:
+                came = after(came, *swap_ties, *[ring_of[k] for k in stages[i]])
+            swapped[key] = lax.ppermute(came, "groups", swap)
 
     run_stage(0)
-    run_stage(1, cosine)
-    *blocks, own_input, pooled_hidden = prepare(
-        scalars, after(hidden, swapped["k1"], swapped["k3"]), gain, member, n_dp
-    )
-    run_stage(2, blocks[0])
+    *blocks, own_input, pooled_hidden = prepare(scalars, hidden, gain, member, n_dp)
+    run_stage(1, blocks[0], cosine)
+    run_stage(2)
     run_stage(3)
-    run_stage(4)
     hidden_lists = dot(hits, (pooled_hidden * inverse).astype(bf16))
 
     shape = jax.ShapeDtypeStruct
     work = 2 * tokens * width
-    (kv_mine,) = call(
-        keyval_kernel,
-        [shape((tokens, w_keyval.shape[1]), bf16)],
-        work * w_keyval.shape[1],
+    q_half = w_query.shape[1] // 2
+    kv_sum, sum_own, sum_oth = call(
+        projection_kernel,
+        [shape((tokens, w_keyval.shape[1]), f32)] + [shape((tokens, q_half), f32)] * 2,
+        work * (q_half * 2 + w_keyval.shape[1]),
         scalars,
         *blocks,
         w_keyval,
-        *[r["k%d" % m] for r in (ring_of, swapped) for m in range(1, n_dp)],
+        w_query,
+        *[ring_of[key] for key in ("q1", "q2", "q3")],
+        *[swapped[key] for key in ("q1", "q3")],
+    )
+    kv_mine, *kv_sent = call(
+        keyval_kernel,
+        [shape(kv_sum.shape, bf16)] + [shape((tokens, HD), bf16)] * 2,
+        tokens * share * HD,
+        scalars,
+        kv_sum,
+        blocks[2],
+        swapped["q2"],
         b_keyval[None, :],
         cosine,
         sine,
     )
-    kv_came = [lax.ppermute(kv_mine, "tp", pairs) for pairs in rounds]
-    run_stage(5, *kv_came)
-    q_half = w_query.shape[1] // 2
-    sum_own, sum_oth = call(
-        query_kernel,
-        [shape((tokens, q_half), f32)] * 2,
-        work * q_half * 2,
-        scalars,
-        *blocks,
-        w_query,
-        *[ring_of[key] for key in ("q1", "q2", "q3")],
-        *[swapped[key] for key in ("q1", "q3")],
-    )
-    run_stage(6, sum_own)
+    kv_came = [lax.ppermute(x, "tp", pairs) for x, pairs in zip(kv_sent, rounds)]
+    run_stage(4, sum_own, swap_ties=[*kv_came, swapped["o1"]])
     attn, attn_lists = attend(
         scalars,
-        after(sum_own, ring_of["o1"]),
+        sum_own,
         sum_oth,
         blocks[2],
         swapped["q2"],
@@ -620,12 +634,13 @@
             scalars,
             attn,
             *weights,
+            vmem=TAIL,
         )
         return sent, kept, lax.ppermute(sent, "tp", core)
 
     def exchange(kept, came, m):
         (total,) = call(
-            add_kernel, [shape(kept.shape, bf16)], kept.size, scalars, kept, came
+            add_kernel, [shape(kept.shape, bf16)], kept.size, scalars, kept, came, vmem=TAIL
         )
         pairs = []
         for d in range(n_dp):
@@ -636,28 +651,25 @@
     def both(key):
         return ring_of[key], swapped[key]
 
-    sent_a, kept_a, came_a = project_pair(
-        project_own_kernel, share, attn, w_out, *both("o2")
-    )
-    block_a = exchange(kept_a, after(came_a, swapped["a3"]), 0)
-
-    attn_lists = after(attn_lists, ring_of["b3"])
+    sent_a, kept_a, came_a = project_pair(project_own_kernel, share, attn, w_out, *both("o2"))
+    block_a = exchange(kept_a, came_a, 0)
+
+    attn_lists = after(attn_lists, ring_of["o2"], ring_of["b3"])
     lists_sum = attn_lists.astype(f32)
     for m in range(1, n_dp):
         pairs = [(source_of[d][m], d) for d in range(n_dp)]
         lists_sum = lists_sum + lax.ppermute(attn_lists, "dp", pairs).astype(f32)
-    lists_sum = after(lists_sum.astype(bf16), sent_a)
+    lists_sum = lists_sum.astype(bf16)
     first = jnp.where(g == 0, lists_sum[:, :q_half], lists_sum[:, q_half:])
     second = jnp.where(g == 0, lists_sum[:, q_half:], lists_sum[:, :q_half])
     plane = dot(jnp.concatenate([first, second], axis=1), w_out).astype(bf16)
     plane = plane.astype(f32) + lax.ppermute(plane, "tp", core).astype(f32)
-    plane16 = after(plane.astype(bf16), block_a[0])
+    plane16 = plane.astype(bf16)
     crossed = lax.ppermute(plane16, "tp", across)
-    rows = after(attn, block_a[0], plane16)
-    sent_b0, kept_b0, came_b0 = project_pair(
-        functools.partial(project_kernel, 0, cut), cut, rows, *both("o1"), *both("a3")
-    )
-    plane = after(plane, sent_b0)
+    sent_b, kept_b, came_b = project_pair(
+        project_kernel, share, after(attn, block_a[0]), *both("o1"), *both("a3"), *both("b3")
+    )
+    plane = after(plane, sent_b)
     plane = plane + crossed.astype(f32)
     plane = (jnp.where(t == z, plane, 0.0) + hidden_lists).astype(bf16)
     vec_lists = dot(plane, w_pool).astype(bf16)
@@ -673,22 +685,13 @@
         ],
         axis=3,
     ).reshape(n_dp * n_tp, lists_own, cols + HD)
-    late = lax.all_to_all(late, ("dp", "tp"), split_axis=0, concat_axis=0, tiled=True)
+    block_b = exchange(kept_b, after(came_b, vec_lists, block_a[1]), 1)
+    late = lax.all_to_all(after(late, block_b[0]), ("dp", "tp"), split_axis=0, concat_axis=0, tiled=True)
     late = late.reshape(n_dp, n_tp, lists_own, cols + HD).astype(f32)
     totals = jnp.sum(late[..., :cols], axis=(0, 1))
     counts = jnp.sum(late[:, 0, :, cols], axis=0)
     residual_sums = totals - counts[:, None] * centroids
     list_counts = counts.astype(jnp.int32)
-    block_b0 = exchange(kept_b0, after(came_b0, swapped["b3"]), 1)
-    rows = after(rows, block_b0[0], vec_lists)
-    _, kept_b1, came_b1 = project_pair(
-        functools.partial(project_kernel, cut, share),
-        share - cut,
-        rows,
-        *both("o1"),
-        *both("b3"),
-    )
-    block_b1 = exchange(kept_b1, came_b1, 1)
     (layer_out,) = call(
         finish_kernel,
         [shape((tokens, share), bf16)],
@@ -696,8 +699,8 @@
         scalars,
         own_input,
         *block_a,
-        *block_b0,
-        *block_b1,
+        *block_b,
+        vmem=TAIL,
     )
     return (layer_out, residual_sums, list_counts)
 

time: 179 us -> 160 us (0.89)
  starting transfers between devices: 53.5 us -> 29.2 us
  blocking collectives: 0 us -> 12.3 us
  Pallas kernels: 50.7 us -> 42.4 us
    ppermute x10 -> x7, waiting for transfers between devices: 25.9 us -> 39 us  [run_stage(): lax.ppermute(after(piece, *ties) if ties else piece, 'dp', pairs)]
    all_to_all x0 -> x1, blocking collectives: none -> 12.3 us  [shards(): lax.all_to_all(after(late, block_b[0]), ('dp', 'tp'), split_axis=0, conca...]
    ppermute x12 -> x9, waiting for transfers between devices: 23.7 us -> 13.4 us  [the longest x7 8.9 us: run_stage(): swapped[key] = lax.ppermute(came, 'groups', swap)]
    pallas_call x9 -> x7, Pallas kernels: 32.6 us -> 24.3 us  [call(): pl.pallas_call(kernel, in_specs=[SMEM] + [VMEM] * len(args), out_specs=[V...]
    all_to_all x1 -> x0, starting transfers between devices: 6.83 us -> none  [shards(): lax.all_to_all(late, ('dp', 'tp'), split_axis=0, concat_axis=0, tiled=True)]
    ppermute x10 -> x7, starting transfers between devices: 17 us -> 11.6 us  [run_stage(): lax.ppermute(after(piece, *ties) if ties else piece, 'dp', pairs)]
    ppermute x12 -> x9, starting transfers between devices: 15.1 us -> 10.1 us  [the longest x7 7.54 us: run_stage(): swapped[key] = lax.ppermute(came, 'groups', swap)]
    ppermute x3 -> x2, waiting for transfers between devices: 4.81 us -> 0.01 us  [exchange(): return (total, lax.ppermute(total, ('dp', 'tp'), pairs))]
  transfers between devices with their start and end apart: 34 -> 25, of which waited for: 15 -> 17; matrix products, arithmetic and copies ran while one was open for 5% -> 6% of each run, Pallas kernels for 25% -> 22%
where the time goes in v4:
time: 160 us; the launch traced here: 159 us
  waiting for transfers between devices  58.3 us (36%)
  Pallas kernels  42.4 us (26%)
  starting transfers between devices  29.2 us (18%)
  blocking collectives  12.3 us (8%)
  local copies, waits for them, and re-layouts  10.6 us (7%)
  other arithmetic  4.04 us (3%)
  matrix products  1.74 us (1%)
    ppermute x7, waiting for transfers between devices, run_stage(): lax.ppermute(after(piece, *ties) if ties else piece, 'dp', pairs)  39 us
    pallas_call x7, Pallas kernels, call(): pl.pallas_call(kernel, in_specs=[SMEM] + [VMEM] * len(args), out_specs=[V...  24.3 us
    all_to_all x1, blocking collectives, shards(): lax.all_to_all(after(late, block_b[0]), ('dp', 'tp'), split_axis=0, conca...  12.3 us
    ppermute x7, starting transfers between devices, run_stage(): lax.ppermute(after(piece, *ties) if ties else piece, 'dp', pairs)  11.6 us
    ppermute x7, waiting for transfers between devices, run_stage(): swapped[key] = lax.ppermute(came, 'groups', swap)  8.9 us
    pallas_call x1, Pallas kernels, attend(): pl.pallas_call(attention_kernel, in_specs=[SMEM] + [VMEM] * (1 + len(rest...  8.56 us
    ppermute x7, starting transfers between devices, run_stage(): swapped[key] = lax.ppermute(came, 'groups', swap)  7.54 us
    pallas_call x1, Pallas kernels, prepare(): pl.pallas_call(prep_kernel, grid_spec=pltpu.PrefetchScalarGridSpec(num_sc...  6.53 us
  transfers between devices with their start and end apart: 25, of which 17 were waited for; matrix products, arithmetic and copies ran while one was open for 6% of the time, Pallas kernels for 22%

profile of v4, /device:TPU:0, one launch (start us, length us, event | category | flops | bytes accessed | tf_op | source)
XLA Modules:
  0.0 159.5 jit_solution(965327559323339929)
XLA Ops:
  0.7 1.2 constant_dynamic-slice_fusion.2
  1.8 1.0 constant_dynamic-slice_fusion.3
  2.9 3.1 %collective-permute-start = (bf16[896,384]{1,0:T(8,128)(2,1)S(1)}, bf16[896,384]{1,0:T(8,128)(2,1)}, u32[]{:S(2)}, u32[]{:S(2)}) collective-permute-start(bf16[896,384]{1,0:T(8,128)(2,1)S(1)} %pad_maximum_fusion), channel_id=1, source_target_pairs={{0,4},{4,12},{12,8},{8,0},{1,5},{5,13},{13,9},{9,1},{2,6},{6,14},{... | collective-permute-start | bytes 2064392 | tf_op jit(solution)/shard_map/ppermute | solution.py:569
  6.6 3.0 %shard_map.157 = (f32[512,128]{1,0:T(8,128)}, f32[512,128]{1,0:T(8,128)}, s32[512,1]{1,0:T(8,128)}, s32[1,512]{1,0:T(1,128)}, bf16[32,512]{1,0:T(8,128)(2,1)}, /...) custom-call(f32[1,128]{1,0:T(1,128)} %constant.33.freq, s32[1,32]{1,0:T(1,128)} %lengths.1, s32[1,32]{1,0:T(1,128)} %ids.1, ...), custom_call_target="tpu_custom_call" | custom-call | flops 4194304 | bytes 524288 | tf_op jit(solution)/shard_map/pallas_call | solution.py:234
  9.6 1.2 fusion.8.sc
  10.8 6.5 %shard_map.158 = (bf16[512,896]{1,0:T(8,128)(2,1)}, bf16[512,896]{1,0:T(8,128)(2,1)}, bf16[512,896]{1,0:T(8,128)(2,1)}, bf16[512,896]{1,0:T(8,128)(2,1)}, bf16[512,896]{1,0:T(8,128)(2,1)}, /*index=5*/f32[32,896]{1,0:T(8,128)}) custom-call(s32[13]{0:T(128)} %fusion.8.sc, bf16[512,3584]{1,0:T(8,128)(2,1)} %hidden_ref.1, f32[1,3584]{1,0:T(1,128)} %broadcast_in_dim.27.gain_ref, ...), custom_call_target="tpu_custom_call" | custom-call | flops 14680064 | bytes 7340032 | tf_op jit(solution)/shard_map/pallas_call | solution.py:279
  17.3 5.3 %collective-permute-done.r1 = bf16[896,384]{1,0:T(8,128)(2,1)} collective-permute-done((bf16[896,384]{1,0:T(8,128)(2,1)S(1)}, bf16[896,384]{1,0:T(8,128)(2,1)}, u32[]{:S(2)}, u32[]{:S(2)}) %collective-permute-start) | collective-permute-done | bytes 688160 | tf_op jit(solution)/shard_map/ppermute | solution.py:569
  22.5 1.7 %collective-permute-start.1 = (bf16[896,384]{1,0:T(8,128)(2,1)S(1)}, bf16[896,384]{1,0:T(8,128)(2,1)S(1)}, u32[]{:S(2)}, u32[]{:S(2)}) collective-permute-start(bf16[896,384]{1,0:T(8,128)(2,1)S(1)} %pad_maximum_fusion), channel_id=1, source_target_pairs={{4,0},{12,4},{8,12},{0,8},{5,1},{13,5},{9,13},{1,9},{6,2},{14,6},{... | collective-permute-start | bytes 2064392 | tf_op jit(solution)/shard_map/ppermute | solution.py:569
  24.3 1.5 collective-permute-start.2
  25.8 13.4 %collective-permute-done.1.r3 = bf16[896,384]{1,0:T(8,128)(2,1)S(1)} collective-permute-done((bf16[896,384]{1,0:T(8,128)(2,1)S(1)}, bf16[896,384]{1,0:T(8,128)(2,1)S(1)}, u32[]{:S(2)}, u32[]{:S(2)}) %collective-permute-start.1) | collective-permute-done | bytes 688160 | tf_op jit(solution)/shard_map/ppermute | solution.py:569
  39.2 1.3 collective-permute-done.2.y1
  40.5 0.9 collective-permute-start.3
  41.4 1.5 collective-permute-start.4
  42.9 13.9 %collective-permute-done.3.r2 = bf16[896,384]{1,0:T(8,128)(2,1)} collective-permute-done((bf16[896,384]{1,0:T(8,128)(2,1)}, bf16[896,384]{1,0:T(8,128)(2,1)}, u32[]{:S(2)}, u32[]{:S(2)}) %collective-permute-start.3) | collective-permute-done | bytes 688160 | tf_op jit(solution)/shard_map/ppermute | solution.py:569
  56.8 1.5 collective-permute-start.5
  59.9 2.3 %collective-permute-start.9 = (bf16[256,512]{1,0:T(8,128)(2,1)}, bf16[256,512]{1,0:T(8,128)(2,1)S(1)}, u32[]{:S(2)}, u32[]{:S(2)}) collective-permute-start(bf16[256,512]{1,0:T(8,128)(2,1)} %constant_dynamic-slice_fusion), channel_id=1, source_target_pairs={{4,0},{12,4},{8,12},{0,8},{5,1},{13,5},{9,13},{1,9},{6,2},{14,6},{... | collective-permute-start | bytes 786440 | tf_op jit(solution)/shard_map/ppermute | solution.py:569
  62.1 8.0 %shard_map.159 = (f32[512,256]{1,0:T(8,128)}, f32[512,256]{1,0:T(8,128)}, f32[512,256]{1,0:T(8,128)}) custom-call(s32[13]{0:T(128)} %fusion.8.sc, bf16[512,896]{1,0:T(8,128)(2,1)} %get-tuple-element.44.b0, bf16[512,896]{1,0:T(8,128)(2,1)} %get-tuple-element.45.b1, bf16[512,896]{1,0:T(8,128)(2,1)} %get-tuple-element.46.b2, ...), custom_call_target="tpu_custom_call" | custom-call | flops 2818572288 | bytes 10059776 | tf_op jit(solution)/shard_map/pallas_call | solution.py:177
  70.2 1.1 collective-permute-done.8.own_a
  71.8 2.2 %collective-permute-done.9.own_b = bf16[256,512]{1,0:T(8,128)(2,1)S(1)} collective-permute-done((bf16[256,512]{1,0:T(8,128)(2,1)}, bf16[256,512]{1,0:T(8,128)(2,1)S(1)}, u32[]{:S(2)}, u32[]{:S(2)}) %collective-permute-start.9) | collective-permute-done | bytes 262176 | tf_op jit(solution)/shard_map/ppermute | solution.py:569
  74.3 1.8 %collective-permute-start.10 = (bf16[256,896]{1,0:T(8,128)(2,1)S(1)}, bf16[256,896]{1,0:T(8,128)(2,1)}, u32[]{:S(2)}, u32[]{:S(2)}) collective-permute-start(bf16[256,896]{1,0:T(8,128)(2,1)S(1)} %collective-permute-done.8.own_a), channel_id=1, source_target_pairs={{0,4},{4,12},{12,8},{8,0},{1,5},{5,13},{13,9},{9,1},{2,6},{6,14},{... | collective-permute-start | bytes 1376264 | tf_op jit(solution)/shard_map/ppermute | solution.py:569
  76.1 1.2 collective-permute-start.12
  77.8 3.0 %shard_map.160 = (bf16[512,256]{1,0:T(8,128)(2,1)}, bf16[512,128]{1,0:T(8,128)(2,1)}, bf16[512,128]{1,0:T(8,128)(2,1)}) custom-call(s32[13]{0:T(128)} %fusion.8.sc, f32[512,256]{1,0:T(8,128)} %get-tuple-element.53.kv_ref, bf16[512,896]{1,0:T(8,128)(2,1)} %get-tuple-element.46.b2, bf16[896,384]{1,0:T(8,128)(2,1)} %collective-permute-done.5.y2, ...), custom_call_target="tpu_custom_call" | custom-call | flops 58720256 | bytes 3180544 | tf_op jit(solution)/shard_map/pallas_call | solution.py:177
  80.9 1.9 %collective-permute-start.6 = (bf16[512,128]{1,0:T(8,128)(2,1)}, bf16[512,128]{1,0:T(8,128)(2,1)S(1)}, u32[]{:S(2)}, u32[]{:S(2)}) collective-permute-start(bf16[512,128]{1,0:T(8,128)(2,1)} %get-tuple-element.56), channel_id=1, source_target_pairs={{2,0},{0,1},{1,2},{6,4},{4,5},{5,6},{10,8},{8,9},{9,10},{14,12},{1... | collective-permute-start | bytes 393224 | tf_op jit(solution)/shard_map/ppermute | solution.py:609
  83.5 4.5 %collective-permute-done.6.x1 = bf16[512,128]{1,0:T(8,128)(2,1)S(1)} collective-permute-done((bf16[512,128]{1,0:T(8,128)(2,1)}, bf16[512,128]{1,0:T(8,128)(2,1)S(1)}, u32[]{:S(2)}, u32[]{:S(2)}) %collective-permute-start.6) | collective-permute-done | bytes 131104 | tf_op jit(solution)/shard_map/ppermute | solution.py:609
  87.9 2.9 %collective-permute-done.12.own_c = bf16[256,384]{1,0:T(8,128)(2,1)S(1)} collective-permute-done((bf16[256,384]{1,0:T(8,128)(2,1)S(1)}, bf16[256,384]{1,0:T(8,128)(2,1)S(1)}, u32[]{:S(2)}, u32[]{:S(2)}) %collective-permute-start.12) | collective-permute-done | bytes 196640 | tf_op jit(solution)/shard_map/ppermute | solution.py:569
  93.0 8.6 %shard_map.161 = (bf16[512,512]{1,0:T(8,128)(2,1)}, bf16[32,512]{1,0:T(8,128)(2,1)}) custom-call(s32[13]{0:T(128)} %fusion.8.sc, f32[512,256]{1,0:T(8,128)} %get-tuple-element.51.own_ref, f32[512,256]{1,0:T(8,128)} %get-tuple-element.52.oth_ref, bf16[512,896]{1,0:T(8,128)(2,1)} %get-tuple-element.46.b2, bf16[896,384]{1,0:T(8,128)(2,1)} %collective-permute-done.5.y2, ...), custom_call_target="tpu_custom_call" | custom-call | flops 536870912 | bytes 8388608 | tf_op jit(solution)/shard_map/pallas_call | solution.py:398
  101.6 3.4 %collective-permute-done.13.oth_b = bf16[256,896]{1,0:T(8,128)(2,1)S(1)} collective-permute-done((bf16[256,896]{1,0:T(8,128)(2,1)}, bf16[256,896]{1,0:T(8,128)(2,1)S(1)}, u32[]{:S(2)}, u32[]{:S(2)}) %collective-permute-start.13) | collective-permute-done | bytes 458784 | tf_op jit(solution)/shard_map/ppermute | solution.py:574
  105.0 1.0 copy-done.8
  106.0 3.4 %shard_map.162 = (bf16[512,896]{1,0:T(8,128)(2,1)}, bf16[512,896]{1,0:T(8,128)(2,1)S(1)}) custom-call(s32[13]{0:T(128)S(1)} %copy-done.7, bf16[512,512]{1,0:T(8,128)(2,1)S(1)} %copy-done.8, bf16[512,896]{1,0:T(8,128)(2,1)S(1)} %copy-done.1, bf16[256,896]{1,0:T(8,128)(2,1)} %collective-permute-done.10.own_b, bf16[256,896]{1,0:T(8,128)(2,1)S(1)} %collective-permute-done.13.oth_b), custom_call_target="tpu_custom_call" | custom-call | flops 939524096 | bytes 4194304 | tf_op jit(solution)/shard_map/pallas_call | solution.py:177
  109.5 0.9 copy-done.4
  110.6 2.3 %collective-permute-start.20 = (bf16[32,512]{1,0:T(8,128)(2,1)}, bf16[32,512]{1,0:T(8,128)(2,1)}, u32[]{:S(2)}, u32[]{:S(2)}) collective-permute-start(bf16[32,512]{1,0:T(8,128)(2,1)} %get-tuple-element.75), channel_id=1, source_target_pairs={{12,0},{8,4},{4,8},{0,12},{13,1},{9,5},{5,9},{1,13},{14,2},{10,6},... | collective-permute-start | bytes 98312 | tf_op jit(solution)/shard_map/ppermute | solution.py:661
  112.9 1.9 %collective-permute-start.21 = (bf16[32,512]{1,0:T(8,128)(2,1)}, bf16[32,512]{1,0:T(8,128)(2,1)}, u32[]{:S(2)}, u32[]{:S(2)}) collective-permute-start(bf16[32,512]{1,0:T(8,128)(2,1)} %get-tuple-element.75), channel_id=1, source_target_pairs={{4,0},{12,4},{0,8},{8,12},{5,1},{13,5},{1,9},{9,13},{6,2},{14,6},{... | collective-permute-start | bytes 98312 | tf_op jit(solution)/shard_map/ppermute | solution.py:661
  115.5 1.3 collective-permute-start.17
  117.1 0.8 add_convert_fusion.1
  118.0 1.2 copy-done.5
  119.2 2.4 %shard_map.163.ta = bf16[512,896]{1,0:T(8,128)(2,1)} custom-call(s32[13]{0:T(128)S(1)} %copy-done.7, bf16[512,896]{1,0:T(8,128)(2,1)S(1)} %copy-done.5, bf16[512,896]{1,0:T(8,128)(2,1)} %collective-permute-done.14.came), custom_call_target="tpu_custom_call" | custom-call | flops 458752 | bytes 2752512 | tf_op jit(solution)/shard_map/pallas_call | solution.py:177
  121.6 1.4 collective-permute-start.15
  123.0 1.0 collective-permute-done.16.oth_b
  124.0 2.9 %collective-permute-done.17.oth_c = bf16[256,384]{1,0:T(8,128)(2,1)S(1)} collective-permute-done((bf16[256,384]{1,0:T(8,128)(2,1)}, bf16[256,384]{1,0:T(8,128)(2,1)S(1)}, u32[]{:S(2)}, u32[]{:S(2)}) %collective-permute-start.17) | collective-permute-done | bytes 196640 | tf_op jit(solution)/shard_map/ppermute | solution.py:574
  126.9 3.2 %shard_map.164 = (bf16[512,896]{1,0:T(8,128)(2,1)}, bf16[512,896]{1,0:T(8,128)(2,1)S(1)}) custom-call(s32[13]{0:T(128)S(1)} %copy-done.7, bf16[512,512]{1,0:T(8,128)(2,1)S(1)} %copy-done.9, bf16[256,896]{1,0:T(8,128)(2,1)S(1)} %copy-done.11, bf16[256,896]{1,0:T(8,128)(2,1)} %collective-permute-done.11.oth_a, ...), custom_call_target="tpu_custom_call" | custom-call | flops 939524096 | bytes 4194304 | tf_op jit(solution)/shard_map/pallas_call | solution.py:177
  131.0 0.9 reduce.1
  132.8 0.8 convert_reduce_fusion
  133.7 4.7 %collective-permute-done.23 = bf16[32,896]{1,0:T(8,128)(2,1)S(1)} collective-permute-done((bf16[32,896]{1,0:T(8,128)(2,1)S(1)}, bf16[32,896]{1,0:T(8,128)(2,1)S(1)}, u32[]{:S(2)}, u32[]{:S(2)}) %collective-permute-start.23) | collective-permute-done | bytes 57376 | tf_op jit(solution)/shard_map/ppermute | solution.py:668
  138.4 1.5 convolution_convert_fusion
  140.0 1.5 shard_map.165.tb
  141.4 1.5 collective-permute-start.24
  143.1 12.3 %all_to_all.5 = bf16[16,8,384]{2,1,0:T(8,128)(2,1)S(1)} all-to-all(bf16[16,8,384]{2,1,0:T(8,128)(2,1)S(1)} %bitcast.13), channel_id=1, replica_groups=mesh['groups'=2,'dp'=4,'tp'=4] {'dp','tp'}, dimensions={0} | all-to-all | bytes 196608 | tf_op jit(solution)/shard_map/all_to_all | solution.py:689
  156.7 2.7 %shard_map.166 = bf16[512,896]{1,0:T(8,128)(2,1)} custom-call(s32[13]{0:T(128)S(1)} %copy-done.7, bf16[512,896]{1,0:T(8,128)(2,1)S(1)} %copy-done.6, bf16[512,896]{1,0:T(8,128)(2,1)} %shard_map.163.ta, bf16[512,896]{1,0:T(8,128)(2,1)} %collective-permute-done.15.ca, bf16[512,896]{1,0:T(8,128)(2,1)S(1)} %shard_map.165.tb, ...), custom_call_target="tpu_custom_call" | custom-call | flops 458752 | bytes 5505024 | tf_op jit(solution)/shard_map/pallas_call | solution.py:177
  (86 shorter events, 11.1 us)
Async XLA Ops:
  0.6 137.8 %copy-start = (bf16[896,1024]{1,0:T(8,128)(2,1)S(1)}, bf16[896,1024]{1,0:T(8,128)(2,1)}, u32[]{:S(2)}) copy-start(bf16[896,1024]{1,0:T(8,128)(2,1)} %param.24) | copy-start | bytes 5505028
  0.6 5.3 %copy-start.17 = (f32[3584]{0:T(1024)S(1)}, f32[3584]{0:T(1024)}, u32[]{:S(2)}) copy-start(f32[3584]{0:T(1024)} %param.18) | copy-start | bytes 43012
  2.9 19.6 %collective-permute-start = (bf16[896,384]{1,0:T(8,128)(2,1)S(1)}, bf16[896,384]{1,0:T(8,128)(2,1)}, u32[]{:S(2)}, u32[]{:S(2)}) collective-permute-start(bf16[896,384]{1,0:T(8,128)(2,1)S(1)} %pad_maximum_fusion), channel_id=1, source_target_pairs={{0,4},{4,12},{12,8},{8,0},{1,5},{5,13},{13,9},{9,1},{2,6},{6,14},{... | collective-permute-start | bytes 2064392 | tf_op jit(solution)/shard_map/ppermute | solution.py:569
  10.8 47.6 %copy-start.1 = (bf16[512,896]{1,0:T(8,128)(2,1)S(1)}, bf16[512,896]{1,0:T(8,128)(2,1)}, u32[]{:S(2)}) copy-start(bf16[512,896]{1,0:T(8,128)(2,1)} %w.1) | copy-start | bytes 2752516
  22.5 16.6 %collective-permute-start.1 = (bf16[896,384]{1,0:T(8,128)(2,1)S(1)}, bf16[896,384]{1,0:T(8,128)(2,1)S(1)}, u32[]{:S(2)}, u32[]{:S(2)}) collective-permute-start(bf16[896,384]{1,0:T(8,128)(2,1)S(1)} %pad_maximum_fusion), channel_id=1, source_target_pairs={{4,0},{12,4},{8,12},{0,8},{5,1},{13,5},{9,13},{1,9},{6,2},{14,6},{... | collective-permute-start | bytes 2064392 | tf_op jit(solution)/shard_map/ppermute | solution.py:569
  24.3 16.2 %collective-permute-start.2 = (bf16[896,384]{1,0:T(8,128)(2,1)}, bf16[896,384]{1,0:T(8,128)(2,1)S(1)}, u32[]{:S(2)}, u32[]{:S(2)}) collective-permute-start(bf16[896,384]{1,0:T(8,128)(2,1)} %collective-permute-done.r1), channel_id=1, source_target_pairs={{0,16},{16,0},{1,17},{17,1},{2,18},{18,2},{3,19},{19,3},{4,20},{20... | collective-permute-start | bytes 2064392 | tf_op jit(solution)/shard_map/ppermute | solution.py:574
  39.2 23.0 %copy-start.21 = (bf16[896,384]{1,0:T(8,128)(2,1)}, bf16[896,384]{1,0:T(8,128)(2,1)S(1)}, u32[]{:S(2)}) copy-start(bf16[896,384]{1,0:T(8,128)(2,1)S(1)} %collective-permute-done.1.r3) | copy-start | bytes 2064388
  40.5 16.3 %copy-start.22 = (bf16[896,384]{1,0:T(8,128)(2,1)}, bf16[896,384]{1,0:T(8,128)(2,1)S(1)}, u32[]{:S(2)}) copy-start(bf16[896,384]{1,0:T(8,128)(2,1)S(1)} %collective-permute-done.2.y1) | copy-start | bytes 2064388
  40.5 16.3 %collective-permute-start.3 = (bf16[896,384]{1,0:T(8,128)(2,1)}, bf16[896,384]{1,0:T(8,128)(2,1)}, u32[]{:S(2)}, u32[]{:S(2)}) collective-permute-start(bf16[896,384]{1,0:T(8,128)(2,1)} %collective-permute-done.r1), channel_id=1, source_target_pairs={{0,4},{4,12},{12,8},{8,0},{1,5},{5,13},{13,9},{9,1},{2,6},{6,14},{... | collective-permute-start | bytes 2064392 | tf_op jit(solution)/shard_map/ppermute | solution.py:569
  41.4 17.0 %collective-permute-start.4 = (bf16[896,384]{1,0:T(8,128)(2,1)S(1)}, bf16[896,384]{1,0:T(8,128)(2,1)S(1)}, u32[]{:S(2)}, u32[]{:S(2)}) collective-permute-start(bf16[896,384]{1,0:T(8,128)(2,1)S(1)} %collective-permute-done.1.r3), channel_id=1, source_target_pairs={{0,16},{16,0},{1,17},{17,1},{2,18},{18,2},{3,19},{19,3},{4,20},{20... | collective-permute-start | bytes 2064392 | tf_op jit(solution)/shard_map/ppermute | solution.py:574
  56.8 17.4 %collective-permute-start.5 = (bf16[896,384]{1,0:T(8,128)(2,1)}, bf16[896,384]{1,0:T(8,128)(2,1)}, u32[]{:S(2)}, u32[]{:S(2)}) collective-permute-start(bf16[896,384]{1,0:T(8,128)(2,1)} %collective-permute-done.3.r2), channel_id=1, source_target_pairs={{0,16},{16,0},{1,17},{17,1},{2,18},{18,2},{3,19},{19,3},{4,20},{20... | collective-permute-start | bytes 2064392 | tf_op jit(solution)/shard_map/ppermute | solution.py:574
  58.4 3.7 %copy-start.23 = (bf16[896,384]{1,0:T(8,128)(2,1)}, bf16[896,384]{1,0:T(8,128)(2,1)S(1)}, u32[]{:S(2)}) copy-start(bf16[896,384]{1,0:T(8,128)(2,1)S(1)} %collective-permute-done.4.y3) | copy-start | bytes 2064388
  58.4 12.8 %collective-permute-start.8 = (bf16[256,896]{1,0:T(8,128)(2,1)S(1)}, bf16[256,896]{1,0:T(8,128)(2,1)S(1)}, u32[]{:S(2)}, u32[]{:S(2)}) collective-permute-start(bf16[256,896]{1,0:T(8,128)(2,1)S(1)} %constant_dynamic-slice_fusion.1), channel_id=1, source_target_pairs={{0,4},{4,12},{12,8},{8,0},{1,5},{5,13},{13,9},{9,1},{2,6},{6,14},{... | collective-permute-start | bytes 1376264 | tf_op jit(solution)/shard_map/ppermute | solution.py:569
  59.9 14.1 %collective-permute-start.9 = (bf16[256,512]{1,0:T(8,128)(2,1)}, bf16[256,512]{1,0:T(8,128)(2,1)S(1)}, u32[]{:S(2)}, u32[]{:S(2)}) collective-permute-start(bf16[256,512]{1,0:T(8,128)(2,1)} %constant_dynamic-slice_fusion), channel_id=1, source_target_pairs={{4,0},{12,4},{8,12},{0,8},{5,1},{13,5},{9,13},{1,9},{6,2},{14,6},{... | collective-permute-start | bytes 786440 | tf_op jit(solution)/shard_map/ppermute | solution.py:569
  62.1 15.1 %copy-start.19 = (bf16[1024]{0:T(1024)(128)(2,1)S(1)}, bf16[1024]{0:T(1024)(128)(2,1)}, u32[]{:S(2)}) copy-start(bf16[1024]{0:T(1024)(128)(2,1)} %param.22) | copy-start | bytes 6148
  70.2 22.3 %copy-start.20 = (bf16[512]{0:T(512)(128)(2,1)S(1)}, bf16[512]{0:T(512)(128)(2,1)}, u32[]{:S(2)}) copy-start(bf16[512]{0:T(512)(128)(2,1)} %param.20) | copy-start | bytes 3076
  71.3 21.8 %copy-start.10 = (bf16[256,896]{1,0:T(8,128)(2,1)}, bf16[256,896]{1,0:T(8,128)(2,1)S(1)}, u32[]{:S(2)}) copy-start(bf16[256,896]{1,0:T(8,128)(2,1)S(1)} %collective-permute-done.8.own_a) | copy-start | bytes 1376260
  71.3 19.6 %collective-permute-start.11 = (bf16[256,896]{1,0:T(8,128)(2,1)S(1)}, bf16[256,896]{1,0:T(8,128)(2,1)}, u32[]{:S(2)}, u32[]{:S(2)}) collective-permute-start(bf16[256,896]{1,0:T(8,128)(2,1)S(1)} %collective-permute-done.8.own_a), channel_id=1, source_target_pairs={{0,16},{16,0},{1,17},{17,1},{2,18},{18,2},{3,19},{19,3},{4,20},{20... | collective-permute-start | bytes 1376264 | tf_op jit(solution)/shard_map/ppermute | solution.py:574
  74.3 17.5 %collective-permute-start.10 = (bf16[256,896]{1,0:T(8,128)(2,1)S(1)}, bf16[256,896]{1,0:T(8,128)(2,1)}, u32[]{:S(2)}, u32[]{:S(2)}) collective-permute-start(bf16[256,896]{1,0:T(8,128)(2,1)S(1)} %collective-permute-done.8.own_a), channel_id=1, source_target_pairs={{0,4},{4,12},{12,8},{8,0},{1,5},{5,13},{13,9},{9,1},{2,6},{6,14},{... | collective-permute-start | bytes 1376264 | tf_op jit(solution)/shard_map/ppermute | solution.py:569
  76.1 14.8 %collective-permute-start.12 = (bf16[256,384]{1,0:T(8,128)(2,1)S(1)}, bf16[256,384]{1,0:T(8,128)(2,1)S(1)}, u32[]{:S(2)}, u32[]{:S(2)}) collective-permute-start(bf16[256,384]{1,0:T(8,128)(2,1)S(1)} %dynamic-slice.1), channel_id=1, source_target_pairs={{4,0},{12,4},{8,12},{0,8},{5,1},{13,5},{9,13},{1,9},{6,2},{14,6},{... | collective-permute-start | bytes 589832 | tf_op jit(solution)/shard_map/ppermute | solution.py:569
  80.9 7.1 %collective-permute-start.6 = (bf16[512,128]{1,0:T(8,128)(2,1)}, bf16[512,128]{1,0:T(8,128)(2,1)S(1)}, u32[]{:S(2)}, u32[]{:S(2)}) collective-permute-start(bf16[512,128]{1,0:T(8,128)(2,1)} %get-tuple-element.56), channel_id=1, source_target_pairs={{2,0},{0,1},{1,2},{6,4},{4,5},{5,6},{10,8},{8,9},{9,10},{14,12},{1... | collective-permute-start | bytes 393224 | tf_op jit(solution)/shard_map/ppermute | solution.py:609
  82.8 5.1 %collective-permute-start.7 = (bf16[512,128]{1,0:T(8,128)(2,1)}, bf16[512,128]{1,0:T(8,128)(2,1)S(1)}, u32[]{:S(2)}, u32[]{:S(2)}) collective-permute-start(bf16[512,128]{1,0:T(8,128)(2,1)} %get-tuple-element.57), channel_id=1, source_target_pairs={{2,1},{3,2},{1,3},{6,5},{7,6},{5,7},{10,9},{11,10},{9,11},{14,13},... | collective-permute-start | bytes 393224 | tf_op jit(solution)/shard_map/ppermute | solution.py:609
  87.9 2.9 %copy-start.14 = (bf16[512,128]{1,0:T(8,128)(2,1)}, bf16[512,128]{1,0:T(8,128)(2,1)S(1)}, u32[]{:S(2)}) copy-start(bf16[512,128]{1,0:T(8,128)(2,1)S(1)} %collective-permute-done.6.x1) | copy-start | bytes 393220
  87.9 3.9 %copy-start.15 = (bf16[512,128]{1,0:T(8,128)(2,1)}, bf16[512,128]{1,0:T(8,128)(2,1)S(1)}, u32[]{:S(2)}) copy-start(bf16[512,128]{1,0:T(8,128)(2,1)S(1)} %collective-permute-done.7.x2) | copy-start | bytes 393220
  91.8 13.2 %collective-permute-start.13 = (bf16[256,896]{1,0:T(8,128)(2,1)}, bf16[256,896]{1,0:T(8,128)(2,1)S(1)}, u32[]{:S(2)}, u32[]{:S(2)}) collective-permute-start(bf16[256,896]{1,0:T(8,128)(2,1)} %collective-permute-done.10.own_b), channel_id=1, source_target_pairs={{0,16},{16,0},{1,17},{17,1},{2,18},{18,2},{3,19},{19,3},{4,20},{20... | collective-permute-start | bytes 1376264 | tf_op jit(solution)/shard_map/ppermute | solution.py:574
  93.0 12.0 %copy-start.7 = (s32[13]{0:T(128)S(1)}, s32[13]{0:T(128)}, u32[]{:S(2)}) copy-start(s32[13]{0:T(128)} %fusion.8.sc) | copy-start | bytes 160
  105.0 1.0 copy-start.8
  106.0 20.8 %copy-start.9 = (bf16[512,512]{1,0:T(8,128)(2,1)S(1)}, bf16[512,512]{1,0:T(8,128)(2,1)}, u32[]{:S(2)}) copy-start(bf16[512,512]{1,0:T(8,128)(2,1)} %get-tuple-element.70.attn) | copy-start | bytes 1572868
  109.5 0.9 copy-start.4
  110.4 7.6 %collective-permute-start.14 = (bf16[512,896]{1,0:T(8,128)(2,1)}, bf16[512,896]{1,0:T(8,128)(2,1)}, u32[]{:S(2)}, u32[]{:S(2)}) collective-permute-start(bf16[512,896]{1,0:T(8,128)(2,1)} %get-tuple-element.69), channel_id=1, source_target_pairs={{0,1},{1,0},{2,3},{3,2},{4,5},{5,4},{6,7},{7,6},{8,9},{9,8},{10,11... | collective-permute-start | bytes 2752520 | tf_op jit(solution)/shard_map/ppermute | solution.py:639
  110.4 5.1 %collective-permute-start.19 = (bf16[32,512]{1,0:T(8,128)(2,1)}, bf16[32,512]{1,0:T(8,128)(2,1)}, u32[]{:S(2)}, u32[]{:S(2)}) collective-permute-start(bf16[32,512]{1,0:T(8,128)(2,1)} %get-tuple-element.75), channel_id=1, source_target_pairs={{8,0},{0,4},{12,8},{4,12},{9,1},{1,5},{13,9},{5,13},{10,2},{2,6},{... | collective-permute-start | bytes 98312 | tf_op jit(solution)/shard_map/ppermute | solution.py:661
  110.6 6.2 %collective-permute-start.20 = (bf16[32,512]{1,0:T(8,128)(2,1)}, bf16[32,512]{1,0:T(8,128)(2,1)}, u32[]{:S(2)}, u32[]{:S(2)}) collective-permute-start(bf16[32,512]{1,0:T(8,128)(2,1)} %get-tuple-element.75), channel_id=1, source_target_pairs={{12,0},{8,4},{4,8},{0,12},{13,1},{9,5},{5,9},{1,13},{14,2},{10,6},... | collective-permute-start | bytes 98312 | tf_op jit(solution)/shard_map/ppermute | solution.py:661
  112.9 4.2 %collective-permute-start.21 = (bf16[32,512]{1,0:T(8,128)(2,1)}, bf16[32,512]{1,0:T(8,128)(2,1)}, u32[]{:S(2)}, u32[]{:S(2)}) collective-permute-start(bf16[32,512]{1,0:T(8,128)(2,1)} %get-tuple-element.75), channel_id=1, source_target_pairs={{4,0},{12,4},{0,8},{8,12},{5,1},{13,5},{1,9},{9,13},{6,2},{14,6},{... | collective-permute-start | bytes 98312 | tf_op jit(solution)/shard_map/ppermute | solution.py:661
  114.8 12.1 %copy-start.13 = (bf16[256,384]{1,0:T(8,128)(2,1)S(1)}, bf16[256,384]{1,0:T(8,128)(2,1)}, u32[]{:S(2)}) copy-start(bf16[256,384]{1,0:T(8,128)(2,1)} %copy-done.12) | copy-start | bytes 589828
  114.8 9.2 %collective-permute-start.16 = (bf16[256,512]{1,0:T(8,128)(2,1)S(1)}, bf16[256,512]{1,0:T(8,128)(2,1)S(1)}, u32[]{:S(2)}, u32[]{:S(2)}) collective-permute-start(bf16[256,512]{1,0:T(8,128)(2,1)S(1)} %collective-permute-done.9.own_b), channel_id=1, source_target_pairs={{0,16},{16,0},{1,17},{17,1},{2,18},{18,2},{3,19},{19,3},{4,20},{20... | collective-permute-start | bytes 786440 | tf_op jit(solution)/shard_map/ppermute | solution.py:574
  115.5 11.3 %collective-permute-start.17 = (bf16[256,384]{1,0:T(8,128)(2,1)}, bf16[256,384]{1,0:T(8,128)(2,1)S(1)}, u32[]{:S(2)}, u32[]{:S(2)}) collective-permute-start(bf16[256,384]{1,0:T(8,128)(2,1)} %copy-done.12), channel_id=1, source_target_pairs={{0,16},{16,0},{1,17},{17,1},{2,18},{18,2},{3,19},{19,3},{4,20},{20... | collective-permute-start | bytes 589832 | tf_op jit(solution)/shard_map/ppermute | solution.py:574
  118.0 1.2 copy-start.5
  119.2 7.7 %copy-start.11 = (bf16[256,896]{1,0:T(8,128)(2,1)S(1)}, bf16[256,896]{1,0:T(8,128)(2,1)}, u32[]{:S(2)}) copy-start(bf16[256,896]{1,0:T(8,128)(2,1)} %copy-done.10) | copy-start | bytes 1376260
  121.6 16.9 %copy-start.16 = (bf16[32,32]{1,0:T(8,128)(2,1)S(1)}, bf16[32,32]{1,0:T(8,128)(2,1)}, u32[]{:S(2)}) copy-start(bf16[32,32]{1,0:T(8,128)(2,1)} %get-tuple-element.61.hits_ref) | copy-start | bytes 6148
  121.6 18.4 %collective-permute-start.15 = (bf16[512,896]{1,0:T(8,128)(2,1)}, bf16[512,896]{1,0:T(8,128)(2,1)}, u32[]{:S(2)}, u32[]{:S(2)}) collective-permute-start(bf16[512,896]{1,0:T(8,128)(2,1)} %shard_map.163.ta), channel_id=1, source_target_pairs={{2,0},{1,3},{7,5},{4,6},{8,10},{11,9},{13,15},{14,12},{18,16},{17,... | collective-permute-start | bytes 2752520 | tf_op jit(solution)/shard_map/ppermute | solution.py:649
  130.1 0.9 copy-start.2
  130.1 9.8 %collective-permute-start.18 = (bf16[512,896]{1,0:T(8,128)(2,1)}, bf16[512,896]{1,0:T(8,128)(2,1)}, u32[]{:S(2)}, u32[]{:S(2)}) collective-permute-start(bf16[512,896]{1,0:T(8,128)(2,1)} %get-tuple-element.73), channel_id=1, source_target_pairs={{0,1},{1,0},{2,3},{3,2},{4,5},{5,4},{6,7},{7,6},{8,9},{9,8},{10,11... | collective-permute-start | bytes 2752520 | tf_op jit(solution)/shard_map/ppermute | solution.py:639
  131.0 1.6 %collective-permute-start.22 = (bf16[32,896]{1,0:T(8,128)(2,1)S(1)}, bf16[32,896]{1,0:T(8,128)(2,1)S(1)}, u32[]{:S(2)}, u32[]{:S(2)}) collective-permute-start(bf16[32,896]{1,0:T(8,128)(2,1)S(1)} %convolution_convert_fusion.1), channel_id=1, source_target_pairs={{0,1},{1,0},{2,3},{3,2},{4,5},{5,4},{6,7},{7,6},{8,9},{9,8},{10,11... | collective-permute-start | bytes 172040 | tf_op jit(solution)/shard_map/ppermute | solution.py:666
  131.0 8.9 %copy-start.3 = (bf16[512,896]{1,0:T(8,128)(2,1)S(1)}, bf16[512,896]{1,0:T(8,128)(2,1)}, u32[]{:S(2)}) copy-start(bf16[512,896]{1,0:T(8,128)(2,1)} %copy-done.2) | copy-start | bytes 2752516
  132.7 5.7 %collective-permute-start.23 = (bf16[32,896]{1,0:T(8,128)(2,1)S(1)}, bf16[32,896]{1,0:T(8,128)(2,1)S(1)}, u32[]{:S(2)}, u32[]{:S(2)}) collective-permute-start(bf16[32,896]{1,0:T(8,128)(2,1)S(1)} %get-tuple-element.81), channel_id=1, source_target_pairs={{0,2},{1,3},{2,0},{3,1},{4,6},{5,7},{6,4},{7,5},{8,10},{9,11},{10,... | collective-permute-start | bytes 172040 | tf_op jit(solution)/shard_map/ppermute | solution.py:668
  139.9 16.2 %copy-start.18 = (f32[8,256]{1,0:T(8,128)S(1)}, f32[8,256]{1,0:T(8,128)}, u32[]{:S(2)}) copy-start(f32[8,256]{1,0:T(8,128)} %param.25) | copy-start | bytes 24580
  139.9 16.8 %copy-start.6 = (bf16[512,896]{1,0:T(8,128)(2,1)S(1)}, bf16[512,896]{1,0:T(8,128)(2,1)}, u32[]{:S(2)}) copy-start(bf16[512,896]{1,0:T(8,128)(2,1)} %get-tuple-element.43.own) | copy-start | bytes 2752516
  141.4 15.3 %collective-permute-start.24 = (bf16[512,896]{1,0:T(8,128)(2,1)S(1)}, bf16[512,896]{1,0:T(8,128)(2,1)S(1)}, u32[]{:S(2)}, u32[]{:S(2)}) collective-permute-start(bf16[512,896]{1,0:T(8,128)(2,1)S(1)} %shard_map.165.tb), channel_id=1, source_target_pairs={{0,2},{3,1},{6,4},{5,7},{9,11},{10,8},{15,13},{12,14},{16,18},{19,... | collective-permute-start | bytes 2752520 | tf_op jit(solution)/shard_map/ppermute | solution.py:649
  (1 other events, 0.7 us)

commit v5 on v4

--- a/solution.py
+++ b/solution.py
@@ -157,7 +157,7 @@
 VMEM = pl.BlockSpec(memory_space=pltpu.VMEM)
 SMEM = pl.BlockSpec(memory_space=pltpu.SMEM)
 T, GROUP, KEEP_0, KEEP_1, MINE_A, KEY_FROM, VALUE_FROM, SEND_1, SEND_2 = range(4, 13)
-TAIL = 20
+TAIL = 60
 
 
 def dot(a, b):
@@ -432,7 +432,7 @@
         project(attn, first, sent)
 
 
-def project_own_kernel(sc, attn, w, own_b, oth_b, sent, kept):
+def project_own_kernel(sc, attn, lists, w, own_b, oth_b, sent, kept, list_sent, list_kept):
     half = attn.shape[1] // 2
     g = sc[GROUP]
 
@@ -444,18 +444,18 @@
             )
         ]
 
-    project_two(sc[KEEP_0], attn, stored, lambda: [(own_b[...], oth_b[...])], sent, kept)
-
-
-def project_kernel(sc, attn, own_a, oth_a, own_b, oth_b, own_c, oth_c, sent, kept):
-    project_two(
-        sc[KEEP_1],
-        attn,
-        lambda: [(own_a[...], oth_a[...])],
-        lambda: [(own_b[...], oth_b[...]), (own_c[...], oth_c[...])],
-        sent,
-        kept,
-    )
+    second = lambda: [(own_b[...], oth_b[...])]
+    project_two(sc[KEEP_0], attn, stored, second, sent, kept)
+    project_two(sc[KEEP_0], lists, stored, second, list_sent, list_kept)
+
+
+def project_kernel(
+    sc, attn, lists, own_a, oth_a, own_b, oth_b, own_c, oth_c, sent, kept, list_sent, list_kept
+):
+    first = lambda: [(own_a[...], oth_a[...])]
+    second = lambda: [(own_b[...], oth_b[...]), (own_c[...], oth_c[...])]
+    project_two(sc[KEEP_1], attn, first, second, sent, kept)
+    project_two(sc[KEEP_1], lists, first, second, list_sent, list_kept)
 
 
 def add_kernel(sc, kept, came, total):
@@ -607,10 +607,10 @@
         sine,
     )
     kv_came = [lax.ppermute(x, "tp", pairs) for x, pairs in zip(kv_sent, rounds)]
-    run_stage(4, sum_own, swap_ties=[*kv_came, swapped["o1"]])
+    run_stage(4, sum_own, swap_ties=[*kv_came, swapped["o1"], swapped["a3"]])
     attn, attn_lists = attend(
         scalars,
-        sum_own,
+        after(sum_own, ring_of["b3"], ring_of["o2"]),
         sum_oth,
         blocks[2],
         swapped["q2"],
@@ -627,16 +627,17 @@
     )
 
     def project_pair(kernel, n, attn, *weights):
-        sent, kept = call(
+        sent, kept, *lists = call(
             kernel,
-            [shape((tokens, n), bf16)] * 2,
+            [shape((tokens, n), bf16)] * 2 + [shape((attn_lists.shape[0], n), bf16)] * 2,
             4 * tokens * q_half * 2 * n,
             scalars,
             attn,
+            attn_lists,
             *weights,
             vmem=TAIL,
         )
-        return sent, kept, lax.ppermute(sent, "tp", core)
+        return sent, kept, lax.ppermute(sent, "tp", core), lists
 
     def exchange(kept, came, m):
         (total,) = call(
@@ -651,28 +652,22 @@
     def both(key):
         return ring_of[key], swapped[key]
 
-    sent_a, kept_a, came_a = project_pair(project_own_kernel, share, attn, w_out, *both("o2"))
+    sent_a, kept_a, came_a, lists_a = project_pair(project_own_kernel, share, attn, w_out, *both("o2"))
     block_a = exchange(kept_a, came_a, 0)
 
-    attn_lists = after(attn_lists, ring_of["o2"], ring_of["b3"])
-    lists_sum = attn_lists.astype(f32)
-    for m in range(1, n_dp):
-        pairs = [(source_of[d][m], d) for d in range(n_dp)]
-        lists_sum = lists_sum + lax.ppermute(attn_lists, "dp", pairs).astype(f32)
-    lists_sum = lists_sum.astype(bf16)
-    first = jnp.where(g == 0, lists_sum[:, :q_half], lists_sum[:, q_half:])
-    second = jnp.where(g == 0, lists_sum[:, q_half:], lists_sum[:, :q_half])
-    plane = dot(jnp.concatenate([first, second], axis=1), w_out).astype(bf16)
-    plane = plane.astype(f32) + lax.ppermute(plane, "tp", core).astype(f32)
-    plane16 = plane.astype(bf16)
-    crossed = lax.ppermute(plane16, "tp", across)
-    sent_b, kept_b, came_b = project_pair(
-        project_kernel, share, after(attn, block_a[0]), *both("o1"), *both("a3"), *both("b3")
-    )
-    plane = after(plane, sent_b)
-    plane = plane + crossed.astype(f32)
-    plane = (jnp.where(t == z, plane, 0.0) + hidden_lists).astype(bf16)
-    vec_lists = dot(plane, w_pool).astype(bf16)
+    sent_b, kept_b, came_b, lists_b = project_pair(
+        project_kernel, share, after(attn, sent_a), *both("o1"), *both("a3"), *both("b3")
+    )
+
+    count = attn_lists.shape[0]
+    mine_a = scalars[MINE_A] == 1
+    list_came = lax.ppermute(jnp.concatenate([lists_a[0], lists_b[0]], axis=0), "tp", core)
+    list_a = lists_a[1].astype(f32) + list_came[:count].astype(f32)
+    list_b = lists_b[1].astype(f32) + list_came[count:].astype(f32)
+    list_give = jnp.where(mine_a, list_b, list_a).astype(bf16)
+    list_got = lax.ppermute(after(list_give, block_a[0]), "tp", across).astype(f32)
+    plane = jnp.where(mine_a, list_a, list_b) + list_got + hidden_lists
+    vec_lists = dot(plane.astype(bf16), w_pool).astype(bf16)
     lists_own, cols = centroids.shape
     late = vec_lists.reshape(n_dp, lists_own, n_tp, cols).transpose(0, 2, 1, 3)
     late = jnp.concatenate(
@@ -685,7 +680,7 @@
         ],
         axis=3,
     ).reshape(n_dp * n_tp, lists_own, cols + HD)
-    block_b = exchange(kept_b, after(came_b, vec_lists, block_a[1]), 1)
+    block_b = exchange(kept_b, after(came_b, block_a[0]), 1)
     late = lax.all_to_all(after(late, block_b[0]), ("dp", "tp"), split_axis=0, concat_axis=0, tiled=True)
     late = late.reshape(n_dp, n_tp, lists_own, cols + HD).astype(f32)
     totals = jnp.sum(late[..., :cols], axis=(0, 1))

time: 160 us -> 158 us (0.988)
  waiting for transfers between devices: 58.3 us -> 45.6 us
  Pallas kernels: 42.4 us -> 47.2 us
  starting transfers between devices: 29.2 us -> 33.3 us
  blocking collectives: 12.3 us -> 15.1 us
    ppermute x7 -> x4, waiting for transfers between devices: 5.9 us -> 0.01 us  [the longest x2 0.01 us: project_pair(): return (sent, kept, lax.ppermute(sent, 'tp', core), lists)]
    pallas_call x7, Pallas kernels: 24.3 us -> 29.2 us  [call(): pl.pallas_call(kernel, in_specs=[SMEM] + [VMEM] * len(args), out_specs=[V...]
    ppermute x2, starting transfers between devices: 2.92 us -> 6.91 us  [exchange(): return (total, lax.ppermute(total, ('dp', 'tp'), pairs))]
    ppermute x7, waiting for transfers between devices: 8.9 us -> 5.4 us  [run_stage(): swapped[key] = lax.ppermute(came, 'groups', swap)]
    all_to_all x1, blocking collectives: 12.3 us -> 15.1 us  [shards(): lax.all_to_all(after(late, block_b[0]), ('dp', 'tp'), split_axis=0, conca...]
    ppermute x2, waiting for transfers between devices: 4.47 us -> 2.41 us  [shards(): lax.ppermute(x, 'tp', pairs)]
    ppermute x7 -> x4, starting transfers between devices: 4.52 us -> 2.74 us  [the longest x2 1.17 us: project_pair(): return (sent, kept, lax.ppermute(sent, 'tp', core), lists)]
  transfers between devices with their start and end apart: 25 -> 22, of which waited for: 17 -> 11; matrix products, arithmetic and copies ran while one was open for 6% -> 5% of each run, Pallas kernels for 22% -> 28%
where the time goes in v5:
time: 158 us; the launch traced here: 157 us
  Pallas kernels  47.2 us (30%)
  waiting for transfers between devices  45.6 us (29%)
  starting transfers between devices  33.3 us (21%)
  blocking collectives  15.1 us (10%)
  local copies, waits for them, and re-layouts  10.1 us (6%)
  other arithmetic  3.36 us (2%)
    ppermute x7, waiting for transfers between devices, run_stage(): lax.ppermute(after(piece, *ties) if ties else piece, 'dp', pairs)  37.7 us
    pallas_call x7, Pallas kernels, call(): pl.pallas_call(kernel, in_specs=[SMEM] + [VMEM] * len(args), out_specs=[V...  29.2 us
    all_to_all x1, blocking collectives, shards(): lax.all_to_all(after(late, block_b[0]), ('dp', 'tp'), split_axis=0, conca...  15.1 us
    ppermute x7, starting transfers between devices, run_stage(): lax.ppermute(after(piece, *ties) if ties else piece, 'dp', pairs)  12.4 us
    ppermute x7, starting transfers between devices, run_stage(): swapped[key] = lax.ppermute(came, 'groups', swap)  8.61 us
    pallas_call x1, Pallas kernels, attend(): pl.pallas_call(attention_kernel, in_specs=[SMEM] + [VMEM] * (1 + len(rest...  8.56 us
    ppermute x2, starting transfers between devices, exchange(): return (total, lax.ppermute(total, ('dp', 'tp'), pairs))  6.91 us
    pallas_call x1, Pallas kernels, prepare(): pl.pallas_call(prep_kernel, grid_spec=pltpu.PrefetchScalarGridSpec(num_sc...  6.52 us
  transfers between devices with their start and end apart: 22, of which 11 were waited for; matrix products, arithmetic and copies ran while one was open for 5% of the time, Pallas kernels for 28%

profile of v5, /device:TPU:0, one launch (start us, length us, event | category | flops | bytes accessed | tf_op | source)
XLA Modules:
  0.0 156.8 jit_solution(11167385311686920837)
XLA Ops:
  0.7 1.2 constant_dynamic-slice_fusion.2
  1.8 1.0 constant_dynamic-slice_fusion.3
  2.9 3.1 %collective-permute-start = (bf16[896,384]{1,0:T(8,128)(2,1)S(1)}, bf16[896,384]{1,0:T(8,128)(2,1)}, u32[]{:S(2)}, u32[]{:S(2)}) collective-permute-start(bf16[896,384]{1,0:T(8,128)(2,1)S(1)} %pad_maximum_fusion), channel_id=1, source_target_pairs={{0,4},{4,12},{12,8},{8,0},{1,5},{5,13},{13,9},{9,1},{2,6},{6,14},{... | collective-permute-start | bytes 2064392 | tf_op jit(solution)/shard_map/ppermute | solution.py:569
  6.6 3.0 %shard_map.157 = (f32[512,128]{1,0:T(8,128)}, f32[512,128]{1,0:T(8,128)}, s32[512,1]{1,0:T(8,128)}, s32[1,512]{1,0:T(1,128)}, bf16[32,512]{1,0:T(8,128)(2,1)}, /...) custom-call(f32[1,128]{1,0:T(1,128)} %constant.36.freq, s32[1,32]{1,0:T(1,128)} %lengths.1, s32[1,32]{1,0:T(1,128)} %ids.1, ...), custom_call_target="tpu_custom_call" | custom-call | flops 4194304 | bytes 524288 | tf_op jit(solution)/shard_map/pallas_call | solution.py:234
  9.6 1.3 constant_dynamic-slice_fusion.4
  10.8 6.5 %shard_map.158 = (bf16[512,896]{1,0:T(8,128)(2,1)}, bf16[512,896]{1,0:T(8,128)(2,1)}, bf16[512,896]{1,0:T(8,128)(2,1)}, bf16[512,896]{1,0:T(8,128)(2,1)}, bf16[512,896]{1,0:T(8,128)(2,1)}, /*index=5*/f32[32,896]{1,0:T(8,128)}) custom-call(s32[13]{0:T(128)} %get-tuple-element.90.sc, bf16[512,3584]{1,0:T(8,128)(2,1)} %hidden_ref.1, ...), custom_call_target="tpu_custom_call" | custom-call | flops 14680064 | bytes 7340032 | tf_op jit(solution)/shard_map/pallas_call | solution.py:279
  17.4 5.2 %collective-permute-done.r1 = bf16[896,384]{1,0:T(8,128)(2,1)} collective-permute-done((bf16[896,384]{1,0:T(8,128)(2,1)S(1)}, bf16[896,384]{1,0:T(8,128)(2,1)}, u32[]{:S(2)}, u32[]{:S(2)}) %collective-permute-start) | collective-permute-done | bytes 688160 | tf_op jit(solution)/shard_map/ppermute | solution.py:569
  22.5 1.7 %collective-permute-start.1 = (bf16[896,384]{1,0:T(8,128)(2,1)S(1)}, bf16[896,384]{1,0:T(8,128)(2,1)S(1)}, u32[]{:S(2)}, u32[]{:S(2)}) collective-permute-start(bf16[896,384]{1,0:T(8,128)(2,1)S(1)} %pad_maximum_fusion), channel_id=1, source_target_pairs={{4,0},{12,4},{8,12},{0,8},{5,1},{13,5},{9,13},{1,9},{6,2},{14,6},{... | collective-permute-start | bytes 2064392 | tf_op jit(solution)/shard_map/ppermute | solution.py:569
  24.3 1.5 collective-permute-start.2
  25.8 13.4 %collective-permute-done.1.r3 = bf16[896,384]{1,0:T(8,128)(2,1)S(1)} collective-permute-done((bf16[896,384]{1,0:T(8,128)(2,1)S(1)}, bf16[896,384]{1,0:T(8,128)(2,1)S(1)}, u32[]{:S(2)}, u32[]{:S(2)}) %collective-permute-start.1) | collective-permute-done | bytes 688160 | tf_op jit(solution)/shard_map/ppermute | solution.py:569
  39.2 1.3 collective-permute-done.2.y1
  40.5 0.9 collective-permute-start.3
  41.4 1.5 collective-permute-start.4
  42.9 13.9 %collective-permute-done.3.r2 = bf16[896,384]{1,0:T(8,128)(2,1)} collective-permute-done((bf16[896,384]{1,0:T(8,128)(2,1)}, bf16[896,384]{1,0:T(8,128)(2,1)}, u32[]{:S(2)}, u32[]{:S(2)}) %collective-permute-start.3) | collective-permute-done | bytes 688160 | tf_op jit(solution)/shard_map/ppermute | solution.py:569
  56.8 1.5 collective-permute-start.7
  58.4 0.7 collective-permute-start.5
  59.1 0.7 constant_dynamic-slice_fusion
  59.8 2.3 %collective-permute-start.6 = (bf16[256,512]{1,0:T(8,128)(2,1)}, bf16[256,512]{1,0:T(8,128)(2,1)}, u32[]{:S(2)}, u32[]{:S(2)}) collective-permute-start(bf16[256,512]{1,0:T(8,128)(2,1)} %constant_dynamic-slice_fusion), channel_id=1, source_target_pairs={{4,0},{12,4},{8,12},{0,8},{5,1},{13,5},{9,13},{1,9},{6,2},{14,6},{... | collective-permute-start | bytes 786440 | tf_op jit(solution)/shard_map/ppermute | solution.py:569
  62.1 8.1 %shard_map.159 = (f32[512,256]{1,0:T(8,128)}, f32[512,256]{1,0:T(8,128)}, f32[512,256]{1,0:T(8,128)}) custom-call(s32[13]{0:T(128)} %get-tuple-element.90.sc, bf16[512,896]{1,0:T(8,128)(2,1)} %get-tuple-element.48.b0, bf16[512,896]{1,0:T(8,128)(2,1)} %get-tuple-element.49.b1, bf16[512,896]{1,0:T(8,128)(2,1)} %get-tuple-element.50.b2, ...), custom_call_target="tpu_custom_call" | custom-call | flops 2818572288 | bytes 10059776 | tf_op jit(solution)/shard_map/pallas_call | solution.py:177
  70.2 1.2 collective-permute-done.5.own_a
  71.9 2.2 %collective-permute-done.6.own_b = bf16[256,512]{1,0:T(8,128)(2,1)} collective-permute-done((bf16[256,512]{1,0:T(8,128)(2,1)}, bf16[256,512]{1,0:T(8,128)(2,1)}, u32[]{:S(2)}, u32[]{:S(2)}) %collective-permute-start.6) | collective-permute-done | bytes 262176 | tf_op jit(solution)/shard_map/ppermute | solution.py:569
  74.1 1.9 %collective-permute-start.9 = (bf16[256,896]{1,0:T(8,128)(2,1)}, bf16[256,896]{1,0:T(8,128)(2,1)}, u32[]{:S(2)}, u32[]{:S(2)}) collective-permute-start(bf16[256,896]{1,0:T(8,128)(2,1)} %collective-permute-done.5.own_a), channel_id=1, source_target_pairs={{0,4},{4,12},{12,8},{8,0},{1,5},{5,13},{13,9},{9,1},{2,6},{6,14},{... | collective-permute-start | bytes 1376264 | tf_op jit(solution)/shard_map/ppermute | solution.py:569
  75.9 1.5 collective-permute-start.13
  77.5 1.9 %collective-permute-start.8 = (bf16[256,384]{1,0:T(8,128)(2,1)S(1)}, bf16[256,384]{1,0:T(8,128)(2,1)S(1)}, u32[]{:S(2)}, u32[]{:S(2)}) collective-permute-start(bf16[256,384]{1,0:T(8,128)(2,1)S(1)} %dynamic-slice), channel_id=1, source_target_pairs={{4,0},{12,4},{8,12},{0,8},{5,1},{13,5},{9,13},{1,9},{6,2},{14,6},{... | collective-permute-start | bytes 589832 | tf_op jit(solution)/shard_map/ppermute | solution.py:569
  80.0 3.0 %shard_map.160 = (bf16[512,256]{1,0:T(8,128)(2,1)}, bf16[512,128]{1,0:T(8,128)(2,1)}, bf16[512,128]{1,0:T(8,128)(2,1)}) custom-call(s32[13]{0:T(128)} %get-tuple-element.90.sc, f32[512,256]{1,0:T(8,128)} %get-tuple-element.62.kv_ref, bf16[512,896]{1,0:T(8,128)(2,1)} %get-tuple-element.50.b2, bf16[896,384]{1,0:T(8,128)(2,1)} %copy-done.1, ...), custom_call_target="tpu_custom_call" | custom-call | flops 58720256 | bytes 3180544 | tf_op jit(solution)/shard_map/pallas_call | solution.py:177
  83.1 1.9 %collective-permute-start.10 = (bf16[512,128]{1,0:T(8,128)(2,1)}, bf16[512,128]{1,0:T(8,128)(2,1)S(1)}, u32[]{:S(2)}, u32[]{:S(2)}) collective-permute-start(bf16[512,128]{1,0:T(8,128)(2,1)} %get-tuple-element.65), channel_id=1, source_target_pairs={{2,0},{0,1},{1,2},{6,4},{4,5},{5,6},{10,8},{8,9},{9,10},{14,12},{1... | collective-permute-start | bytes 393224 | tf_op jit(solution)/shard_map/ppermute | solution.py:609
  85.0 2.1 %collective-permute-done.13.oth_b = bf16[256,512]{1,0:T(8,128)(2,1)} collective-permute-done((bf16[256,512]{1,0:T(8,128)(2,1)}, bf16[256,512]{1,0:T(8,128)(2,1)}, u32[]{:S(2)}, u32[]{:S(2)}) %collective-permute-start.13) | collective-permute-done | bytes 262176 | tf_op jit(solution)/shard_map/ppermute | solution.py:574
  87.7 2.4 %collective-permute-done.10.x1 = bf16[512,128]{1,0:T(8,128)(2,1)S(1)} collective-permute-done((bf16[512,128]{1,0:T(8,128)(2,1)}, bf16[512,128]{1,0:T(8,128)(2,1)S(1)}, u32[]{:S(2)}, u32[]{:S(2)}) %collective-permute-start.10) | collective-permute-done | bytes 131104 | tf_op jit(solution)/shard_map/ppermute | solution.py:609
  90.1 1.1 collective-permute-done.8.own_c
  91.2 0.8 collective-permute-done.9.own_b
  92.4 1.7 %collective-permute-start.17 = (bf16[256,384]{1,0:T(8,128)(2,1)S(1)}, bf16[256,384]{1,0:T(8,128)(2,1)S(1)}, u32[]{:S(2)}, u32[]{:S(2)}) collective-permute-start(bf16[256,384]{1,0:T(8,128)(2,1)S(1)} %collective-permute-done.8.own_c), channel_id=1, source_target_pairs={{0,16},{16,0},{1,17},{17,1},{2,18},{18,2},{3,19},{19,3},{4,20},{20... | collective-permute-start | bytes 589832 | tf_op jit(solution)/shard_map/ppermute | solution.py:574
  94.6 8.6 %shard_map.161 = (bf16[512,512]{1,0:T(8,128)(2,1)}, bf16[32,512]{1,0:T(8,128)(2,1)}) custom-call(s32[13]{0:T(128)} %get-tuple-element.90.sc, f32[512,256]{1,0:T(8,128)} %get-tuple-element.60.own_ref, f32[512,256]{1,0:T(8,128)} %get-tuple-element.61.oth_ref, bf16[512,896]{1,0:T(8,128)(2,1)} %get-tuple-element.50.b2, bf16[896,384]{1,0:T(8,128)(2,1)} %copy-done.1, ...), custom_call_target="tpu_custom_call" | custom-call | flops 536870912 | bytes 8388608 | tf_op jit(solution)/shard_map/pallas_call | solution.py:398
  103.2 2.0 %collective-permute-done.14.oth_b = bf16[256,896]{1,0:T(8,128)(2,1)S(1)} collective-permute-done((bf16[256,896]{1,0:T(8,128)(2,1)}, bf16[256,896]{1,0:T(8,128)(2,1)S(1)}, u32[]{:S(2)}, u32[]{:S(2)}) %collective-permute-start.14) | collective-permute-done | bytes 458784 | tf_op jit(solution)/shard_map/ppermute | solution.py:574
  105.1 0.8 copy-done.21
  105.9 4.7 %shard_map.162 = (bf16[512,896]{1,0:T(8,128)(2,1)}, bf16[512,896]{1,0:T(8,128)(2,1)}, bf16[32,896]{1,0:T(8,128)(2,1)}, bf16[32,896]{1,0:T(8,128)(2,1)}) custom-call(s32[13]{0:T(128)} %get-tuple-element.90.sc, bf16[512,512]{1,0:T(8,128)(2,1)} %get-tuple-element.76.attn, bf16[32,512]{1,0:T(8,128)(2,1)} %get-tuple-element.72.lists, bf16[512,896]{1,0:T(8,128)(2,1)} %w.1, ...), custom_call_target="tpu_custom_call" | custom-call | flops 939524096 | bytes 4341760 | tf_op jit(solution)/shard_map/pallas_call | solution.py:177
  110.6 1.1 collective-permute-start.15
  112.5 4.6 %shard_map.164 = (bf16[512,896]{1,0:T(8,128)(2,1)}, bf16[512,896]{1,0:T(8,128)(2,1)}, bf16[32,896]{1,0:T(8,128)(2,1)}, bf16[32,896]{1,0:T(8,128)(2,1)}) custom-call(s32[13]{0:T(128)} %get-tuple-element.90.sc, bf16[512,512]{1,0:T(8,128)(2,1)} %get-tuple-element.76.attn, bf16[32,512]{1,0:T(8,128)(2,1)} %get-tuple-element.72.lists, ...), custom_call_target="tpu_custom_call" | custom-call | flops 939524096 | bytes 4341760 | tf_op jit(solution)/shard_map/pallas_call | solution.py:177
  117.1 0.8 pad_maximum_fusion.1
  119.8 0.9 select_convert_fusion
  120.7 2.6 %shard_map.163.ta = bf16[512,896]{1,0:T(8,128)(2,1)} custom-call(s32[13]{0:T(128)} %get-tuple-element.90.sc, bf16[512,896]{1,0:T(8,128)(2,1)} %get-tuple-element.74.kept, bf16[512,896]{1,0:T(8,128)(2,1)} %collective-permute-done.15.came), custom_call_target="tpu_custom_call" | custom-call | flops 458752 | bytes 2752512 | tf_op jit(solution)/shard_map/pallas_call | solution.py:177
  123.3 1.0 collective-permute-start.21
  124.6 1.3 collective-permute-start.16
  125.9 0.9 copy-done.3
  126.8 2.6 %shard_map.165.tb = bf16[512,896]{1,0:T(8,128)(2,1)} custom-call(s32[13]{0:T(128)} %get-tuple-element.90.sc, bf16[512,896]{1,0:T(8,128)(2,1)} %get-tuple-element.78.kept, bf16[512,896]{1,0:T(8,128)(2,1)} %copy-done.3), custom_call_target="tpu_custom_call" | custom-call | flops 458752 | bytes 2752512 | tf_op jit(solution)/shard_map/pallas_call | solution.py:177
  129.4 5.6 %collective-permute-start.19 = (bf16[512,896]{1,0:T(8,128)(2,1)}, bf16[512,896]{1,0:T(8,128)(2,1)S(1)}, u32[]{:S(2)}, u32[]{:S(2)}) collective-permute-start(bf16[512,896]{1,0:T(8,128)(2,1)} %shard_map.165.tb), channel_id=1, source_target_pairs={{0,2},{3,1},{6,4},{5,7},{9,11},{10,8},{15,13},{12,14},{16,18},{19,... | collective-permute-start | bytes 2752520 | tf_op jit(solution)/shard_map/ppermute | solution.py:650
  135.8 15.1 %all_to_all.5 = bf16[16,8,384]{2,1,0:T(8,128)(2,1)S(1)} all-to-all(bf16[16,8,384]{2,1,0:T(8,128)(2,1)S(1)} %bitcast.13), channel_id=1, replica_groups=mesh['groups'=2,'dp'=4,'tp'=4] {'dp','tp'}, dimensions={0} | all-to-all | bytes 196608 | tf_op jit(solution)/shard_map/all_to_all | solution.py:684
  152.3 0.9 copy-done.4
  153.2 3.6 %shard_map.166 = bf16[512,896]{1,0:T(8,128)(2,1)} custom-call(s32[13]{0:T(128)} %get-tuple-element.90.sc, bf16[512,896]{1,0:T(8,128)(2,1)} %get-tuple-element.47.own, bf16[512,896]{1,0:T(8,128)(2,1)} %shard_map.163.ta, bf16[512,896]{1,0:T(8,128)(2,1)} %collective-permute-done.16.ca, bf16[512,896]{1,0:T(8,128)(2,1)} %shard_map.165.tb, bf16[512,896]{1,0:T(8,128)(2,1)} %copy-done.4), custom_call_target="tpu_custom_call" | custom-call | flops 458752 | bytes 5505024 | tf_op jit(solution)/shard_map/pallas_call | solution.py:177
  (79 shorter events, 7.8 us)
Async XLA Ops:
  0.6 134.4 %copy-start = (bf16[896,1024]{1,0:T(8,128)(2,1)S(1)}, bf16[896,1024]{1,0:T(8,128)(2,1)}, u32[]{:S(2)}) copy-start(bf16[896,1024]{1,0:T(8,128)(2,1)} %param.24) | copy-start | bytes 5505028
  0.6 5.3 %copy-start.14 = (f32[3584]{0:T(1024)S(1)}, f32[3584]{0:T(1024)}, u32[]{:S(2)}) copy-start(f32[3584]{0:T(1024)} %param.18) | copy-start | bytes 43012
  2.9 19.6 %collective-permute-start = (bf16[896,384]{1,0:T(8,128)(2,1)S(1)}, bf16[896,384]{1,0:T(8,128)(2,1)}, u32[]{:S(2)}, u32[]{:S(2)}) collective-permute-start(bf16[896,384]{1,0:T(8,128)(2,1)S(1)} %pad_maximum_fusion), channel_id=1, source_target_pairs={{0,4},{4,12},{12,8},{8,0},{1,5},{5,13},{13,9},{9,1},{2,6},{6,14},{... | collective-permute-start | bytes 2064392 | tf_op jit(solution)/shard_map/ppermute | solution.py:569
  10.8 47.5 %copy-start.2 = (bf16[512,896]{1,0:T(8,128)(2,1)S(1)}, bf16[512,896]{1,0:T(8,128)(2,1)}, u32[]{:S(2)}) copy-start(bf16[512,896]{1,0:T(8,128)(2,1)} %w.1) | copy-start | bytes 2752516
  22.5 16.6 %collective-permute-start.1 = (bf16[896,384]{1,0:T(8,128)(2,1)S(1)}, bf16[896,384]{1,0:T(8,128)(2,1)S(1)}, u32[]{:S(2)}, u32[]{:S(2)}) collective-permute-start(bf16[896,384]{1,0:T(8,128)(2,1)S(1)} %pad_maximum_fusion), channel_id=1, source_target_pairs={{4,0},{12,4},{8,12},{0,8},{5,1},{13,5},{9,13},{1,9},{6,2},{14,6},{... | collective-permute-start | bytes 2064392 | tf_op jit(solution)/shard_map/ppermute | solution.py:569
  24.3 16.2 %collective-permute-start.2 = (bf16[896,384]{1,0:T(8,128)(2,1)}, bf16[896,384]{1,0:T(8,128)(2,1)S(1)}, u32[]{:S(2)}, u32[]{:S(2)}) collective-permute-start(bf16[896,384]{1,0:T(8,128)(2,1)} %collective-permute-done.r1), channel_id=1, source_target_pairs={{0,16},{16,0},{1,17},{17,1},{2,18},{18,2},{3,19},{19,3},{4,20},{20... | collective-permute-start | bytes 2064392 | tf_op jit(solution)/shard_map/ppermute | solution.py:574
  39.2 23.0 %copy-start.18 = (bf16[896,384]{1,0:T(8,128)(2,1)}, bf16[896,384]{1,0:T(8,128)(2,1)S(1)}, u32[]{:S(2)}) copy-start(bf16[896,384]{1,0:T(8,128)(2,1)S(1)} %collective-permute-done.1.r3) | copy-start | bytes 2064388
  40.5 16.3 %copy-start.19 = (bf16[896,384]{1,0:T(8,128)(2,1)}, bf16[896,384]{1,0:T(8,128)(2,1)S(1)}, u32[]{:S(2)}) copy-start(bf16[896,384]{1,0:T(8,128)(2,1)S(1)} %collective-permute-done.2.y1) | copy-start | bytes 2064388
  40.5 16.3 %collective-permute-start.3 = (bf16[896,384]{1,0:T(8,128)(2,1)}, bf16[896,384]{1,0:T(8,128)(2,1)}, u32[]{:S(2)}, u32[]{:S(2)}) collective-permute-start(bf16[896,384]{1,0:T(8,128)(2,1)} %collective-permute-done.r1), channel_id=1, source_target_pairs={{0,4},{4,12},{12,8},{8,0},{1,5},{5,13},{13,9},{9,1},{2,6},{6,14},{... | collective-permute-start | bytes 2064392 | tf_op jit(solution)/shard_map/ppermute | solution.py:569
  41.4 17.0 %collective-permute-start.4 = (bf16[896,384]{1,0:T(8,128)(2,1)S(1)}, bf16[896,384]{1,0:T(8,128)(2,1)S(1)}, u32[]{:S(2)}, u32[]{:S(2)}) collective-permute-start(bf16[896,384]{1,0:T(8,128)(2,1)S(1)} %collective-permute-done.1.r3), channel_id=1, source_target_pairs={{0,16},{16,0},{1,17},{17,1},{2,18},{18,2},{3,19},{19,3},{4,20},{20... | collective-permute-start | bytes 2064392 | tf_op jit(solution)/shard_map/ppermute | solution.py:574
  56.8 17.2 %collective-permute-start.7 = (bf16[896,384]{1,0:T(8,128)(2,1)}, bf16[896,384]{1,0:T(8,128)(2,1)S(1)}, u32[]{:S(2)}, u32[]{:S(2)}) collective-permute-start(bf16[896,384]{1,0:T(8,128)(2,1)} %collective-permute-done.3.r2), channel_id=1, source_target_pairs={{0,16},{16,0},{1,17},{17,1},{2,18},{18,2},{3,19},{19,3},{4,20},{20... | collective-permute-start | bytes 2064392 | tf_op jit(solution)/shard_map/ppermute | solution.py:574
  58.4 3.7 %copy-start.20 = (bf16[896,384]{1,0:T(8,128)(2,1)}, bf16[896,384]{1,0:T(8,128)(2,1)S(1)}, u32[]{:S(2)}) copy-start(bf16[896,384]{1,0:T(8,128)(2,1)S(1)} %collective-permute-done.4.y3) | copy-start | bytes 2064388
  58.4 12.9 %collective-permute-start.5 = (bf16[256,896]{1,0:T(8,128)(2,1)S(1)}, bf16[256,896]{1,0:T(8,128)(2,1)}, u32[]{:S(2)}, u32[]{:S(2)}) collective-permute-start(bf16[256,896]{1,0:T(8,128)(2,1)S(1)} %constant_dynamic-slice_fusion.1), channel_id=1, source_target_pairs={{0,4},{4,12},{12,8},{8,0},{1,5},{5,13},{13,9},{9,1},{2,6},{6,14},{... | collective-permute-start | bytes 1376264 | tf_op jit(solution)/shard_map/ppermute | solution.py:569
  59.8 14.2 %collective-permute-start.6 = (bf16[256,512]{1,0:T(8,128)(2,1)}, bf16[256,512]{1,0:T(8,128)(2,1)}, u32[]{:S(2)}, u32[]{:S(2)}) collective-permute-start(bf16[256,512]{1,0:T(8,128)(2,1)} %constant_dynamic-slice_fusion), channel_id=1, source_target_pairs={{4,0},{12,4},{8,12},{0,8},{5,1},{13,5},{9,13},{1,9},{6,2},{14,6},{... | collective-permute-start | bytes 786440 | tf_op jit(solution)/shard_map/ppermute | solution.py:569
  62.1 17.3 %copy-start.16 = (bf16[1024]{0:T(1024)(128)(2,1)S(1)}, bf16[1024]{0:T(1024)(128)(2,1)}, u32[]{:S(2)}) copy-start(bf16[1024]{0:T(1024)(128)(2,1)} %param.22) | copy-start | bytes 6148
  70.2 23.9 %copy-start.17 = (bf16[512]{0:T(512)(128)(2,1)S(1)}, bf16[512]{0:T(512)(128)(2,1)}, u32[]{:S(2)}) copy-start(bf16[512]{0:T(512)(128)(2,1)} %param.20) | copy-start | bytes 3076
  71.4 19.8 %collective-permute-start.12 = (bf16[256,896]{1,0:T(8,128)(2,1)}, bf16[256,896]{1,0:T(8,128)(2,1)}, u32[]{:S(2)}, u32[]{:S(2)}) collective-permute-start(bf16[256,896]{1,0:T(8,128)(2,1)} %collective-permute-done.5.own_a), channel_id=1, source_target_pairs={{0,16},{16,0},{1,17},{17,1},{2,18},{18,2},{3,19},{19,3},{4,20},{20... | collective-permute-start | bytes 1376264 | tf_op jit(solution)/shard_map/ppermute | solution.py:574
  74.1 5.9 %copy-start.1 = (bf16[896,384]{1,0:T(8,128)(2,1)}, bf16[896,384]{1,0:T(8,128)(2,1)S(1)}, u32[]{:S(2)}) copy-start(bf16[896,384]{1,0:T(8,128)(2,1)S(1)} %collective-permute-done.7.y2) | copy-start | bytes 2064388
  74.1 17.9 %collective-permute-start.9 = (bf16[256,896]{1,0:T(8,128)(2,1)}, bf16[256,896]{1,0:T(8,128)(2,1)}, u32[]{:S(2)}, u32[]{:S(2)}) collective-permute-start(bf16[256,896]{1,0:T(8,128)(2,1)} %collective-permute-done.5.own_a), channel_id=1, source_target_pairs={{0,4},{4,12},{12,8},{8,0},{1,5},{5,13},{13,9},{9,1},{2,6},{6,14},{... | collective-permute-start | bytes 1376264 | tf_op jit(solution)/shard_map/ppermute | solution.py:569
  75.9 11.1 %collective-permute-start.13 = (bf16[256,512]{1,0:T(8,128)(2,1)}, bf16[256,512]{1,0:T(8,128)(2,1)}, u32[]{:S(2)}, u32[]{:S(2)}) collective-permute-start(bf16[256,512]{1,0:T(8,128)(2,1)} %collective-permute-done.6.own_b), channel_id=1, source_target_pairs={{0,16},{16,0},{1,17},{17,1},{2,18},{18,2},{3,19},{19,3},{4,20},{20... | collective-permute-start | bytes 786440 | tf_op jit(solution)/shard_map/ppermute | solution.py:574
  77.5 13.7 %collective-permute-start.8 = (bf16[256,384]{1,0:T(8,128)(2,1)S(1)}, bf16[256,384]{1,0:T(8,128)(2,1)S(1)}, u32[]{:S(2)}, u32[]{:S(2)}) collective-permute-start(bf16[256,384]{1,0:T(8,128)(2,1)S(1)} %dynamic-slice), channel_id=1, source_target_pairs={{4,0},{12,4},{8,12},{0,8},{5,1},{13,5},{9,13},{1,9},{6,2},{14,6},{... | collective-permute-start | bytes 589832 | tf_op jit(solution)/shard_map/ppermute | solution.py:569
  83.1 7.1 %collective-permute-start.10 = (bf16[512,128]{1,0:T(8,128)(2,1)}, bf16[512,128]{1,0:T(8,128)(2,1)S(1)}, u32[]{:S(2)}, u32[]{:S(2)}) collective-permute-start(bf16[512,128]{1,0:T(8,128)(2,1)} %get-tuple-element.65), channel_id=1, source_target_pairs={{2,0},{0,1},{1,2},{6,4},{4,5},{5,6},{10,8},{8,9},{9,10},{14,12},{1... | collective-permute-start | bytes 393224 | tf_op jit(solution)/shard_map/ppermute | solution.py:609
  87.1 3.1 %collective-permute-start.11 = (bf16[512,128]{1,0:T(8,128)(2,1)}, bf16[512,128]{1,0:T(8,128)(2,1)S(1)}, u32[]{:S(2)}, u32[]{:S(2)}) collective-permute-start(bf16[512,128]{1,0:T(8,128)(2,1)} %get-tuple-element.66), channel_id=1, source_target_pairs={{2,1},{3,2},{1,3},{6,5},{7,6},{5,7},{10,9},{11,10},{9,11},{14,13},... | collective-permute-start | bytes 393224 | tf_op jit(solution)/shard_map/ppermute | solution.py:609
  90.1 4.5 %copy-start.7 = (bf16[512,128]{1,0:T(8,128)(2,1)}, bf16[512,128]{1,0:T(8,128)(2,1)S(1)}, u32[]{:S(2)}) copy-start(bf16[512,128]{1,0:T(8,128)(2,1)S(1)} %collective-permute-done.10.x1) | copy-start | bytes 393220
  90.1 4.5 %copy-start.8 = (bf16[512,128]{1,0:T(8,128)(2,1)}, bf16[512,128]{1,0:T(8,128)(2,1)S(1)}, u32[]{:S(2)}) copy-start(bf16[512,128]{1,0:T(8,128)(2,1)S(1)} %collective-permute-done.11.x2) | copy-start | bytes 393220
  91.2 12.0 %copy-start.22 = (bf16[256,384]{1,0:T(8,128)(2,1)}, bf16[256,384]{1,0:T(8,128)(2,1)S(1)}, u32[]{:S(2)}) copy-start(bf16[256,384]{1,0:T(8,128)(2,1)S(1)} %collective-permute-done.8.own_c) | copy-start | bytes 589828
  92.0 13.1 %collective-permute-start.14 = (bf16[256,896]{1,0:T(8,128)(2,1)}, bf16[256,896]{1,0:T(8,128)(2,1)S(1)}, u32[]{:S(2)}, u32[]{:S(2)}) collective-permute-start(bf16[256,896]{1,0:T(8,128)(2,1)} %collective-permute-done.9.own_b), channel_id=1, source_target_pairs={{0,16},{16,0},{1,17},{17,1},{2,18},{18,2},{3,19},{19,3},{4,20},{20... | collective-permute-start | bytes 1376264 | tf_op jit(solution)/shard_map/ppermute | solution.py:574
  92.4 19.4 %collective-permute-start.17 = (bf16[256,384]{1,0:T(8,128)(2,1)S(1)}, bf16[256,384]{1,0:T(8,128)(2,1)S(1)}, u32[]{:S(2)}, u32[]{:S(2)}) collective-permute-start(bf16[256,384]{1,0:T(8,128)(2,1)S(1)} %collective-permute-done.8.own_c), channel_id=1, source_target_pairs={{0,16},{16,0},{1,17},{17,1},{2,18},{18,2},{3,19},{19,3},{4,20},{20... | collective-permute-start | bytes 589832 | tf_op jit(solution)/shard_map/ppermute | solution.py:574
  105.1 0.8 copy-start.21
  110.6 6.5 %copy-start.11 = (bf16[32,896]{1,0:T(8,128)(2,1)S(1)}, bf16[32,896]{1,0:T(8,128)(2,1)}, u32[]{:S(2)}) copy-start(bf16[32,896]{1,0:T(8,128)(2,1)} %get-tuple-element.82) | copy-start | bytes 172036
  110.6 8.4 %copy-start.10 = (f32[32,1]{1,0:T(8,128)S(1)}, f32[32,1]{1,0:T(8,128)}, u32[]{:S(2)}) copy-start(f32[32,1]{1,0:T(8,128)} %get-tuple-element.69.inverse_ref) | copy-start | bytes 388
  110.6 9.2 %copy-start.5 = (bf16[32,896]{1,0:T(8,128)(2,1)S(1)}, bf16[32,896]{1,0:T(8,128)(2,1)}, u32[]{:S(2)}) copy-start(bf16[32,896]{1,0:T(8,128)(2,1)} %get-tuple-element.81) | copy-start | bytes 172036
  110.6 10.1 %collective-permute-start.15 = (bf16[512,896]{1,0:T(8,128)(2,1)}, bf16[512,896]{1,0:T(8,128)(2,1)}, u32[]{:S(2)}, u32[]{:S(2)}) collective-permute-start(bf16[512,896]{1,0:T(8,128)(2,1)} %get-tuple-element.75), channel_id=1, source_target_pairs={{0,1},{1,0},{2,3},{3,2},{4,5},{5,4},{6,7},{7,6},{8,9},{9,8},{10,11... | collective-permute-start | bytes 2752520 | tf_op jit(solution)/shard_map/ppermute | solution.py:640
  111.7 0.7 copy-start.23
  117.0 7.4 %copy-start.13 = (f32[32,1]{1,0:T(8,128)S(1)}, f32[32,1]{1,0:T(8,128)}, u32[]{:S(2)}) copy-start(f32[32,1]{1,0:T(8,128)} %get-tuple-element.87) | copy-start | bytes 388
  117.0 8.9 %collective-permute-start.18 = (bf16[512,896]{1,0:T(8,128)(2,1)}, bf16[512,896]{1,0:T(8,128)(2,1)S(1)}, u32[]{:S(2)}, u32[]{:S(2)}) collective-permute-start(bf16[512,896]{1,0:T(8,128)(2,1)} %get-tuple-element.79), channel_id=1, source_target_pairs={{0,1},{1,0},{2,3},{3,2},{4,5},{5,4},{6,7},{7,6},{8,9},{9,8},{10,11... | collective-permute-start | bytes 2752520 | tf_op jit(solution)/shard_map/ppermute | solution.py:640
  117.9 1.9 %collective-permute-start.20 = (bf16[64,896]{1,0:T(8,128)(2,1)S(1)}, bf16[64,896]{1,0:T(8,128)(2,1)S(1)}, u32[]{:S(2)}, u32[]{:S(2)}) collective-permute-start(bf16[64,896]{1,0:T(8,128)(2,1)S(1)} %pad_maximum_fusion.1), channel_id=1, source_target_pairs={{0,1},{1,0},{2,3},{3,2},{4,5},{5,4},{6,7},{7,6},{8,9},{9,8},{10,11... | collective-permute-start | bytes 344072 | tf_op jit(solution)/shard_map/ppermute | solution.py:664
  123.3 11.7 %copy-start.6 = (bf16[32,896]{1,0:T(8,128)(2,1)S(1)}, bf16[32,896]{1,0:T(8,128)(2,1)}, u32[]{:S(2)}) copy-start(bf16[32,896]{1,0:T(8,128)(2,1)} %get-tuple-element.84) | copy-start | bytes 172036
  123.3 11.7 %copy-start.9 = (f32[32,896]{1,0:T(8,128)S(1)}, f32[32,896]{1,0:T(8,128)}, u32[]{:S(2)}) copy-start(f32[32,896]{1,0:T(8,128)} %get-tuple-element.86) | copy-start | bytes 344068
  123.3 11.8 %copy-start.12 = (bf16[32,32]{1,0:T(8,128)(2,1)S(1)}, bf16[32,32]{1,0:T(8,128)(2,1)}, u32[]{:S(2)}) copy-start(bf16[32,32]{1,0:T(8,128)(2,1)} %get-tuple-element.70.hits_ref) | copy-start | bytes 6148
  123.3 11.7 %collective-permute-start.21 = (bf16[32,896]{1,0:T(8,128)(2,1)S(1)}, bf16[32,896]{1,0:T(8,128)(2,1)S(1)}, u32[]{:S(2)}, u32[]{:S(2)}) collective-permute-start(bf16[32,896]{1,0:T(8,128)(2,1)S(1)} %select_convert_fusion), channel_id=1, source_target_pairs={{0,2},{1,3},{2,0},{3,1},{4,6},{5,7},{6,4},{7,5},{8,10},{9,11},{10,... | collective-permute-start | bytes 172040 | tf_op jit(solution)/shard_map/ppermute | solution.py:668
  124.6 27.7 %collective-permute-start.16 = (bf16[512,896]{1,0:T(8,128)(2,1)}, bf16[512,896]{1,0:T(8,128)(2,1)}, u32[]{:S(2)}, u32[]{:S(2)}) collective-permute-start(bf16[512,896]{1,0:T(8,128)(2,1)} %shard_map.163.ta), channel_id=1, source_target_pairs={{2,0},{1,3},{7,5},{4,6},{8,10},{11,9},{13,15},{14,12},{18,16},{17,... | collective-permute-start | bytes 2752520 | tf_op jit(solution)/shard_map/ppermute | solution.py:650
  125.9 0.9 copy-start.3
  129.4 22.2 %copy-start.15 = (f32[8,256]{1,0:T(8,128)S(1)}, f32[8,256]{1,0:T(8,128)}, u32[]{:S(2)}) copy-start(f32[8,256]{1,0:T(8,128)} %param.25) | copy-start | bytes 24580
  129.4 22.9 %collective-permute-start.19 = (bf16[512,896]{1,0:T(8,128)(2,1)}, bf16[512,896]{1,0:T(8,128)(2,1)S(1)}, u32[]{:S(2)}, u32[]{:S(2)}) collective-permute-start(bf16[512,896]{1,0:T(8,128)(2,1)} %shard_map.165.tb), channel_id=1, source_target_pairs={{0,2},{3,1},{6,4},{5,7},{9,11},{10,8},{15,13},{12,14},{16,18},{19,... | collective-permute-start | bytes 2752520 | tf_op jit(solution)/shard_map/ppermute | solution.py:650
  152.3 0.9 copy-start.4
